TPU v7x, 32 devices: a whole 2x2x4 slice. The times are simulated.
32 devices in a mesh: dp: 8 (over z, y), tensor: 4 (over x, core).
Axes of the slice: x: 2, y: 2, z: 4, core: 2. Of those that a mesh axis runs over, the one named last changes fastest.
Arguments:
- resid_in: float32 [16384, 1536], P(('dp', 'tensor')), may hold values from -6 to 6
- cotangent: float32 [16384, 1536], P(('dp', 'tensor')), may hold values from -6 to 6
- w_zx: float32 [2, 1536, 2, 3072], P(None, 'dp', None, 'tensor'), may hold values from -0.15625 to 0.15625
- w_bc: float32 [2, 1536, 256], P(None, ('dp', 'tensor')), may hold values from -0.15625 to 0.15625
- w_dt: float32 [2, 1536, 48], P(None, 'dp', 'tensor'), may hold values from -0.15625 to 0.15625
- w_out: float32 [2, 3072, 1536], P(None, 'tensor', 'dp'), may hold values from -0.109375 to 0.109375
- chan_par: float32 [2, 6, 3072], P(None, None, 'tensor'), may hold values from -2.4 to 2.4
- head_par: float32 [2, 3, 48], P(None, None, 'tensor'), may hold values from -6 to 1.5
- bc_par: float32 [2, 5, 256], P(None, None, ('dp', 'tensor')), may hold values from -0.8 to 0.8
- norm_gain: float32 [2, 1536], P(None, ('dp', 'tensor')), may hold values from 0.5 to 1.5
- zx_first: float32 [2, 1536, 2, 3072], P(None, 'dp', None, 'tensor'), as said below
- zx_second: float32 [2, 1536, 2, 3072], P(None, 'dp', None, 'tensor'), as said below
- bc_first: float32 [2, 1536, 256], P(None, ('dp', 'tensor')), as said below
- bc_second: float32 [2, 1536, 256], P(None, ('dp', 'tensor')), as said below
- dt_first: float32 [2, 1536, 48], P(None, 'dp', 'tensor'), as said below
- dt_second: float32 [2, 1536, 48], P(None, 'dp', 'tensor'), as said below
- out_first: float32 [2, 3072, 1536], P(None, 'tensor', 'dp'), as said below
- out_second: float32 [2, 3072, 1536], P(None, 'tensor', 'dp'), as said below
- chan_first: float32 [2, 6, 3072], P(None, None, 'tensor'), as said below
- chan_second: float32 [2, 6, 3072], P(None, None, 'tensor'), as said below
- head_first: float32 [2, 3, 48], P(None, None, 'tensor'), as said below
- head_second: float32 [2, 3, 48], P(None, None, 'tensor'), as said below
- bcpar_first: float32 [2, 5, 256], P(None, None, ('dp', 'tensor')), as said below
- bcpar_second: float32 [2, 5, 256], P(None, None, ('dp', 'tensor')), as said below
- gain_first: float32 [2, 1536], P(None, ('dp', 'tensor')), as said below
- gain_second: float32 [2, 1536], P(None, ('dp', 'tensor')), as said below
Outputs:
- resid_out: float32 [16384, 1536], P(('dp', 'tensor'))
- resid_grad: float32 [16384, 1536], P(('dp', 'tensor'))
- zx_updated: float32 [2, 1536, 2, 3072], P(None, 'dp', None, 'tensor')
- zx_first_new: float32 [2, 1536, 2, 3072], P(None, 'dp', None, 'tensor')
- zx_second_new: float32 [2, 1536, 2, 3072], P(None, 'dp', None, 'tensor')
- bc_updated: float32 [2, 1536, 256], P(None, ('dp', 'tensor'))
- bc_first_new: float32 [2, 1536, 256], P(None, ('dp', 'tensor'))
- bc_second_new: float32 [2, 1536, 256], P(None, ('dp', 'tensor'))
- dt_updated: float32 [2, 1536, 48], P(None, 'dp', 'tensor')
- dt_first_new: float32 [2, 1536, 48], P(None, 'dp', 'tensor')
- dt_second_new: float32 [2, 1536, 48], P(None, 'dp', 'tensor')
- out_updated: float32 [2, 3072, 1536], P(None, 'tensor', 'dp')
- out_first_new: float32 [2, 3072, 1536], P(None, 'tensor', 'dp')
- out_second_new: float32 [2, 3072, 1536], P(None, 'tensor', 'dp')
- chan_updated: float32 [2, 6, 3072], P(None, None, 'tensor')
- chan_first_new: float32 [2, 6, 3072], P(None, None, 'tensor')
- chan_second_new: float32 [2, 6, 3072], P(None, None, 'tensor')
- head_updated: float32 [2, 3, 48], P(None, None, 'tensor')
- head_first_new: float32 [2, 3, 48], P(None, None, 'tensor')
- head_second_new: float32 [2, 3, 48], P(None, None, 'tensor')
- bcpar_updated: float32 [2, 5, 256], P(None, None, ('dp', 'tensor'))
- bcpar_first_new: float32 [2, 5, 256], P(None, None, ('dp', 'tensor'))
- bcpar_second_new: float32 [2, 5, 256], P(None, None, ('dp', 'tensor'))
- gain_updated: float32 [2, 1536], P(None, ('dp', 'tensor'))
- gain_first_new: float32 [2, 1536], P(None, ('dp', 'tensor'))
- gain_second_new: float32 [2, 1536], P(None, ('dp', 'tensor'))
Inputs may be any that keep to these rules, and one draw needn't show every extreme that they name: `zx_first`: of both signs. `zx_second`: positive. `bc_first`: of both signs. `bc_second`: positive. `dt_first`: of both signs. `dt_second`: positive. `out_first`: of both signs. `out_second`: positive. `chan_first`: of both signs. `chan_second`: positive. `head_first`: of both signs. `head_second`: positive. `bcpar_first`: of both signs. `bcpar_second`: positive. `gain_first`: of both signs. `gain_second`: positive.
All inputs are finite; a program needn't handle non-finite values.
Results may differ from a plain program's by a relative error of at most 0.01.
The roundings to bfloat16 on the way count: a program that leaves them out, or rounds other values in their place, can miss the bound.
Values may be sent and summed in bfloat16 or wider, within the bound.
No kernel may reach another device: no remote copies, remote signals or barrier semaphores. Data moves between devices by JAX's collectives and lax.ppermute only.
A program may use at most 320 MiB of HBM per device.

v0:
```python
import jax
import jax.numpy as jnp
from jax import lax
from jax.sharding import PartitionSpec as P

BLOCK = 256
STEP = 10
INNER = 3072


NORM_EPS = 1e-05
BETA_ONE = 0.9
BETA_TWO = 0.95
ADAM_EPS = 1e-08
MATRIX_RATE = 0.02
MATRIX_DECAY = 0.1
SMALL_RATE = 0.3
HEAD_RATE = 2.0
PRECISE = lax.Precision.HIGHEST


def pre_norm(residual, gain_vals):
    return (
        residual
        * lax.rsqrt(jnp.mean(residual * residual, axis=1, keepdims=True) + NORM_EPS)
        * gain_vals[None, :]
    )


def causal_conv(values, tap_weights, conv_bias):
    tap_count = tap_weights.shape[0]
    padded = jnp.pad(values, ((tap_count - 1, 0), (0, 0)))
    summed = conv_bias[None, :] + tap_weights[tap_count - 1][None, :] * values
    for offset in range(tap_count - 1):
        summed = summed + tap_weights[offset][None, :] * padded[offset : offset + values.shape[0]]
    return summed


def block_step(carried_in, block_parts):
    old_state, decay_rate = carried_in
    block_x, block_dt, block_b, block_c = block_parts
    run_sum = jnp.cumsum(block_dt * decay_rate[None, :], axis=0).T
    positions = jnp.arange(block_dt.shape[0])
    causal = (positions[:, None] >= positions[None, :])[None, :, :]
    spread = jnp.where(causal, run_sum[:, :, None] - run_sum[:, None, :], 0.0)
    fading = jnp.where(causal, jnp.exp(spread), 0.0)
    affinity = jnp.dot(block_c, block_b.T, precision=PRECISE)
    mixing = affinity[None, :, :] * fading * block_dt.T[:, None, :]
    inside = jnp.einsum("hts,shp->thp", mixing, block_x, precision=PRECISE)
    from_state = jnp.exp(run_sum).T[:, :, None] * jnp.einsum(
        "tn,hpn->thp", block_c, old_state, precision=PRECISE
    )
    tail_scale = jnp.exp(run_sum[:, -1:] - run_sum) * block_dt.T
    fresh = jnp.einsum("hs,shp,sn->hpn", tail_scale, block_x, block_b, precision=PRECISE)
    new_state = jnp.exp(run_sum[:, -1])[:, None, None] * old_state + fresh
    return ((new_state, decay_rate), inside + from_state)


def scan_blocks(inputs_x, step_dt, decay_rate, input_b, input_c):
    seq_len, head_count, head_width = inputs_x.shape
    block_count = seq_len // BLOCK
    block_parts = (
        inputs_x.reshape(block_count, BLOCK, head_count, head_width),
        step_dt.reshape(block_count, BLOCK, head_count),
        input_b.reshape(block_count, BLOCK, input_b.shape[1]),
        input_c.reshape(block_count, BLOCK, input_c.shape[1]),
    )
    start_state = jnp.zeros((head_count, head_width, input_b.shape[1]), jnp.float32)
    final_carry, outputs = lax.scan(
        jax.checkpoint(block_step), (start_state, decay_rate), block_parts
    )
    return outputs.reshape(seq_len, head_count, head_width)


def mixer_local(proj_zx, proj_bc, proj_dt, chan_taps, head_vals, bc_vals):
    gate_z = proj_zx[:, 0, :]
    conv_x = jax.nn.silu(causal_conv(proj_zx[:, 1, :], chan_taps[:-1], chan_taps[-1]))
    conv_bc = jax.nn.silu(causal_conv(proj_bc, bc_vals[:-1], bc_vals[-1]))
    state_size = proj_bc.shape[1] // 2
    step_dt = jax.nn.softplus(proj_dt + head_vals[0][None, :])
    decay_rate = -jnp.exp(head_vals[1])
    head_count = proj_dt.shape[1]
    inputs_x = conv_x.reshape(conv_x.shape[0], head_count, conv_x.shape[1] // head_count)
    mixed = scan_blocks(
        inputs_x, step_dt, decay_rate, conv_bc[:, :state_size], conv_bc[:, state_size:]
    )
    mixed = mixed + head_vals[2][None, :, None] * inputs_x
    gated_vals = mixed.reshape(conv_x.shape) * jax.nn.silu(gate_z)
    return (gated_vals, jnp.sum(gated_vals * gated_vals, axis=1))


def gated_norm(gated_vals, square_sum, norm_scale):
    return gated_vals * lax.rsqrt(square_sum[:, None] / INNER + NORM_EPS) * norm_scale[None, :]


def adam_update(current, gradient, moment_old, square_old, step_rate, decay_coef):
    moment_new = BETA_ONE * moment_old + (1.0 - BETA_ONE) * gradient
    square_new = BETA_TWO * square_old + (1.0 - BETA_TWO) * gradient * gradient
    moment_hat = moment_new / (1.0 - BETA_ONE**STEP)
    square_hat = square_new / (1.0 - BETA_TWO**STEP)
    updated = current - step_rate * (
        moment_hat / (jnp.sqrt(square_hat) + ADAM_EPS) + decay_coef * current
    )
    return (updated, moment_new, square_new)


def contract_rows(left, right):
    return lax.dot_general(
        left, right, (((0,), (0,)), ((), ())), preferred_element_type=jnp.float32
    )


def contract_cols(left, right):
    return lax.dot_general(
        left, right, (((1,), (1,)), ((), ())), preferred_element_type=jnp.float32
    )


def local(
    resid_in,
    cotangent,
    w_zx,
    w_bc,
    w_dt,
    w_out,
    chan_par,
    head_par,
    bc_par,
    norm_gain,
    zx_first,
    zx_second,
    bc_first,
    bc_second,
    dt_first,
    dt_second,
    out_first,
    out_second,
    chan_first,
    chan_second,
    head_first,
    head_second,
    bcpar_first,
    bcpar_second,
    gain_first,
    gain_second,
):
    layer_total = w_zx.shape[0]
    gain_all, bcpar_all = (
        lax.all_gather(norm_gain, ("dp", "tensor"), axis=1, tiled=True),
        lax.all_gather(bc_par, ("dp", "tensor"), axis=2, tiled=True),
    )
    hidden = resid_in
    kept_state = []
    for layer_index in range(layer_total):
        big_weights = (
            lax.all_gather(w_zx[layer_index].astype(jnp.bfloat16), "dp", axis=0, tiled=True),
            lax.all_gather(w_dt[layer_index].astype(jnp.bfloat16), "dp", axis=0, tiled=True),
            lax.all_gather(w_out[layer_index].astype(jnp.bfloat16), "dp", axis=1, tiled=True),
        )
        bc_weight = lax.all_gather(
            w_bc[layer_index].astype(jnp.bfloat16), ("dp", "tensor"), axis=0, tiled=True
        )
        zx_weight, dt_weight, out_weight = big_weights
        normed, norm_pull = jax.vjp(pre_norm, hidden, gain_all[layer_index])
        normed_low = normed.astype(jnp.bfloat16)
        full_rows = lax.all_gather(normed_low, "tensor", axis=0, tiled=True)
        proj_zx = jnp.einsum(
            "td,dki->tki", full_rows, zx_weight, preferred_element_type=jnp.float32
        )
        proj_bc = jnp.dot(full_rows, bc_weight, preferred_element_type=jnp.float32)
        proj_dt = jnp.dot(full_rows, dt_weight, preferred_element_type=jnp.float32)
        chan_vals = chan_par[layer_index]
        mixer_out, mixer_pull = jax.vjp(
            mixer_local,
            proj_zx,
            proj_bc,
            proj_dt,
            chan_vals[:-1],
            head_par[layer_index],
            bcpar_all[layer_index],
        )
        gated_vals, square_part = mixer_out
        square_sum = lax.psum(square_part, "tensor")
        scaled, scale_pull = jax.vjp(gated_norm, gated_vals, square_sum, chan_vals[-1])
        scaled_low = scaled.astype(jnp.bfloat16)
        branch = lax.psum_scatter(
            jnp.dot(scaled_low, out_weight, preferred_element_type=jnp.float32),
            "tensor",
            scatter_dimension=0,
            tiled=True,
        )
        held_weights = None
        kept_state.append(
            (
                held_weights,
                bc_weight,
                norm_pull,
                mixer_pull,
                scale_pull,
                full_rows,
                normed_low,
                scaled_low,
            )
        )
        hidden = hidden + branch
    grad_hidden = cotangent
    zx_list = [None] * layer_total
    dt_list = [None] * layer_total
    out_list = [None] * layer_total
    bc_list = [None] * layer_total
    gain_list = [None] * layer_total
    bcpar_list = [None] * layer_total
    chan_list = [None] * layer_total
    head_list = [None] * layer_total
    for layer_index in reversed(range(layer_total)):
        (
            held_weights,
            bc_weight,
            norm_pull,
            mixer_pull,
            scale_pull,
            full_rows,
            normed_low,
            scaled_low,
        ) = kept_state[layer_index]
        zx_weight, dt_weight, out_weight = (
            lax.all_gather(w_zx[layer_index].astype(jnp.bfloat16), "dp", axis=0, tiled=True),
            lax.all_gather(w_dt[layer_index].astype(jnp.bfloat16), "dp", axis=0, tiled=True),
            lax.all_gather(w_out[layer_index].astype(jnp.bfloat16), "dp", axis=1, tiled=True),
        )
        branch_low = grad_hidden.astype(jnp.bfloat16)
        full_grad = lax.all_gather(branch_low, "tensor", axis=0, tiled=True)
        out_grad = contract_rows(scaled_low, full_grad)
        scaled_grad = contract_cols(full_grad, out_weight)
        gated_grad, square_grad, gain_five = scale_pull(scaled_grad)
        square_total = lax.psum(square_grad, "tensor")
        zx_grad, bc_grad, dt_grad, taps_grad, head_grad, bcpar_grad = mixer_pull(
            (gated_grad, square_total)
        )
        zx_low = zx_grad.astype(jnp.bfloat16)
        dt_low = dt_grad.astype(jnp.bfloat16)
        bc_piece = lax.psum_scatter(bc_grad, "tensor", scatter_dimension=0, tiled=True)
        bc_low = bc_piece.astype(jnp.bfloat16)
        summed = jnp.einsum("tki,dki->td", zx_low, zx_weight, preferred_element_type=jnp.float32)
        normed_grad = lax.psum_scatter(
            summed + contract_cols(dt_low, dt_weight), "tensor", scatter_dimension=0, tiled=True
        )
        normed_grad = normed_grad + contract_cols(bc_low, bc_weight)
        resid_part, gain_grad = norm_pull(normed_grad)
        grad_hidden = grad_hidden + resid_part
        zx_wgrad = jnp.einsum("td,tki->dki", full_rows, zx_low, preferred_element_type=jnp.float32)
        dt_wgrad = contract_rows(full_rows, dt_low)
        bc_wgrad = contract_rows(normed_low, bc_low)
        zx_list[layer_index], dt_list[layer_index], out_list[layer_index] = (
            lax.psum_scatter(zx_wgrad, "dp", scatter_dimension=0, tiled=True),
            lax.psum_scatter(dt_wgrad, "dp", scatter_dimension=0, tiled=True),
            lax.psum_scatter(out_grad, "dp", scatter_dimension=1, tiled=True),
        )
        bc_list[layer_index], gain_list[layer_index], bcpar_list[layer_index] = (
            lax.psum_scatter(bc_wgrad, ("dp", "tensor"), scatter_dimension=0, tiled=True),
            lax.psum_scatter(gain_grad, ("dp", "tensor"), scatter_dimension=0, tiled=True),
            lax.psum_scatter(bcpar_grad, ("dp", "tensor"), scatter_dimension=1, tiled=True),
        )
        chan_grad = jnp.concatenate([taps_grad, gain_five[None, :]], axis=0)
        chan_list[layer_index], head_list[layer_index] = lax.psum((chan_grad, head_grad), "dp")
    zx_stack = jnp.stack(zx_list, 0)
    dt_stack = jnp.stack(dt_list, 0)
    out_stack = jnp.stack(out_list, 0)
    zx_updated, zx_first_new, zx_second_new = adam_update(
        w_zx, zx_stack, zx_first, zx_second, MATRIX_RATE, MATRIX_DECAY
    )
    bc_updated, bc_first_new, bc_second_new = adam_update(
        w_bc, jnp.stack(bc_list, 0), bc_first, bc_second, MATRIX_RATE, MATRIX_DECAY
    )
    dt_updated, dt_first_new, dt_second_new = adam_update(
        w_dt, dt_stack, dt_first, dt_second, MATRIX_RATE, MATRIX_DECAY
    )
    out_updated, out_first_new, out_second_new = adam_update(
        w_out, out_stack, out_first, out_second, MATRIX_RATE, MATRIX_DECAY
    )
    chan_updated, chan_first_new, chan_second_new = adam_update(
        chan_par, jnp.stack(chan_list, 0), chan_first, chan_second, SMALL_RATE, 0.0
    )
    head_updated, head_first_new, head_second_new = adam_update(
        head_par, jnp.stack(head_list, 0), head_first, head_second, HEAD_RATE, 0.0
    )
    bcpar_updated, bcpar_first_new, bcpar_second_new = adam_update(
        bc_par, jnp.stack(bcpar_list, 0), bcpar_first, bcpar_second, SMALL_RATE, 0.0
    )
    gain_updated, gain_first_new, gain_second_new = adam_update(
        norm_gain, jnp.stack(gain_list, 0), gain_first, gain_second, SMALL_RATE, 0.0
    )
    return (
        hidden,
        grad_hidden,
        zx_updated,
        zx_first_new,
        zx_second_new,
        bc_updated,
        bc_first_new,
        bc_second_new,
        dt_updated,
        dt_first_new,
        dt_second_new,
        out_updated,
        out_first_new,
        out_second_new,
        chan_updated,
        chan_first_new,
        chan_second_new,
        head_updated,
        head_first_new,
        head_second_new,
        bcpar_updated,
        bcpar_first_new,
        bcpar_second_new,
        gain_updated,
        gain_first_new,
        gain_second_new,
    )


def solution(mesh):
    in_specs = (
        P(("dp", "tensor"), None),
        P(("dp", "tensor"), None),
        P(None, "dp", None, "tensor"),
        P(None, ("dp", "tensor"), None),
        P(None, "dp", "tensor"),
        P(None, "tensor", "dp"),
        P(None, None, "tensor"),
        P(None, None, "tensor"),
        P(None, None, ("dp", "tensor")),
        P(None, ("dp", "tensor")),
        P(None, "dp", None, "tensor"),
        P(None, "dp", None, "tensor"),
        P(None, ("dp", "tensor"), None),
        P(None, ("dp", "tensor"), None),
        P(None, "dp", "tensor"),
        P(None, "dp", "tensor"),
        P(None, "tensor", "dp"),
        P(None, "tensor", "dp"),
        P(None, None, "tensor"),
        P(None, None, "tensor"),
        P(None, None, "tensor"),
        P(None, None, "tensor"),
        P(None, None, ("dp", "tensor")),
        P(None, None, ("dp", "tensor")),
        P(None, ("dp", "tensor")),
        P(None, ("dp", "tensor")),
    )
    out_specs = (
        P(("dp", "tensor"), None),
        P(("dp", "tensor"), None),
        P(None, "dp", None, "tensor"),
        P(None, "dp", None, "tensor"),
        P(None, "dp", None, "tensor"),
        P(None, ("dp", "tensor"), None),
        P(None, ("dp", "tensor"), None),
        P(None, ("dp", "tensor"), None),
        P(None, "dp", "tensor"),
        P(None, "dp", "tensor"),
        P(None, "dp", "tensor"),
        P(None, "tensor", "dp"),
        P(None, "tensor", "dp"),
        P(None, "tensor", "dp"),
        P(None, None, "tensor"),
        P(None, None, "tensor"),
        P(None, None, "tensor"),
        P(None, None, "tensor"),
        P(None, None, "tensor"),
        P(None, None, "tensor"),
        P(None, None, ("dp", "tensor")),
        P(None, None, ("dp", "tensor")),
        P(None, None, ("dp", "tensor")),
        P(None, ("dp", "tensor")),
        P(None, ("dp", "tensor")),
        P(None, ("dp", "tensor")),
    )
    return jax.shard_map(local, mesh=mesh, in_specs=in_specs, out_specs=out_specs, check_vma=False)
```

profile of v0, /device:TPU:0, one launch (start us, length us, event | category | flops | bytes accessed | tf_op | source)
XLA Modules:
  0.0 3604.3 jit_solution(17608271968862989228)
XLA Ops:
  10.1 43.5 %all-gather.8 = f32[32,48,2]{1,2,0:T(2,128)S(1)} all-gather(f32[1,48,2]{1,2,0:T(2,128)} %bitcast.875), channel_id=1, replica_groups=mesh['dp'=8,'tensor'=4] {'dp','tensor'}, dimensions={0}, use_global_device_ids=true | all-gather | bytes 12672 | tf_op jit(solution)/shard_map/all_gather | solution.py:149
  64.6 38.0 %all_gather.52 = f32[2,5,256]{1,0,2:T(2,128)S(1)} all-gather(f32[2,5,8]{1,0,2:T(2,128)S(1)} %copy.472), channel_id=1, replica_groups=mesh['dp'=8,'tensor'=4] {'dp','tensor'}, dimensions={2}, use_global_device_ids=true | all-gather | bytes 10560 | tf_op jit(solution)/shard_map/all_gather | solution.py:150
  113.6 43.6 %all-gather.2 = bf16[1,1536,256]{2,1,0:T(8,128)(2,1)S(1)} all-gather(bf16[1,48,256]{2,1,0:T(8,128)(2,1)S(1)} %get-tuple-element.1872), channel_id=4, replica_groups=mesh['dp'=8,'tensor'=4] {'dp','tensor'}, dimensions={1}, use_global_device_ids=true | all-gather | bytes 811008 | tf_op jit(solution)/shard_map/all_gather | solution.py:160
  157.2 34.2 all-gather
  254.2 274.1 %while.92 = (s32[]{:T(128)}, f32[12,64,128]{2,1,0:T(8,128)S(1)}, f32[8,256,12,64]{1,0,3,2:T(8,128)}, f32[8,12,64,128]{3,2,1,0:T(8,128)}, f32[8,12]{1,0:T(8,128)}...) while((s32[]{:T(128)}, f32[12,64,128]{2,1,0:T(8,128)S(1)}, ...), condition=%wide.region_4.6_spmd.clone.clone, body=%wide.region_1.5_spmd.clone.clone.sunk | while | flops 1314038784 | bytes 10506048 | solution.py:69
  270.0 18.5 dynamic_update_slice.162
  304.2 18.5 dynamic_update_slice.162
  338.4 18.5 dynamic_update_slice.162
  372.6 18.5 dynamic_update_slice.162
  406.8 18.5 dynamic_update_slice.162
  441.0 18.5 dynamic_update_slice.162
  475.2 18.5 dynamic_update_slice.162
  509.5 18.5 dynamic_update_slice.162
  570.6 96.7 %reduce-scatter.21.cloned.1.call-done = f32[512,1536]{1,0:T(8,128)} async-done(((f32[2048,1536]{1,0:T(8,128)}), f32[512,1536]{1,0:T(8,128)}) %reduce-scatter.21.cloned.1.call-update) | async-done | bytes 3145744 | tf_op jit(solution)/shard_map/reduce_scatter | solution.py:186
  676.5 32.3 all-gather.4
  709.3 45.4 %all-gather.6 = bf16[1,1536,256]{2,1,0:T(8,128)(2,1)S(1)} all-gather(bf16[1,48,256]{2,1,0:T(8,128)(2,1)} %get-tuple-element.1871), channel_id=8, replica_groups=mesh['dp'=8,'tensor'=4] {'dp','tensor'}, dimensions={1}, use_global_device_ids=true | all-gather | bytes 811008 | tf_op jit(solution)/shard_map/all_gather | solution.py:160
  768.2 36.6 %all-gather.30.cloned.1.call-done = bf16[1,1536,2,768]{3,1,2,0:T(8,128)(2,1)} async-done(((bf16[1,192,2,768]{3,1,2,0:T(8,128)(2,1)}), bf16[1,1536,2,768]{3,1,2,0:T(8,128)(2,1)}) %all-gather.30.cloned.1.call-update) | async-done | bytes 4718608 | tf_op jit(solution)/shard_map/all_gather | solution.py:156
  853.7 274.4 %while.93 = (s32[]{:T(128)}, f32[12,64,128]{2,1,0:T(8,128)S(1)}, f32[8,256,12,64]{1,0,3,2:T(8,128)}, f32[8,12,64,128]{3,2,1,0:T(8,128)}, f32[8,12]{1,0:T(8,128)}...) while((s32[]{:T(128)}, f32[12,64,128]{2,1,0:T(8,128)S(1)}, ...), condition=%wide.region_12.14_spmd.clone.clone, body=%wide.region_9.13_spmd.clone.clone.sunk | while | flops 1314038784 | bytes 10506048 | solution.py:69
  869.8 18.6 dynamic_update_slice.165
  904.1 18.5 dynamic_update_slice.165
  938.4 18.5 dynamic_update_slice.165
  972.6 18.5 dynamic_update_slice.165
  1006.8 18.5 dynamic_update_slice.165
  1041.1 18.5 dynamic_update_slice.165
  1075.4 18.5 dynamic_update_slice.165
  1109.6 18.5 dynamic_update_slice.165
  1216.4 464.4 %while.90 = (s32[]{:T(128)}, f32[12,64,128]{2,1,0:T(8,128)S(1)}, f32[12]{0:T(128)}, f32[8,256,12,64]{1,0,3,2:T(8,128)}, f32[8,256,12]{1,0,2:T(8,128)}, /*index=5...) while((s32[]{:T(128)}, f32[12,64,128]{2,1,0:T(8,128)S(1)}, ...), condition=%wide.region_31.33_spmd.clone, body=%wide.region_18.32_spmd.clone.sunk | while | flops 3038798848 | bytes 26197460 | solution.py:69
  1777.7 82.2 %reduce-scatter.25.cloned.1.call-done = f32[512,1536]{1,0:T(8,128)} async-done(((f32[2048,1536]{1,0:T(8,128)}), f32[512,1536]{1,0:T(8,128)}) %reduce-scatter.25.cloned.1.call-update) | async-done | bytes 3145744 | tf_op jit(solution)/shard_map/reduce_scatter | solution.py:245
  1865.5 96.3 %reduce-scatter.23.cloned.1.call-done = f32[512,1536]{1,0:T(8,128)} async-done(((f32[2048,1536]{1,0:T(8,128)}), f32[512,1536]{1,0:T(8,128)}) %reduce-scatter.23.cloned.1.call-update) | async-done | bytes 3145744 | tf_op jit(solution)/shard_map/reduce_scatter | solution.py:186
  1969.8 46.4 %all-gather.24.cloned.1.call-done = bf16[2048,1536]{1,0:T(8,128)(2,1)} async-done(((bf16[512,1536]{1,0:T(8,128)(2,1)}), bf16[2048,1536]{1,0:T(8,128)(2,1)}) %all-gather.24.cloned.1.call-update) | async-done | bytes 6291472 | tf_op jit(solution)/shard_map/all_gather | solution.py:232
  2073.0 463.5 %while.91 = (s32[]{:T(128)}, f32[12,64,128]{2,1,0:T(8,128)S(1)}, f32[12]{0:T(128)}, f32[8,256,12,64]{1,0,3,2:T(8,128)}, f32[8,256,12]{1,0,2:T(8,128)}, /*index=5...) while((s32[]{:T(128)}, f32[12,64,128]{2,1,0:T(8,128)S(1)}, ...), condition=%wide.region_50.52_spmd.clone, body=%wide.region_37.51_spmd.clone.sunk | while | flops 3038798848 | bytes 26197460 | solution.py:69
  2112.3 18.5 dynamic_update_slice.159
  2170.2 18.5 dynamic_update_slice.159
  2228.2 18.5 dynamic_update_slice.159
  2286.1 18.5 dynamic_update_slice.159
  2344.1 18.5 dynamic_update_slice.159
  2402.0 18.5 dynamic_update_slice.159
  2459.9 18.5 dynamic_update_slice.159
  2517.9 18.5 dynamic_update_slice.159
  2734.3 39.2 %all-reduce.63 = (f32[1,6,768]{2,1,0:T(8,128)}, f32[1,6,768]{2,1,0:T(8,128)}, f32[1,3,12]{2,1,0:T(4,128)}, f32[1,3,12]{2,1,0:T(4,128)}) all-reduce(f32[1,6,768]{2,1,0:T(8,128)} %get-tuple-element.1891, f32[1,6,768]{2,1,0:T(8,128)} %get-tuple-element.1892, ...), channel_id=1, replica_groups=mesh['dp'=8,'tensor'=4] {'dp'}, use_global_device_ids=true, to_apply=%region_68.70 | all-reduce | flops 9288 | bytes 74304 | tf_op jit(solution)/shard_map/psum | solution.py:265
  2787.9 24.6 reduce-scatter.39.cloned.1.call-done
  2812.6 101.8 %reduce-scatter.37.cloned.1.call-done = f32[48,256]{1,0:T(8,128)} async-done(((f32[1536,256]{1,0:T(8,128)}), f32[48,256]{1,0:T(8,128)}) %reduce-scatter.37.cloned.1.call-update) | async-done | bytes 49168 | tf_op jit(solution)/shard_map/reduce_scatter | solution.py:260
  2916.1 96.2 %reduce-scatter.43.cloned.1.call-done = f32[768,192]{0,1:T(8,128)} async-done(((f32[768,1536]{0,1:T(8,128)}), f32[768,192]{0,1:T(8,128)}) %reduce-scatter.43.cloned.1.call-update) | async-done | bytes 589840 | tf_op jit(solution)/shard_map/reduce_scatter | solution.py:257
  3012.3 98.7 %reduce-scatter.41.cloned.1.call-done = f32[768,192]{0,1:T(8,128)} async-done(((f32[768,1536]{0,1:T(8,128)}), f32[768,192]{0,1:T(8,128)}) %reduce-scatter.41.cloned.1.call-update) | async-done | bytes 589840 | tf_op jit(solution)/shard_map/reduce_scatter | solution.py:257
  3115.4 162.2 %reduce-scatter.35.cloned.1.call-done = f32[192,2,768]{2,0,1:T(8,128)} async-done(((f32[1536,2,768]{2,0,1:T(8,128)}), f32[192,2,768]{2,0,1:T(8,128)}) %reduce-scatter.35.cloned.1.call-update) | async-done | bytes 1179664 | tf_op jit(solution)/shard_map/reduce_scatter | solution.py:255
  3277.6 166.2 %reduce-scatter.33.cloned.1.call-done = f32[192,2,768]{2,0,1:T(8,128)} async-done(((f32[1536,2,768]{2,0,1:T(8,128)}), f32[192,2,768]{2,0,1:T(8,128)}) %reduce-scatter.33.cloned.1.call-update) | async-done | bytes 1179664 | tf_op jit(solution)/shard_map/reduce_scatter | solution.py:255
  3458.0 86.6 %reduce-scatter.29.cloned.1.call-done = f32[512,1536]{1,0:T(8,128)} async-done(((f32[2048,1536]{1,0:T(8,128)}), f32[512,1536]{1,0:T(8,128)}) %reduce-scatter.29.cloned.1.call-update) | async-done | bytes 3145744 | tf_op jit(solution)/shard_map/reduce_scatter | solution.py:245
  3549.6 39.8 %all-reduce.62 = (f32[5,256]{1,0:T(8,128)S(1)}, f32[5,256]{1,0:T(8,128)S(1)}, f32[1536]{0:T(1024)S(1)}, f32[1536]{0:T(1024)S(1)}) all-reduce(f32[5,256]{1,0:T(8,128)S(1)} %copy-done.79, f32[5,256]{1,0:T(8,128)S(1)} %copy-done.80, f32[1536]{0:T(1024)S(1)} %copy-done.78, ...), channel_id=25, replica_groups=mesh['dp'=8,'tensor'=4] {'dp','tensor'}, use_global_device_ids=true, to_apply=%region_95.97.clone | all-reduce | flops 5632 | bytes 45056
  (1784 shorter events, 1728.2 us)
Async XLA Ops:
  7.2 184.7 %all-gather.18.cloned.1.call-start = ((), (), s32[]{:S(2)}) async-start(), calls=%async_computation.14 | async-start | bytes 7864320 | tf_op jit(solution)/shard_map/all_gather | solution.py:166
  53.8 615.9 %copy-start.39 = (f32[1536]{0:T(1024)}, f32[1536]{0:T(1024)S(1)}, u32[]{:S(2)}) copy-start(f32[1536]{0:T(1024)S(1)} %get-tuple-element.1652) | copy-start | bytes 18436
  57.8 147.5 %all-gather.26.cloned.1.call-start = ((), (), s32[]{:S(2)}) async-start(), calls=%async_computation.30 | async-start | bytes 5308416 | tf_op jit(solution)/shard_map/all_gather | solution.py:156
  59.2 500.0 %all-gather.28.cloned.1.call-start = ((), (), s32[]{:S(2)}) async-start(), calls=%async_computation.31 | async-start | bytes 2654208 | tf_op jit(solution)/shard_map/all_gather | solution.py:158
  60.2 607.1 %reduce-scatter.21.cloned.1.call-start = ((), (), s32[]{:S(2)}) async-start(), calls=%async_computation.15 | async-start | bytes 15728640 | tf_op jit(solution)/shard_map/reduce_scatter | solution.py:186
  61.5 482.0 %copy-start.44 = (f32[768]{0:T(1024)}, f32[768]{0:T(1024)S(1)}, u32[]{:S(2)}) copy-start(f32[768]{0:T(1024)S(1)} %mul.1697) | copy-start | bytes 9220
  63.5 161.0 %copy-start.54 = (f32[768]{0:T(1024)}, f32[768]{0:T(1024)S(1)}, u32[]{:S(2)}) copy-start(f32[768]{0:T(1024)S(1)} %get-tuple-element.1650) | copy-start | bytes 9220
  63.5 161.0 %copy-start.56 = (f32[768]{0:T(1024)}, f32[768]{0:T(1024)S(1)}, u32[]{:S(2)}) copy-start(f32[768]{0:T(1024)S(1)} %get-tuple-element.1647) | copy-start | bytes 9220
  63.5 161.0 %copy-start.58 = (f32[768]{0:T(1024)}, f32[768]{0:T(1024)S(1)}, u32[]{:S(2)}) copy-start(f32[768]{0:T(1024)S(1)} %get-tuple-element.1648) | copy-start | bytes 9220
  63.6 161.0 %copy-start.60 = (f32[768]{0:T(1024)}, f32[768]{0:T(1024)S(1)}, u32[]{:S(2)}) copy-start(f32[768]{0:T(1024)S(1)} %get-tuple-element.1649) | copy-start | bytes 9220
  63.6 495.7 %copy-start.91 = (f32[768]{0:T(1024)}, f32[768]{0:T(1024)S(1)}, u32[]{:S(2)}) copy-start(f32[768]{0:T(1024)S(1)} %get-tuple-element.1646) | copy-start | bytes 9220
  63.6 760.6 %copy-start.62 = (f32[768]{0:T(1024)}, f32[768]{0:T(1024)S(1)}, u32[]{:S(2)}) copy-start(f32[768]{0:T(1024)S(1)} %get-tuple-element.1644) | copy-start | bytes 9220
  63.6 760.6 %copy-start.64 = (f32[768]{0:T(1024)}, f32[768]{0:T(1024)S(1)}, u32[]{:S(2)}) copy-start(f32[768]{0:T(1024)S(1)} %get-tuple-element.1641) | copy-start | bytes 9220
  63.6 760.6 %copy-start.66 = (f32[768]{0:T(1024)}, f32[768]{0:T(1024)S(1)}, u32[]{:S(2)}) copy-start(f32[768]{0:T(1024)S(1)} %get-tuple-element.1642) | copy-start | bytes 9220
  63.6 760.6 %copy-start.68 = (f32[768]{0:T(1024)}, f32[768]{0:T(1024)S(1)}, u32[]{:S(2)}) copy-start(f32[768]{0:T(1024)S(1)} %get-tuple-element.1643) | copy-start | bytes 9220
  570.5 96.8 %copy-start = (f32[512,1536]{1,0:T(8,128)S(1)}, f32[512,1536]{1,0:T(8,128)}, u32[]{:S(2)}) copy-start(f32[512,1536]{1,0:T(8,128)} %param.35) | copy-start | bytes 9437188
  570.6 184.1 %all-gather.20.cloned.1.call-start = ((), (), s32[]{:S(2)}) async-start(), calls=%async_computation.16 | async-start | bytes 7864320 | tf_op jit(solution)/shard_map/all_gather | solution.py:166
  672.8 132.0 %all-gather.30.cloned.1.call-start = ((), (), s32[]{:S(2)}) async-start(), calls=%async_computation.32 | async-start | bytes 5308416 | tf_op jit(solution)/shard_map/all_gather | solution.py:156
  673.4 485.4 %all-gather.32.cloned.1.call-start = ((), (), s32[]{:S(2)}) async-start(), calls=%async_computation.33 | async-start | bytes 2654208 | tf_op jit(solution)/shard_map/all_gather | solution.py:158
  674.2 484.7 %all-gather.22.cloned.1.call-start = ((), (), s32[]{:S(2)}) async-start(), calls=%async_computation.18 | async-start | bytes 7864320 | tf_op jit(solution)/shard_map/all_gather | solution.py:232
  675.6 1102.2 %reduce-scatter.27.cloned.1.call-start = ((), (), s32[]{:S(2)}) async-start(), calls=%async_computation.20 | async-start | bytes 2621440 | tf_op jit(solution)/shard_map/reduce_scatter | solution.py:242
  676.5 501.0 %copy-start.47 = (f32[768]{0:T(1024)}, f32[768]{0:T(1024)S(1)}, u32[]{:S(2)}) copy-start(f32[768]{0:T(1024)S(1)} %mul.1742) | copy-start | bytes 9220
  1691.4 168.5 %reduce-scatter.25.cloned.1.call-start = ((), (), s32[]{:S(2)}) async-start(), calls=%async_computation.19 | async-start | bytes 15728640 | tf_op jit(solution)/shard_map/reduce_scatter | solution.py:245
  1762.3 199.5 %reduce-scatter.23.cloned.1.call-start = ((), (), s32[]{:S(2)}) async-start(), calls=%async_computation.17 | async-start | bytes 15728640 | tf_op jit(solution)/shard_map/reduce_scatter | solution.py:186
  1777.7 87.8 %copy-start.85 = (f32[512]{0:T(512)S(1)}, f32[512]{0:T(512)}, u32[]{:S(2)}) copy-start(f32[512]{0:T(512)} %copy-done.84) | copy-start | bytes 6148
  1777.7 238.6 %all-gather.24.cloned.1.call-start = ((), (), s32[]{:S(2)}) async-start(), calls=%async_computation.21 | async-start | bytes 7864320 | tf_op jit(solution)/shard_map/all_gather | solution.py:232
  1969.7 609.2 %reduce-scatter.31.cloned.1.call-start = ((), (), s32[]{:S(2)}) async-start(), calls=%async_computation.23 | async-start | bytes 2621440 | tf_op jit(solution)/shard_map/reduce_scatter | solution.py:242
  2546.2 171.9 %reduce-scatter.47.cloned.1.call-start = ((), (), s32[]{:S(2)}) async-start(), calls=%async_computation.35 | async-start | bytes 884736
  2551.8 231.8 %reduce-scatter.45.cloned.1.call-start = ((), (), s32[]{:S(2)}) async-start(), calls=%async_computation.34 | async-start | bytes 884736
  2558.8 253.7 %reduce-scatter.39.cloned.1.call-start = ((), (), s32[]{:S(2)}) async-start(), calls=%async_computation.27 | async-start | bytes 1622016 | tf_op jit(solution)/shard_map/reduce_scatter | solution.py:260
  2561.7 352.6 %reduce-scatter.37.cloned.1.call-start = ((), (), s32[]{:S(2)}) async-start(), calls=%async_computation.26 | async-start | bytes 1622016 | tf_op jit(solution)/shard_map/reduce_scatter | solution.py:260
  2581.8 430.6 %reduce-scatter.43.cloned.1.call-start = ((), (), s32[]{:S(2)}) async-start(), calls=%async_computation.29 | async-start | bytes 5308416 | tf_op jit(solution)/shard_map/reduce_scatter | solution.py:257
  2592.7 518.3 %reduce-scatter.41.cloned.1.call-start = ((), (), s32[]{:S(2)}) async-start(), calls=%async_computation.28 | async-start | bytes 5308416 | tf_op jit(solution)/shard_map/reduce_scatter | solution.py:257
  2604.0 673.6 %reduce-scatter.35.cloned.1.call-start = ((), (), s32[]{:S(2)}) async-start(), calls=%async_computation.25 | async-start | bytes 10616832 | tf_op jit(solution)/shard_map/reduce_scatter | solution.py:255
  2621.4 822.4 %reduce-scatter.33.cloned.1.call-start = ((), (), s32[]{:S(2)}) async-start(), calls=%async_computation.24 | async-start | bytes 10616832 | tf_op jit(solution)/shard_map/reduce_scatter | solution.py:255
  2687.0 857.6 %reduce-scatter.29.cloned.1.call-start = ((), (), s32[]{:S(2)}) async-start(), calls=%async_computation.22 | async-start | bytes 15728640 | tf_op jit(solution)/shard_map/reduce_scatter | solution.py:245
  2707.9 403.1 %copy-start.21 = (f32[2,768,192]{1,2,0:T(8,128)S(1)}, f32[2,768,192]{1,2,0:T(8,128)}, u32[]{:S(2)}) copy-start(f32[2,768,192]{1,2,0:T(8,128)} %param.40) | copy-start | bytes 3538948
  2707.9 735.9 %copy-start.10 = (f32[2,192,2,768]{3,2,1,0:T(2,128)S(1)}, f32[2,192,2,768]{3,2,1,0:T(2,128)}, u32[]{:S(2)}) copy-start(f32[2,192,2,768]{3,2,1,0:T(2,128)} %param.37) | copy-start | bytes 7077892
  3447.9 96.7 %copy-start.1 = (f32[512,1536]{1,0:T(8,128)S(1)}, f32[512,1536]{1,0:T(8,128)}, u32[]{:S(2)}) copy-start(f32[512,1536]{1,0:T(8,128)} %param.35) | copy-start | bytes 9437188
  3447.9 96.7 %copy-start.38 = (f32[1536]{0:T(1024)S(1)}, f32[1536]{0:T(1024)}, u32[]{:S(2)}) copy-start(f32[1536]{0:T(1024)} %copy-done.37) | copy-start | bytes 18436
  3447.9 96.7 %copy-start.71 = (f32[512]{0:T(512)S(1)}, f32[512]{0:T(512)}, u32[]{:S(2)}) copy-start(f32[512]{0:T(512)} %copy-done.70) | copy-start | bytes 6148
  3457.9 91.6 %copy-start.87 = (f32[512]{0:T(512)S(1)}, f32[512]{0:T(512)}, u32[]{:S(2)}) copy-start(f32[512]{0:T(512)} %copy-done.86) | copy-start | bytes 6148
  3457.9 91.7 %copy-start.78 = (f32[1536]{0:T(1024)S(1)}, f32[1536]{0:T(1024)}, u32[]{:S(2)}) copy-start(f32[1536]{0:T(1024)} %get-tuple-element.1608) | copy-start | bytes 18436
  3457.9 91.7 %copy-start.79 = (f32[5,256]{1,0:T(8,128)S(1)}, f32[5,256]{1,0:T(8,128)}, u32[]{:S(2)}) copy-start(f32[5,256]{1,0:T(8,128)} %pad_add_fusion.12) | copy-start | bytes 15364
  3457.9 91.7 %copy-start.80 = (f32[5,256]{1,0:T(8,128)S(1)}, f32[5,256]{1,0:T(8,128)}, u32[]{:S(2)}) copy-start(f32[5,256]{1,0:T(8,128)} %pad_add_fusion.13) | copy-start | bytes 15364
  3457.9 131.5 %copy-start.83 = (f32[2,5,8]{2,0,1:T(2,128)S(1)}, f32[2,5,8]{2,0,1:T(2,128)}, u32[]{:S(2)}) copy-start(f32[2,5,8]{2,0,1:T(2,128)} %param.43) | copy-start | bytes 964
  3457.9 131.5 %copy-start.114 = (f32[2,5,8]{2,0,1:T(2,128)S(1)}, f32[2,5,8]{2,0,1:T(2,128)}, u32[]{:S(2)}) copy-start(f32[2,5,8]{2,0,1:T(2,128)} %param.57) | copy-start | bytes 964
  3457.9 131.5 %copy-start.115 = (f32[2,5,8]{2,0,1:T(2,128)S(1)}, f32[2,5,8]{2,0,1:T(2,128)}, u32[]{:S(2)}) copy-start(f32[2,5,8]{2,0,1:T(2,128)} %param.58) | copy-start | bytes 964
  (152 other events, 2153.8 us)
Sparse Core Ops, SparseCore 0:
  57.9 45.0 all-gather.17
  105.9 95.6 all-gather.25
  204.3 51.4 all-gather.27
  570.7 96.5 reduce-scatter.20
  673.0 47.9 all-gather.19
  723.0 81.7 all-gather.29
  807.0 50.2 all-gather.31
  858.8 44.8 all-gather.21
  1691.6 29.3 reduce-scatter.26
  1762.4 97.4 reduce-scatter.24
  1862.7 99.0 reduce-scatter.22
  1969.8 46.3 all-gather.23
  2546.3 32.5 reduce-scatter.30
  2582.6 62.5 reduce-scatter.46
  2649.3 61.4 reduce-scatter.44
  2716.5 96.0 reduce-scatter.38
  2818.2 96.0 reduce-scatter.36
  2917.8 94.4 reduce-scatter.42
  3015.9 95.0 reduce-scatter.40
  3114.5 163.0 reduce-scatter.34
  3281.2 162.5 reduce-scatter.32
  3446.4 98.1 reduce-scatter.28
where the time goes:
time: 3640 us; the launch traced here: 3600 us
  waiting for transfers between devices  1110 us (30%)
  local copies, waits for them, and re-layouts  1060 us (29%)
  matrix products  685 us (19%)
  other arithmetic  386 us (11%)
  blocking collectives  340 us (9%)
    dynamic_update_slice x112, local copies, waits for them, and re-layouts, scan_blocks(): lax.scan(jax.checkpoint(block_step), (start_state, decay_rate), block_parts)  663 us
    reduce_scatter x2, waiting for transfers between devices, local(): lax.psum_scatter(zx_wgrad, 'dp', scatter_dimension=0, tiled=True)  328 us
    dot_general x48, matrix products, block_step(): inside = jnp.einsum('hts,shp->thp', mixing, block_x, precision=PRECISE)  234 us
    reduce_scatter x2, waiting for transfers between devices, local(): lax.psum_scatter(out_grad, 'dp', scatter_dimension=1, tiled=True)  195 us
    reduce_scatter x2, waiting for transfers between devices, local(): lax.psum_scatter(jnp.dot(scaled_low, out_weight, preferred_element_type=j...  193 us
    reduce_scatter x2, waiting for transfers between devices, local(): lax.psum_scatter(summed + contract_cols(dt_low, dt_weight), 'tensor', sca...  169 us
    reduce_scatter x2, waiting for transfers between devices, local(): lax.psum_scatter(bc_wgrad, ('dp', 'tensor'), scatter_dimension=0, tiled=T...  126 us
    unnamed x269, local copies, waits for them, and re-layouts  107 us
  transfers between devices with their start and end apart: 22, of which 13 were waited for; matrix products, arithmetic and copies ran while one was open for 29% of the time, Pallas kernels for 0%

commit v1 on v0

v1 whole, which is shorter than its diff:
```python
import functools
import math

import jax
import jax.numpy as jnp
from jax import lax
from jax.experimental import pallas as pl
from jax.experimental.layout import Layout, with_layout_constraint
from jax.experimental.pallas import tpu as pltpu
from jax.sharding import PartitionSpec as P

BLOCK = 256
STEP = 10
INNER = 3072
LANES = 128
HEAD_WIDTH = 64

NORM_EPS = 1e-05
BETA_ONE = 0.9
BETA_TWO = 0.95
ADAM_EPS = 1e-08
MATRIX_RATE = 0.02
MATRIX_DECAY = 0.1
SMALL_RATE = 0.3
HEAD_RATE = 2.0
PRECISE = lax.Precision.HIGHEST
LOG2E = math.log2(math.e)
LOW = jnp.bfloat16
F32 = jnp.float32
VMEM_BYTES = 56 * 1024 * 1024


def dot(left, right, left_dim=1, right_dim=0, precision=None):
    return lax.dot_general(
        left,
        right,
        (((left_dim,), (right_dim,)), ((), ())),
        preferred_element_type=F32,
        precision=precision,
    )


def split(vals):
    high = vals.astype(LOW)
    return high, (vals - high.astype(F32)).astype(LOW)


def halves(vals):
    return jnp.concatenate(split(vals), axis=1)


def left_parts(vals, axis):
    high, low = split(vals)
    return jnp.concatenate([high, low, high], axis=axis)


def right_parts(vals, axis):
    high, low = split(vals)
    return jnp.concatenate([high, high, low], axis=axis)


def mix_pair(mixing, pair):
    out = dot(jnp.concatenate(split(mixing), axis=1), jnp.concatenate([pair, pair], axis=0))
    return out[:, :LANES] + out[:, LANES:]


def softplus(vals):
    return jnp.maximum(vals, 0.0) + jnp.log1p(jnp.exp(-jnp.abs(vals)))


def conv_block(ext, conv_ref):
    rows = ext.shape[0] - 8
    total = conv_ref[4:5, :] + conv_ref[3:4, :] * ext[8 : 8 + rows, :]
    for tap in range(3):
        total = total + conv_ref[tap : tap + 1, :] * ext[5 + tap : 5 + tap + rows, :]
    return total


def decay_sums(step_dt, head_ref):
    size = step_dt.shape[0]
    row = lax.broadcasted_iota(jnp.int32, (size, size), 0)
    col = lax.broadcasted_iota(jnp.int32, (size, size), 1)
    lower = jnp.where(row >= col, 1.0, 0.0).astype(F32)
    return dot(lower, step_dt * head_ref[1:2, :], precision=PRECISE)


def scan_kernel(
    me_ref, rows_ref, weight_ref, conv_ref, head_ref, skip_ref, spread_ref,
    pre_ref, y_ref, kept_ref, state, ext,
):
    width = y_ref.shape[1]
    conv_width = ext.shape[1]
    half = (conv_width - width) // 2
    size = rows_ref.shape[0]

    @pl.when(pl.program_id(0) == 0)
    def _():
        state[...] = jnp.zeros_like(state)
        ext[0:8, :] = jnp.zeros((8, conv_width), F32)

    @pl.when(pl.program_id(0) > 0)
    def _():
        ext[0:8, :] = ext[size : size + 8, :]

    pre = dot(rows_ref[...], weight_ref[...])
    pre_ref[...] = pre
    ext[8 : 8 + size, :] = pre[:, :conv_width]
    conv = conv_block(ext, conv_ref)
    act = conv * jax.nn.sigmoid(conv)
    inputs_x = act[:, :width]
    left_c = left_parts(act[:, width + half :], 1)
    step_dt = softplus(pre[:, conv_width:] + head_ref[0:1, :])
    cum = decay_sums(step_dt, head_ref)
    cum_t = cum.T
    last = cum[size - 1 : size, :]
    spread = spread_ref[...]
    dt_wide = dot(halves(step_dt), spread)
    cum_wide = dot(halves(jnp.exp2(cum)), spread)
    tail_wide = dot(halves(jnp.exp2(last - cum)), spread)
    scaled_x = inputs_x * dt_wide
    high_x, low_x = split(scaled_x)
    row = lax.broadcasted_iota(jnp.int32, (size, size), 0)
    col = lax.broadcasted_iota(jnp.int32, (size, size), 1)
    affinity = jnp.where(row >= col, dot(left_c, right_parts(act[:, width : width + half], 1), 1, 1), 0.0)
    old_state = state[...]
    kept_ref[0] = old_state
    y_ref[...] = (
        cum_wide * dot(left_c, right_parts(old_state, 0)) + skip_ref[0:1, :] * inputs_x
    )
    state[...] = cum_wide[size - 1 : size, :] * old_state + dot(
        left_parts(act[:, width : width + half], 0), right_parts(scaled_x * tail_wide, 0), 0, 0
    )
    first_half = lax.broadcasted_iota(jnp.int32, (size, LANES), 1) < HEAD_WIDTH
    for pair in range(width // LANES):
        cols = slice(pair * LANES, (pair + 1) * LANES)
        pair_x = jnp.concatenate([high_x[:, cols], low_x[:, cols]], axis=1)
        parts = []
        for head in (2 * pair, 2 * pair + 1):
            gap = cum[:, head : head + 1] - cum_t[head : head + 1, :]
            parts.append(mix_pair(affinity * jnp.exp2(jnp.minimum(gap, 0.0)), pair_x))
        y_ref[:, cols] += jnp.where(first_half, parts[0], parts[1])


def gate_kernel(rows_ref, y_ref, z_weight_ref, out_weight_ref, gain_ref, *refs):
    z_ref, sent_ref, own_ref, sq_ref = refs[-4:]
    gate_z = dot(rows_ref[...], z_weight_ref[...])
    z_ref[...] = gate_z
    gated = y_ref[...] * (gate_z * jax.nn.sigmoid(gate_z))
    sq_ref[...] = jnp.sum(gated * gated, axis=1, keepdims=True)
    low_gated = (gated * gain_ref[...]).astype(LOW)
    partial = dot(low_gated, out_weight_ref[...], 1, 1).astype(LOW)
    sending = pl.program_id(0) < pl.num_programs(0) // 2

    @pl.when(sending)
    def _():
        sent_ref[...] = partial

    @pl.when(jnp.logical_not(sending))
    def _():
        own_ref[...] = partial


def gate_back_kernel(
    grad_ref, y_ref, z_ref, stat_ref, out_weight_ref, gain_ref,
    dz_ref, dy_ref, scaled_ref, gain_grad_ref,
):
    @pl.when(pl.program_id(0) == 0)
    def _():
        gain_grad_ref[...] = jnp.zeros_like(gain_grad_ref)

    dscaled = dot(grad_ref[...], out_weight_ref[...])
    gate_z = z_ref[...]
    y = y_ref[...]
    gain = gain_ref[...]
    inv = stat_ref[:, 0:1]
    shift = stat_ref[:, 1:2] * inv * inv * inv * (1.0 / INNER)
    sig = jax.nn.sigmoid(gate_z)
    silu_z = gate_z * sig
    gated = y * silu_z
    normed = gated * inv
    scaled_ref[...] = (normed * gain).astype(LOW)
    gain_grad_ref[...] += jnp.sum(dscaled * normed, axis=0, keepdims=True)
    dgated = inv * gain * dscaled - gated * shift
    dz_ref[...] = (dgated * y * (sig + silu_z * (1.0 - sig))).astype(LOW)
    dy_ref[...] = dgated * silu_z


def scan_back_kernel(
    me_ref, dy_ref, y_ref, pre_ref, halo_ref, kept_ref, conv_ref, head_ref, skip_ref,
    spread_ref, gather_ref, dz_ref, z_weight_ref, weight_ref,
    grad_ref, dnormed_ref, conv_grad_ref, head_grad_ref, skip_grad_ref,
    dstate, ext, dext,
):
    size, width = dy_ref.shape
    conv_width = ext.shape[1]
    half = (conv_width - width) // 2
    step = pl.program_id(0)
    last_step = pl.num_programs(0) - 1

    @pl.when(step == 0)
    def _():
        dstate[...] = jnp.zeros_like(dstate)
        dext[size : size + 8, :] = jnp.zeros((8, conv_width), F32)
        conv_grad_ref[...] = jnp.zeros_like(conv_grad_ref)
        head_grad_ref[...] = jnp.zeros_like(head_grad_ref)
        skip_grad_ref[...] = jnp.zeros_like(skip_grad_ref)

    ext[0:8, :] = jnp.where(step == last_step, 0.0, halo_ref[:, :conv_width])
    ext[8 : 8 + size, :] = pre_ref[:, :conv_width]
    conv = conv_block(ext, conv_ref)
    sig = jax.nn.sigmoid(conv)
    act = conv * sig
    slope = sig + act * (1.0 - sig)
    inputs_x = act[:, :width]
    full_b = act[:, width : width + half]
    full_c = act[:, width + half :]
    low_b = full_b.astype(LOW)
    low_c = full_c.astype(LOW)
    left_b = left_parts(full_b, 1)
    pre_dt = pre_ref[:, conv_width:] + head_ref[0:1, :]
    step_dt = softplus(pre_dt)
    cum = decay_sums(step_dt, head_ref)
    cum_t = cum.T
    last = cum[size - 1 : size, :]
    spread = spread_ref[...]
    gather = gather_ref[...]
    dt_wide = dot(halves(step_dt), spread)
    cum_wide = dot(halves(jnp.exp2(cum)), spread)
    tail_wide = dot(halves(jnp.exp2(last - cum)), spread)
    scaled_x = inputs_x * dt_wide
    low_x = scaled_x.astype(LOW)
    tail_x = (scaled_x * tail_wide).astype(LOW)
    dy = dy_ref[...]
    high_dy, low_dy = split(dy)
    fade_dy = dy * cum_wide
    old_state = kept_ref[0]
    out_dstate = dstate[...]
    low_dstate = out_dstate.astype(LOW)
    tail_dx = tail_wide * dot(left_b, right_parts(out_dstate, 0))
    decay_all = cum_wide[size - 1 : size, :]
    state_sum = jnp.sum(old_state * out_dstate, axis=0, keepdims=True) * decay_all
    state_sum = state_sum + jnp.sum(scaled_x * tail_dx, axis=0, keepdims=True)
    state_dot = dot(halves(state_sum * jnp.ones((8, 1), F32)), gather)[0:1, :]
    dstate[...] = decay_all * out_dstate + dot(
        left_parts(full_c, 0), right_parts(fade_dy, 0), 0, 0
    )

    row = lax.broadcasted_iota(jnp.int32, (size, size), 0)
    col = lax.broadcasted_iota(jnp.int32, (size, size), 1)
    causal = col >= row
    affinity = jnp.where(causal, dot(left_b, right_parts(full_c, 1), 1, 1), 0.0)
    first_half = lax.broadcasted_iota(jnp.int32, (size, LANES), 1) < HEAD_WIDTH
    daffinity = jnp.zeros((size, size), F32)
    parts = []
    for pair in range(width // LANES):
        cols = slice(pair * LANES, (pair + 1) * LANES)
        pair_x = low_x[:, cols]
        pair_dy = high_dy[:, cols]
        both_dy = jnp.concatenate([pair_dy, low_dy[:, cols]], axis=1)
        zero = jnp.zeros_like(pair_x)
        here = []
        for which, head in enumerate((2 * pair, 2 * pair + 1)):
            gap = cum_t[head : head + 1, :] - cum[:, head : head + 1]
            fading = jnp.exp2(jnp.minimum(gap, 0.0))
            own_x = jnp.where(first_half, pair_x, zero) if which == 0 else jnp.where(first_half, zero, pair_x)
            daffinity = daffinity + fading * dot(own_x, pair_dy, 1, 1)
            here.append(mix_pair(affinity * fading, both_dy))
        parts.append(jnp.where(first_half, here[0], here[1]))
    low_daff = jnp.where(causal, daffinity, 0.0).astype(LOW)
    dx_wide = jnp.concatenate(parts, axis=1) + tail_dx
    d_b = dot(low_daff, low_c) + dot(tail_x, low_dstate, 1, 1)
    d_c = dot(low_daff, low_b, 0, 0) + dot(fade_dy.astype(LOW), old_state.astype(LOW), 1, 1)
    skip_x = skip_ref[0:1, :] * inputs_x
    from_y = dy * (y_ref[...] - skip_x) - scaled_x * dx_wide
    dcum = dot(halves(from_y), gather)
    from_dt = dot(halves(inputs_x * dx_wide), gather)
    upper = jnp.where(causal, 1.0, 0.0).astype(F32)
    da = dot(upper, dcum, precision=PRECISE) + state_dot
    ddt = from_dt + head_ref[2:3, :] * da
    dpre_dt = ddt * jax.nn.sigmoid(pre_dt)
    skip_grad_ref[0:1, :] += jnp.sum(dy * inputs_x, axis=0, keepdims=True)
    head_grad_ref[0:1, :] += jnp.sum(dpre_dt, axis=0, keepdims=True)
    head_grad_ref[1:2, :] += head_ref[2:3, :] * jnp.sum(step_dt * da, axis=0, keepdims=True)
    dinputs = dt_wide * dx_wide + skip_ref[0:1, :] * dy
    dconv = jnp.concatenate([dinputs, d_b, d_c], axis=1) * slope
    dext[0:size, :] = dconv
    inner = ext[8 : 8 + size, :]
    du = conv_ref[3:4, :] * dconv
    conv_grad_ref[4:5, :] += jnp.sum(dconv, axis=0, keepdims=True)
    conv_grad_ref[3:4, :] += jnp.sum(inner * dconv, axis=0, keepdims=True)
    for tap in range(3):
        moved = dext[3 - tap : 3 - tap + size, :]
        du = du + conv_ref[tap : tap + 1, :] * moved
        conv_grad_ref[tap : tap + 1, :] += jnp.sum(inner * moved, axis=0, keepdims=True)
    dext[size : size + 8, :] = dconv[0:8, :]
    low_grad = jnp.concatenate([du.astype(LOW), dpre_dt.astype(LOW)], axis=1)
    low_dz = dz_ref[...]
    grad_ref[:, :width] = low_dz
    grad_ref[:, width:] = low_grad
    dnormed = dot(low_dz, z_weight_ref[...], 1, 1) + dot(low_grad, weight_ref[...], 1, 1)
    dnormed_ref[...] = dnormed.astype(LOW)


def whole(shape):
    return pl.BlockSpec(shape, lambda *_: (0,) * len(shape))


def params():
    return pltpu.CompilerParams(
        vmem_limit_bytes=VMEM_BYTES, dimension_semantics=("arbitrary",)
    )


def spread_matrix(head_count, width):
    lanes = jnp.arange(LANES)[:, None]
    heads = (jnp.arange(width) // HEAD_WIDTH)[None, :]
    once = (lanes == heads).astype(LOW)
    return jnp.concatenate([once, once], axis=0)


def position(block, me, count, blocks_per_piece):
    slot = (block // blocks_per_piece) ^ me
    half = count // blocks_per_piece // 2
    return ((slot % 2) * half + slot // 2) * blocks_per_piece + block % blocks_per_piece


def scan_forward(me, rows, weight, conv_par, head_vals, skip, spread, blocks_per_piece, cover):
    total, depth = rows.shape
    width = skip.shape[1]
    conv_width = conv_par.shape[1]
    count = total // BLOCK
    pre_width = weight.shape[1]
    state_size = (conv_width - width) // 2

    def place(step, me_ref):
        return position(step, me_ref[0], count, blocks_per_piece)

    def at(step, me_ref):
        return (place(step, me_ref), 0)

    return pl.pallas_call(
        scan_kernel,
        out_shape=(
            jax.ShapeDtypeStruct((total, pre_width), F32),
            jax.ShapeDtypeStruct((total, width), F32),
            jax.ShapeDtypeStruct((count, state_size, width), F32),
        ),
        grid_spec=pltpu.PrefetchScalarGridSpec(
            num_scalar_prefetch=1,
            grid=(count,),
            in_specs=[
                pl.BlockSpec((BLOCK, depth), at),
                whole(weight.shape),
                whole(conv_par.shape),
                whole(head_vals.shape),
                whole(skip.shape),
                whole(spread.shape),
            ],
            out_specs=[
                pl.BlockSpec((BLOCK, pre_width), at),
                pl.BlockSpec((BLOCK, width), at),
                pl.BlockSpec((1, state_size, width), lambda step, me_ref: (step, 0, 0)),
            ],
            scratch_shapes=[
                pltpu.VMEM((state_size, width), F32),
                pltpu.VMEM((BLOCK + 8, conv_width), F32),
            ],
        ),
        compiler_params=params(),
        cost_estimate=pl.CostEstimate(
            flops=int(cover * total * depth * pre_width),
            bytes_accessed=total * width,
            transcendentals=0,
        ),
        name="scan_forward",
    )(me, rows, weight, conv_par, head_vals, skip, spread)


def gate_forward(rows, y, gate_weight, gain, z_all, part, blocks_per_piece):
    total, depth = rows.shape
    width = y.shape[1]
    count = total // BLOCK // blocks_per_piece
    middle = count // 2
    earlier = () if z_all is None else (z_all,)

    def spot(step):
        return (step + middle) % count

    def at(step):
        return (spot(step) * blocks_per_piece + part, 0)

    return pl.pallas_call(
        gate_kernel,
        out_shape=(
            jax.ShapeDtypeStruct((total, width), F32),
            jax.ShapeDtypeStruct((middle * BLOCK, depth), LOW),
            jax.ShapeDtypeStruct((middle * BLOCK, depth), LOW),
            jax.ShapeDtypeStruct((count * BLOCK, 1), F32),
        ),
        grid=(count,),
        in_specs=[
            pl.BlockSpec((BLOCK, depth), at),
            pl.BlockSpec((BLOCK, width), at),
            pl.BlockSpec((depth, width), lambda step: (0, 0)),
            pl.BlockSpec((depth, width), lambda step: (0, 1)),
            whole(gain.shape),
            *[pl.BlockSpec(memory_space=pl.ANY) for _ in earlier],
        ],
        out_specs=[
            pl.BlockSpec((BLOCK, width), at),
            pl.BlockSpec((BLOCK, depth), lambda step: (jnp.minimum(step, middle - 1), 0)),
            pl.BlockSpec((BLOCK, depth), lambda step: (jnp.maximum(step - middle, 0), 0)),
            pl.BlockSpec((BLOCK, 1), lambda step: (spot(step), 0)),
        ],
        input_output_aliases={5: 0} if earlier else {},
        compiler_params=params(),
        cost_estimate=pl.CostEstimate(
            flops=16 * count * BLOCK * depth * width,
            bytes_accessed=count * BLOCK * (4 * depth + 8 * width),
            transcendentals=count * BLOCK * width,
        ),
        name="gate_forward",
    )(rows, y, gate_weight, gate_weight, gain, *earlier)


def gate_backward(grad_rows, y, gate_z, stats, gate_weight, gain):
    total, depth = grad_rows.shape
    width = y.shape[1]

    def at(step):
        return (step, 0)

    return pl.pallas_call(
        gate_back_kernel,
        out_shape=(
            jax.ShapeDtypeStruct((total, width), LOW),
            jax.ShapeDtypeStruct((total, width), F32),
            jax.ShapeDtypeStruct((total, width), LOW),
            jax.ShapeDtypeStruct((1, width), F32),
        ),
        grid=(total // BLOCK,),
        in_specs=[
            pl.BlockSpec((BLOCK, depth), at),
            pl.BlockSpec((BLOCK, width), at),
            pl.BlockSpec((BLOCK, width), at),
            pl.BlockSpec((BLOCK, 2), at),
            pl.BlockSpec((depth, width), lambda step: (0, 1)),
            whole(gain.shape),
        ],
        out_specs=[
            pl.BlockSpec((BLOCK, width), at),
            pl.BlockSpec((BLOCK, width), at),
            pl.BlockSpec((BLOCK, width), at),
            whole(gain.shape),
        ],
        compiler_params=params(),
        cost_estimate=pl.CostEstimate(
            flops=total * width, bytes_accessed=total * width, transcendentals=0,
        ),
        name="gate_backward",
    )(grad_rows, y, gate_z, stats, gate_weight, gain)


def scan_backward(
    me, dy, y, pre, kept, conv_par, head_vals, skip, spread, dz, gate_weight, weight, blocks_per_piece
):
    total, width = dy.shape
    pre_width = pre.shape[1]
    conv_width = conv_par.shape[1]
    state_size = kept.shape[1]
    count = total // BLOCK
    halo_blocks = BLOCK // 8
    gather = spread.T
    gather = jnp.concatenate([gather[:, :LANES]] * 2, axis=0)

    def place(block, me_ref):
        return position(block, me_ref[0], count, blocks_per_piece)

    def at(step, me_ref):
        return (place(count - 1 - step, me_ref), 0)

    def parted(step, me_ref):
        spot = place(count - 1 - step, me_ref)
        return ((spot % blocks_per_piece) * (count // blocks_per_piece) + spot // blocks_per_piece, 0)

    def before(step, me_ref):
        return (place(jnp.maximum(count - 2 - step, 0), me_ref) * halo_blocks + halo_blocks - 1, 0)

    return pl.pallas_call(
        scan_back_kernel,
        out_shape=(
            jax.ShapeDtypeStruct((total, width + pre_width), LOW),
            jax.ShapeDtypeStruct((total, weight.shape[0]), LOW),
            jax.ShapeDtypeStruct((8, conv_width), F32),
            jax.ShapeDtypeStruct((8, LANES), F32),
            jax.ShapeDtypeStruct((8, width), F32),
        ),
        grid_spec=pltpu.PrefetchScalarGridSpec(
            num_scalar_prefetch=1,
            grid=(count,),
            in_specs=[
                pl.BlockSpec((BLOCK, width), at),
                pl.BlockSpec((BLOCK, width), at),
                pl.BlockSpec((BLOCK, pre_width), at),
                pl.BlockSpec((8, pre_width), before),
                pl.BlockSpec((1, state_size, width), lambda step, me_ref: (count - 1 - step, 0, 0)),
                whole(conv_par.shape),
                whole(head_vals.shape),
                whole(skip.shape),
                whole(spread.shape),
                whole(gather.shape),
                pl.BlockSpec((BLOCK, width), at),
                pl.BlockSpec((weight.shape[0], width), lambda step, me_ref: (0, 0)),
                whole(weight.shape),
            ],
            out_specs=[
                pl.BlockSpec((BLOCK, width + pre_width), at),
                pl.BlockSpec((BLOCK, weight.shape[0]), parted),
                whole((8, conv_width)),
                whole((8, LANES)),
                whole((8, width)),
            ],
            scratch_shapes=[
                pltpu.VMEM((state_size, width), F32),
                pltpu.VMEM((BLOCK + 8, conv_width), F32),
                pltpu.VMEM((BLOCK + 8, conv_width), F32),
            ],
        ),
        compiler_params=params(),
        cost_estimate=pl.CostEstimate(
            flops=total * width, bytes_accessed=total * width, transcendentals=0,
        ),
        name="scan_backward",
    )(me, dy, y, pre, pre, kept, conv_par, head_vals, skip, spread, gather, dz, gate_weight, weight)


def root_kernel(rows_ref, root_ref):
    vals = rows_ref[...]
    root_ref[...] = lax.rsqrt(jnp.mean(vals * vals, axis=1, keepdims=True) + NORM_EPS)


def first_root(rows):
    return pl.pallas_call(
        root_kernel,
        out_shape=jax.ShapeDtypeStruct((rows.shape[0], 1), F32),
        compiler_params=pltpu.CompilerParams(vmem_limit_bytes=VMEM_BYTES),
        cost_estimate=pl.CostEstimate(flops=10**11, bytes_accessed=rows.size * 4, transcendentals=0),
        name="first_root",
    )(rows)


def swap(vals, distance, count):
    return lax.ppermute(vals, "tensor", [(src, src ^ distance) for src in range(count)])


def gather_pieces(own, count):
    far = swap(own, 2, count)
    return [own, far, swap(own, 1, count), swap(far, 1, count)]


def gather_slots(own, count, beside=None):
    far = swap(own, 2, count)
    if beside is not None:
        far, beside = lax.optimization_barrier((far, beside))
    full = jnp.concatenate([own, far, swap(own, 1, count), swap(far, 1, count)], axis=0)
    return full if beside is None else (full, beside)


def gather_parts(parts, kept, count):
    parts = list(parts)
    gathered = []
    for spot, part in enumerate(parts):
        far = swap(part, 2, count)
        if spot + 1 < len(parts):
            far, parts[spot + 1] = lax.optimization_barrier((far, parts[spot + 1]))
        gathered.append([kept[spot], far, swap(part, 1, count), swap(far, 1, count)])
    return jnp.concatenate([part[spot] for spot in range(count) for part in gathered], axis=0)


def reduce_slots(sent, held, count, wire):
    return reduce_far(reduce_near(sent, held, count, wire), count, wire)


def reduce_near(sent, held, count, wire):
    return held.astype(F32) + swap(sent.astype(wire), 1, count).astype(F32)


def reduce_far(near, count, wire):
    return add_far(near, swap_far(near, count, wire))


def swap_far(near, count, wire):
    return swap(near[near.shape[0] // 2 :].astype(wire), 2, count)


def add_far(near, far):
    return near[: far.shape[0]] + far.astype(F32)


def ring_index(place, count):
    return jnp.where(place < count // 2, 2 * place, 2 * (count - place) - 1)


def ring_place(index, count):
    return jnp.where(index % 2 == 0, index // 2, count - (index + 1) // 2)


def ring_step(vals, way, count):
    order = list(range(0, count, 2)) + list(range(count - 1, 0, -2))
    pairs = [(order[spot], order[(spot + way) % count]) for spot in range(count)]
    return lax.ppermute(vals, "dp", pairs)


class RingReduce:
    def __init__(self, vals, count):
        self.vals, self.count = vals, count
        self.share = vals.shape[0] // count
        self.place = ring_place(lax.axis_index("dp"), count)
        self.total_hops = count // 2
        self.hops = {1: count // 2, -1: count - 1 - count // 2}
        self.moving = {way: self.chunk(way * hops).astype(LOW) for way, hops in self.hops.items()}
        self.done = 0

    def chunk(self, offset):
        index = ring_index((self.place + offset) % self.count, self.count)
        return lax.dynamic_slice_in_dim(self.vals, index * self.share, self.share, 0).astype(F32)

    def hop(self):
        self.done += 1
        for way, hops in self.hops.items():
            if self.done > hops:
                continue
            moved = ring_step(self.moving[way], way, self.count)
            if self.done < hops:
                moved = (moved.astype(F32) + self.chunk(way * (hops - self.done))).astype(LOW)
            self.moving[way] = moved

    def finish(self):
        while self.done < self.total_hops:
            self.hop()
        return self.chunk(0) + self.moving[1].astype(F32) + self.moving[-1].astype(F32)


def xor_step(vals, axis, distance, count):
    return lax.ppermute(vals, axis, [(src, src ^ distance) for src in range(count)])


def xor_sum(vals, axis, count):
    distance = 1
    while distance < count:
        vals = vals + xor_step(vals, axis, distance, count)
        distance *= 2
    return vals


def xor_gather(own, dp_count, tensor_count):
    stack = own
    for axis, count in (("dp", dp_count), ("tensor", tensor_count)):
        distance = 1
        while distance < count:
            stack = jnp.concatenate([stack, xor_step(stack, axis, distance, count)], axis=0)
            distance *= 2
    total = dp_count * tensor_count
    spots = jnp.arange(total)
    owner = (lax.axis_index("dp") ^ (spots % dp_count)) * tensor_count + (
        lax.axis_index("tensor") ^ (spots // dp_count)
    )
    chosen = owner[None, :] == spots[:, None]
    return jnp.sum(jnp.where(chosen[:, :, None], stack[None], 0.0), axis=1)


def adam_update(current, gradient, moment_old, square_old, step_rate, decay_coef):
    moment_new = BETA_ONE * moment_old + (1.0 - BETA_ONE) * gradient
    square_new = BETA_TWO * square_old + (1.0 - BETA_TWO) * gradient * gradient
    moment_hat = moment_new / (1.0 - BETA_ONE**STEP)
    square_hat = square_new / (1.0 - BETA_TWO**STEP)
    updated = current - step_rate * (
        moment_hat / (jnp.sqrt(square_hat) + ADAM_EPS) + decay_coef * current
    )
    return (updated, moment_new, square_new)


def inv_rms(vals):
    return lax.rsqrt(jnp.mean(vals * vals, axis=1, keepdims=True) + NORM_EPS)


def pad_rows(vals, rows):
    return jnp.pad(vals, ((0, rows - vals.shape[0]), (0, 0)))


def pad_lanes(vals, lanes):
    return jnp.pad(vals, ((0, 0), (0, lanes - vals.shape[1])))


def local(
    dp_count,
    tensor_count,
    resid_in,
    cotangent,
    w_zx,
    w_bc,
    w_dt,
    w_out,
    chan_par,
    head_par,
    bc_par,
    norm_gain,
    zx_first,
    zx_second,
    bc_first,
    bc_second,
    dt_first,
    dt_second,
    out_first,
    out_second,
    chan_first,
    chan_second,
    head_first,
    head_second,
    bcpar_first,
    bcpar_second,
    gain_first,
    gain_second,
):
    layer_total, depth_share, _, width = w_zx.shape
    rows_own, depth = resid_in.shape
    head_count = w_dt.shape[2]
    state_two = w_bc.shape[2]
    conv_width = width + state_two
    tap_total = bc_par.shape[1]
    pieces = rows_own // BLOCK
    me_dp = lax.axis_index("dp")
    me_tensor = lax.axis_index("tensor")
    me = me_tensor.astype(jnp.int32).reshape((1,))
    place = me_dp * tensor_count + me_tensor

    gain_share, bcpar_share = norm_gain.shape[1], bc_par.shape[2]
    flat = jnp.concatenate([norm_gain.reshape(-1), bc_par.reshape(-1)])[None, :]
    bc_weights = lax.all_gather(w_bc.astype(LOW), "tensor", axis=1, tiled=True)
    bc_weights, opening = lax.optimization_barrier((bc_weights, resid_in))
    flat, opening = lax.optimization_barrier((flat, first_root(opening)))
    weights = []
    for layer in range(layer_total):
        scan_share = jnp.concatenate(
            [
                w_zx[layer, :, 1, :].astype(LOW),
                bc_weights[layer],
                pad_lanes(w_dt[layer].astype(LOW), LANES),
            ],
            axis=1,
        )
        gate_share = jnp.concatenate(
            [w_zx[layer, :, 0, :].astype(LOW), w_out[layer].T.astype(LOW)], axis=1
        )
        if layer == 0:
            small = xor_gather(flat, dp_count, tensor_count)
        scan_weight = lax.all_gather(scan_share, "dp", axis=0, tiled=True)
        gate_weight = lax.all_gather(gate_share, "dp", axis=0, tiled=True)
        weights.append((scan_weight, gate_weight))
    gain_len = layer_total * gain_share
    gain_all = small[:, :gain_len].reshape(-1, layer_total, gain_share)
    gain_all = gain_all.transpose(1, 0, 2).reshape(layer_total, depth)
    bcpar_all = small[:, gain_len:].reshape(-1, layer_total, tap_total, bcpar_share)
    bcpar_all = bcpar_all.transpose(1, 2, 0, 3).reshape(layer_total, tap_total, state_two)

    spread = spread_matrix(head_count, width)
    def in_parts(vals):
        return [vals[part * BLOCK : (part + 1) * BLOCK] for part in range(pieces)]

    def in_turn(far_list, make):
        made, ready = [], []
        for spot, far in enumerate(far_list):
            if spot:
                far, held = lax.optimization_barrier((far, made[-1][0]))
                ready.append(held)
            made.append(make(spot, far))
        ready.append(made[-1][0])
        return made, ready

    hidden = in_parts(resid_in)
    roots = in_parts(opening)
    low_rows = ready_rows = None
    kept = []
    for layer in range(layer_total):
        scan_weight, gate_weight = weights[layer]
        conv_par = pad_rows(jnp.concatenate([chan_par[layer, :-1], bcpar_all[layer]], axis=1), 8)
        decay = -jnp.exp(head_par[layer, 1])
        head_vals = pad_rows(
            pad_lanes(jnp.stack([head_par[layer, 0], decay * LOG2E, decay], 0), LANES), 8
        )
        skip = pad_rows(jnp.repeat(head_par[layer, 2], HEAD_WIDTH)[None, :], 8)
        gain_q = chan_par[layer, -1:]
        if layer == 0:
            normed = (resid_in * opening * gain_all[layer][None, :]).astype(LOW)
            rows, scan_weight = gather_slots(normed, tensor_count, scan_weight)
            weights[0] = (scan_weight, gate_weight)
            rows, first_grad = lax.optimization_barrier((rows, cotangent.astype(LOW)))
            first_far = swap(first_grad, 2, tensor_count)
        else:
            rows = gather_parts(low_rows, ready_rows, tensor_count)
        pre, y, states = scan_forward(
            me, rows, scan_weight, conv_par, head_vals, skip, spread, pieces, 0.1 if layer else 8.0
        )
        if layer == 0:
            y, first_far = lax.optimization_barrier((y, first_far))
            first_full = jnp.concatenate(
                [first_grad, first_far, swap(first_grad, 1, tensor_count), swap(first_far, 1, tensor_count)], axis=0
            )
        gate_z = None
        far_list, near_list, inv_list = [], [], []
        for part in range(pieces):
            gate_z, sent, held, squares = gate_forward(rows, y, gate_weight, gain_q, gate_z, part, pieces)
            near = reduce_near(sent, held, tensor_count, LOW)
            near, squares = lax.optimization_barrier((near, squares))
            middle = squares.shape[0] // 2
            square_own = reduce_slots(squares[middle:], squares[:middle], tensor_count, F32)
            inv_list.append(lax.rsqrt(square_own / INNER + NORM_EPS))
            near_list.append(near)
            far_list.append(swap_far(near, tensor_count, LOW))
        next_gain = gain_all[min(layer + 1, layer_total - 1)][None, :]

        def next_rows(spot, far, near_list=near_list, inv_list=inv_list, hidden=hidden, next_gain=next_gain):
            branch = add_far(near_list[spot], far)
            out = hidden[spot] + inv_list[spot] * branch
            root = inv_rms(out)
            return (out * root * next_gain).astype(LOW), out, root, branch

        made, ready_rows = in_turn(far_list, next_rows)
        kept.append(
            (
                hidden, roots, rows, pre, y, states, gate_z, inv_list, [entry[3] for entry in made],
                conv_par, head_vals, skip, gain_q,
            )
        )
        low_rows = [entry[0] for entry in made]
        hidden = [entry[1] for entry in made]
        roots = [entry[2] for entry in made]

    grad_hidden = in_parts(cotangent)
    zx_list = [None] * layer_total
    dt_list = [None] * layer_total
    out_list = [None] * layer_total
    bc_list = [None] * layer_total
    small_list = [None] * layer_total
    shared_list = [None] * layer_total
    gain_list = [None] * layer_total
    def place_scan(layer, total):
        z_sum, scan_sum = total[:, :width], total[:, width:]
        zx_list[layer] = jnp.stack([z_sum, scan_sum[:, :width]], axis=1)
        share = depth_share // tensor_count
        parts = [
            lax.dynamic_slice_in_dim(scan_sum[:, width:conv_width], (me_tensor ^ slot) * share, share, 0)
            for slot in [*range(0, tensor_count, 2), *range(1, tensor_count, 2)]
        ]
        middle = tensor_count // 2
        bc_list[layer] = reduce_slots(
            jnp.concatenate(parts[middle:], axis=0), jnp.concatenate(parts[:middle], axis=0), tensor_count, F32
        )
        dt_list[layer] = scan_sum[:, conv_width : conv_width + head_count]

    late = ()

    def owned(grad):
        return lax.psum_scatter(grad, "dp", scatter_dimension=0, tiled=True)

    for layer in reversed(range(layer_total)):
        scan_weight, gate_weight = weights[layer]
        (
            entering, roots, rows, pre, y, states, gate_z, inv_list, projected, conv_par, head_vals, skip, gain_q,
        ) = kept[layer]
        if layer == layer_total - 1:
            branch_low = [part.astype(LOW) for part in grad_hidden]
        stats = [
            jnp.concatenate([inv, jnp.sum(low.astype(F32) * branch, axis=1, keepdims=True)], axis=1)
            for inv, low, branch in zip(inv_list, branch_low, projected)
        ]
        stats = gather_slots(jnp.concatenate(stats, axis=0), tensor_count)
        full_grad = first_full if layer == layer_total - 1 else gather_parts(branch_low, ready_low, tensor_count)
        dz, dy, scaled, gain_five = gate_backward(full_grad, y, gate_z, stats, gate_weight, gain_q)
        out_grad = dot(full_grad, scaled, 0, 0).astype(LOW)
        dy, out_grad = lax.optimization_barrier((dy, out_grad))
        if layer + 1 < layer_total:
            late, out_grad = lax.optimization_barrier((late, out_grad))
            place_scan(layer + 1, late.astype(F32))
        out_sum = owned(out_grad)
        dmerged, dnormed, conv_grad, head_grad, skip_grad = scan_backward(
            me, dy, y, pre, states, conv_par, head_vals, skip, spread, dz, gate_weight, scan_weight, pieces
        )
        out_sum, dnormed, dmerged = lax.optimization_barrier((out_sum, dnormed, dmerged))
        part_rows = dnormed.shape[0] // pieces
        near_list = []
        for part in range(pieces):
            vals = dnormed[part * part_rows : (part + 1) * part_rows]
            near_list.append(
                reduce_near(vals[part_rows // 2 :], vals[: part_rows // 2], tensor_count, LOW)
            )
        merged_grad = dot(rows, dmerged, 0, 0)
        if layer == 0:
            small_sums = (conv_grad, head_grad, skip_grad, gain_five)
            near_list, merged_grad, small_sums = lax.optimization_barrier((near_list, merged_grad, small_sums))
            conv_grad, head_grad, skip_grad, gain_five = small_sums
        far_list = [swap_far(near, tensor_count, LOW) for near in near_list]
        if layer == 0:
            place_scan(layer, RingReduce(merged_grad, dp_count).finish())
        else:
            far_list[-1], merged_grad = lax.optimization_barrier((far_list[-1], merged_grad.astype(LOW)))
            late = owned(merged_grad)
        out_list[layer] = out_sum.astype(F32).T
        gain = gain_all[layer][None, :]

        def next_grad(
            spot, far, near_list=near_list, entering=entering, roots=roots, grad_hidden=grad_hidden, gain=gain
        ):
            part_grad = add_far(near_list[spot], far)
            part_in, root = entering[spot], roots[spot]
            gained = part_grad * gain
            shift = jnp.mean(gained * part_in, axis=1, keepdims=True) * root * root * root
            out = grad_hidden[spot] + root * gained - part_in * shift
            return out.astype(LOW), out, jnp.sum(part_grad * part_in * root, axis=0)

        made, ready_low = in_turn(far_list, next_grad)
        branch_low = [entry[0] for entry in made]
        grad_hidden = [entry[1] for entry in made]
        gain_grad = sum(entry[2] for entry in made)

        chan_grad = jnp.concatenate([conv_grad[:5, :width], gain_five], axis=0)
        skip_sum = skip_grad[0].reshape(head_count, HEAD_WIDTH).sum(axis=1)
        head_all = jnp.concatenate(
            [head_grad[0, :head_count], head_grad[1, :head_count], skip_sum]
        )
        small_list[layer] = jnp.concatenate([chan_grad.reshape(-1), head_all])
        gain_list[layer] = gain_grad
        shared_list[layer] = conv_grad[:5, width:].reshape(-1)

    shared = xor_sum(jnp.stack(shared_list, 0), "tensor", tensor_count)
    both = xor_sum(jnp.concatenate([jnp.stack(small_list, 0), shared], axis=1), "dp", dp_count)
    chan_len = chan_par.shape[1] * width
    head_len = head_par.shape[1] * head_count
    chan_stack = both[:, :chan_len].reshape(chan_par.shape)
    head_stack = both[:, chan_len : chan_len + head_len].reshape(head_par.shape)
    shared = both[:, chan_len + head_len :]
    gains = xor_sum(xor_sum(jnp.stack(gain_list, 0), "tensor", tensor_count), "dp", dp_count)
    gain_stack = lax.dynamic_slice_in_dim(gains, place * gain_share, gain_share, axis=1)
    bcpar_stack = lax.dynamic_slice_in_dim(
        shared.reshape(layer_total, tap_total, state_two), place * bcpar_share, bcpar_share, axis=2
    )

    zx_stack = with_layout_constraint(jnp.stack(zx_list, 0), Layout((0, 1, 2, 3)))
    zx_new = adam_update(w_zx, zx_stack, zx_first, zx_second, MATRIX_RATE, MATRIX_DECAY)
    bc_new = adam_update(w_bc, jnp.stack(bc_list, 0), bc_first, bc_second, MATRIX_RATE, MATRIX_DECAY)
    dt_new = adam_update(w_dt, jnp.stack(dt_list, 0), dt_first, dt_second, MATRIX_RATE, MATRIX_DECAY)
    out_new = adam_update(w_out, jnp.stack(out_list, 0), out_first, out_second, MATRIX_RATE, MATRIX_DECAY)
    chan_new = adam_update(chan_par, chan_stack, chan_first, chan_second, SMALL_RATE, 0.0)
    head_new = adam_update(head_par, head_stack, head_first, head_second, HEAD_RATE, 0.0)
    bcpar_new = adam_update(bc_par, bcpar_stack, bcpar_first, bcpar_second, SMALL_RATE, 0.0)
    gain_new = adam_update(norm_gain, gain_stack, gain_first, gain_second, SMALL_RATE, 0.0)
    return (
        jnp.concatenate(hidden, axis=0), jnp.concatenate(grad_hidden, axis=0), *zx_new, *bc_new, *dt_new, *out_new, *chan_new, *head_new, *bcpar_new, *gain_new,
    )


def solution(mesh):
    in_specs = (
        P(("dp", "tensor"), None),
        P(("dp", "tensor"), None),
        P(None, "dp", None, "tensor"),
        P(None, ("dp", "tensor"), None),
        P(None, "dp", "tensor"),
        P(None, "tensor", "dp"),
        P(None, None, "tensor"),
        P(None, None, "tensor"),
        P(None, None, ("dp", "tensor")),
        P(None, ("dp", "tensor")),
        P(None, "dp", None, "tensor"),
        P(None, "dp", None, "tensor"),
        P(None, ("dp", "tensor"), None),
        P(None, ("dp", "tensor"), None),
        P(None, "dp", "tensor"),
        P(None, "dp", "tensor"),
        P(None, "tensor", "dp"),
        P(None, "tensor", "dp"),
        P(None, None, "tensor"),
        P(None, None, "tensor"),
        P(None, None, "tensor"),
        P(None, None, "tensor"),
        P(None, None, ("dp", "tensor")),
        P(None, None, ("dp", "tensor")),
        P(None, ("dp", "tensor")),
        P(None, ("dp", "tensor")),
    )
    out_specs = (
        P(("dp", "tensor"), None),
        P(("dp", "tensor"), None),
        P(None, "dp", None, "tensor"),
        P(None, "dp", None, "tensor"),
        P(None, "dp", None, "tensor"),
        P(None, ("dp", "tensor"), None),
        P(None, ("dp", "tensor"), None),
        P(None, ("dp", "tensor"), None),
        P(None, "dp", "tensor"),
        P(None, "dp", "tensor"),
        P(None, "dp", "tensor"),
        P(None, "tensor", "dp"),
        P(None, "tensor", "dp"),
        P(None, "tensor", "dp"),
        P(None, None, "tensor"),
        P(None, None, "tensor"),
        P(None, None, "tensor"),
        P(None, None, "tensor"),
        P(None, None, "tensor"),
        P(None, None, "tensor"),
        P(None, None, ("dp", "tensor")),
        P(None, None, ("dp", "tensor")),
        P(None, None, ("dp", "tensor")),
        P(None, ("dp", "tensor")),
        P(None, ("dp", "tensor")),
        P(None, ("dp", "tensor")),
    )
    return jax.shard_map(
        functools.partial(local, mesh.shape["dp"], mesh.shape["tensor"]), mesh=mesh, in_specs=in_specs, out_specs=out_specs, check_vma=False)
```

time: 3640 us -> 905 us (0.25)
  local copies, waits for them, and re-layouts: 1060 us -> 94.7 us
  waiting for transfers between devices: 1110 us -> 279 us
  matrix products: 685 us -> 54.2 us
  blocking collectives: 340 us -> 6.84 us
  Pallas kernels: 0 us -> 283 us
  other arithmetic: 386 us -> 104 us
  starting transfers between devices: 0.91 us -> 61.9 us
    reduce_scatter x12 -> x3, waiting for transfers between devices: 1030 us -> 17.9 us  [owned(): return lax.psum_scatter(grad, 'dp', scatter_dimension=0, tiled=True)]
    dynamic_update_slice x112 -> x0, local copies, waits for them, and re-layouts: 663 us -> none  [scan_blocks(): lax.scan(jax.checkpoint(block_step), (start_state, decay_rate), block_parts)]
    dot_general x246 -> x4, matrix products: 674 us -> 54.2 us  [dot(): lax.dot_general(left, right, (((left_dim,), (right_dim,)), ((), ())), pre...]
    pallas_call x0 -> x11, Pallas kernels: none -> 283 us  [the longest x2 128 us: scan_backward(): pl.pallas_call(scan_back_kernel, out_shape=(jax.ShapeDtypeStruct((total,...]
    ppermute x0 -> x74, waiting for transfers between devices: none -> 233 us  [the longest x52 199 us: swap(): lax.ppermute(vals, 'tensor', [(src, src ^ distance) for src in range(coun...]
    all_gather x6 -> x1, blocking collectives: 237 us -> 6.84 us  [local(): bc_weights = lax.all_gather(w_bc.astype(LOW), 'tensor', axis=1, tiled=True)]
    reduce_sum x46 -> x11, other arithmetic: 117 us -> 22 us  [the longest x3 12.8 us: local(): jnp.sum(low.astype(F32) * branch, axis=1, keepdims=True)]
    another operation x212 -> x9, other arithmetic: 98 us -> 3.53 us  [the longest x2 3.4 us: local(): jnp.stack(zx_list, 0)]
  transfers between devices with their start and end apart: 22 -> 81, of which waited for: 13 -> 35; matrix products, arithmetic and copies ran while one was open for 29% -> 22% of each run, Pallas kernels for 0% -> 30%
where the time goes in v1:
time: 905 us; the launch traced here: 899 us
  Pallas kernels  283 us (31%)
  waiting for transfers between devices  279 us (31%)
  other arithmetic  104 us (11%)
  local copies, waits for them, and re-layouts  94.7 us (10%)
  starting transfers between devices  61.9 us (7%)
  matrix products  54.2 us (6%)
  between operations  16.2 us (2%)
    ppermute x52, waiting for transfers between devices, swap(): lax.ppermute(vals, 'tensor', [(src, src ^ distance) for src in range(coun...  199 us
    pallas_call x2, Pallas kernels, scan_backward(): pl.pallas_call(scan_back_kernel, out_shape=(jax.ShapeDtypeStruct((total,...  128 us
    pallas_call x2, Pallas kernels, scan_forward(): pl.pallas_call(scan_kernel, out_shape=(jax.ShapeDtypeStruct((total, pre_w...  70.1 us
    dot_general x4, matrix products, dot(): lax.dot_general(left, right, (((left_dim,), (right_dim,)), ((), ())), pre...  54.2 us
    pallas_call x4, Pallas kernels, gate_forward(): pl.pallas_call(gate_kernel, out_shape=(jax.ShapeDtypeStruct((total, width...  47.4 us
    unnamed x250, local copies, waits for them, and re-layouts  40.4 us
    pallas_call x2, Pallas kernels, gate_backward(): pl.pallas_call(gate_back_kernel, out_shape=(jax.ShapeDtypeStruct((total,...  35 us
    ppermute x52, starting transfers between devices, swap(): lax.ppermute(vals, 'tensor', [(src, src ^ distance) for src in range(coun...  34.8 us
  transfers between devices with their start and end apart: 81, of which 35 were waited for; matrix products, arithmetic and copies ran while one was open for 22% of the time, Pallas kernels for 30%

profile of v1, /device:TPU:0, one launch (start us, length us, event | category | flops | bytes accessed | tf_op | source)
XLA Modules:
  0.0 899.5 jit_solution(7814052577905834532)
XLA Ops:
  9.0 6.8 all_gather.15
  21.8 3.0 first_root.1
  32.3 2.9 collective-permute-start.2
  50.0 32.7 %collective-permute-done.5 = bf16[512,1536]{1,0:T(8,128)(2,1)} collective-permute-done((bf16[512,1536]{1,0:T(8,128)(2,1)}, bf16[512,1536]{1,0:T(8,128)(2,1)}, u32[]{:S(2)}, u32[]{:S(2)}) %collective-permute-start.5) | collective-permute-done | bytes 1572896 | tf_op jit(solution)/shard_map/ppermute | solution.py:553
  82.7 2.9 all-gather.5.cloned.1.call-done.weight_ref
  90.5 3.3 convert_element_type.235
  96.7 6.6 pad_maximum_fusion.rows_ref
  104.9 34.9 %scan_forward.2 = (f32[2048,1152]{1,0:T(8,128)}, f32[2048,768]{1,0:T(8,128)}, f32[8,128,768]{2,1,0:T(8,128)}) custom-call(s32[1]{0:T(128)} %bitcast.5.me_ref, bf16[2048,1536]{1,0:T(8,128)(2,1)} %pad_maximum_fusion.rows_ref, bf16[1536,1152]{1,0:T(8,128)(2,1)} %all-gather.5.cloned.1.call-done.weight_ref, f32[8,1024]{1,0:T(8,128)} %select_maximum_fusion.1.conv_ref, ...), custom_call_target="tpu_custom_call" | custom-call | flops 28991029248 | bytes 1572864 | tf_op jit(solution)/shard_map/scan_forward/pallas_call | solution.py:341
  141.4 25.3 %all-gather.7.cloned.1.call-done.z_weight_ref.out_weight_ref = bf16[1536,1536]{1,0:T(8,128)(2,1)} async-done(((bf16[192,1536]{1,0:T(8,128)(2,1)}), bf16[1536,1536]{1,0:T(8,128)(2,1)}) %all-gather.7.cloned.1.call-update) | async-done | bytes 4718608 | tf_op jit(solution)/shard_map/all_gather | solution.py:758
  166.7 11.8 %gate_forward.4 = (f32[2048,768]{1,0:T(8,128)}, bf16[512,1536]{1,0:T(8,128)(2,1)}, bf16[512,1536]{1,0:T(8,128)(2,1)}, f32[1024,1]{1,0:T(8,128)}) custom-call(bf16[2048,1536]{1,0:T(8,128)(2,1)} %pad_maximum_fusion.rows_ref, f32[2048,768]{1,0:T(8,128)} %get-tuple-element.122.y_ref, bf16[1536,1536]{1,0:T(8,128)(2,1)} %all-gather.7.cloned.1.call-done.z_weight_ref.out_weight_ref, ...), custom_call_target="tpu_custom_call" | custom-call | flops 19327352832 | bytes 12582912 | tf_op jit(solution)/shard_map/gate_forward/pallas_call | solution.py:392
  178.6 11.9 %gate_forward.5 = (f32[2048,768]{1,0:T(8,128)}, bf16[512,1536]{1,0:T(8,128)(2,1)}, bf16[512,1536]{1,0:T(8,128)(2,1)}, f32[1024,1]{1,0:T(8,128)}) custom-call(bf16[2048,1536]{1,0:T(8,128)(2,1)} %pad_maximum_fusion.rows_ref, f32[2048,768]{1,0:T(8,128)} %get-tuple-element.122.y_ref, ...), custom_call_target="tpu_custom_call", output_to_operand_aliasing={{0}: (5, {})} | custom-call | flops 19327352832 | bytes 12582912 | tf_op jit(solution)/shard_map/gate_forward/pallas_call | solution.py:392
  202.0 31.8 %collective-permute-done.11 = f32[256,1]{1,0:T(8,128)S(1)} collective-permute-done((f32[256,1]{1,0:T(8,128)S(1)}, f32[256,1]{1,0:T(8,128)S(1)}, u32[]{:S(2)}, u32[]{:S(2)}) %collective-permute-start.11) | collective-permute-done | bytes 1056 | tf_op jit(solution)/shard_map/ppermute | solution.py:553
  245.6 12.8 %collective-permute-done.17 = bf16[256,1536]{1,0:T(8,128)(2,1)S(1)} collective-permute-done((bf16[256,1536]{1,0:T(8,128)(2,1)}, bf16[256,1536]{1,0:T(8,128)(2,1)S(1)}, u32[]{:S(2)}, u32[]{:S(2)}) %collective-permute-start.17) | collective-permute-done | bytes 786464 | tf_op jit(solution)/shard_map/ppermute | solution.py:553
  266.2 11.7 %collective-permute-done.18 = bf16[256,1536]{1,0:T(8,128)(2,1)} collective-permute-done((bf16[256,1536]{1,0:T(8,128)(2,1)}, bf16[256,1536]{1,0:T(8,128)(2,1)}, u32[]{:S(2)}, u32[]{:S(2)}) %collective-permute-start.18) | collective-permute-done | bytes 786464 | tf_op jit(solution)/shard_map/ppermute | solution.py:553
  285.5 35.1 %scan_forward.3 = (f32[2048,1152]{1,0:T(8,128)}, f32[2048,768]{1,0:T(8,128)}, f32[8,128,768]{2,1,0:T(8,128)}) custom-call(s32[1]{0:T(128)} %bitcast.5.me_ref, bf16[2048,1536]{1,0:T(8,128)(2,1)} %constant_dynamic-update-slice_fusion.rows_ref, bf16[1536,1152]{1,0:T(8,128)(2,1)} %all-gather.9.cloned.1.call-done.weight_ref, ...), custom_call_target="tpu_custom_call" | custom-call | flops 362387872 | bytes 1572864 | tf_op jit(solution)/shard_map/scan_forward/pallas_call | solution.py:341
  320.6 11.8 %gate_forward.6 = (f32[2048,768]{1,0:T(8,128)}, bf16[512,1536]{1,0:T(8,128)(2,1)}, bf16[512,1536]{1,0:T(8,128)(2,1)}, f32[1024,1]{1,0:T(8,128)}) custom-call(bf16[2048,1536]{1,0:T(8,128)(2,1)} %constant_dynamic-update-slice_fusion.rows_ref, f32[2048,768]{1,0:T(8,128)} %get-tuple-element.138.y_ref, ...), custom_call_target="tpu_custom_call" | custom-call | flops 19327352832 | bytes 12582912 | tf_op jit(solution)/shard_map/gate_forward/pallas_call | solution.py:392
  332.5 11.9 %gate_forward.7 = (f32[2048,768]{1,0:T(8,128)}, bf16[512,1536]{1,0:T(8,128)(2,1)}, bf16[512,1536]{1,0:T(8,128)(2,1)}, f32[1024,1]{1,0:T(8,128)}) custom-call(bf16[2048,1536]{1,0:T(8,128)(2,1)} %constant_dynamic-update-slice_fusion.rows_ref, f32[2048,768]{1,0:T(8,128)} %get-tuple-element.138.y_ref, ...), custom_call_target="tpu_custom_call", output_to_operand_aliasing={{0}: (5, {})} | custom-call | flops 19327352832 | bytes 12582912 | tf_op jit(solution)/shard_map/gate_forward/pallas_call | solution.py:392
  350.2 2.8 constant_dynamic-update-slice_fusion.8.grad_ref
  362.7 32.6 %collective-permute-done.25 = f32[256,1]{1,0:T(8,128)S(1)} collective-permute-done((f32[256,1]{1,0:T(8,128)S(1)}, f32[256,1]{1,0:T(8,128)S(1)}, u32[]{:S(2)}, u32[]{:S(2)}) %collective-permute-start.25) | collective-permute-done | bytes 1056 | tf_op jit(solution)/shard_map/ppermute | solution.py:553
  399.5 5.4 multiply_reduce_fusion.10
  411.2 17.3 %gate_backward.2 = (bf16[2048,768]{1,0:T(8,128)(2,1)}, f32[2048,768]{1,0:T(8,128)}, bf16[2048,768]{1,0:T(8,128)(2,1)}, f32[1,768]{1,0:T(1,128)}) custom-call(bf16[2048,1536]{1,0:T(8,128)(2,1)} %constant_dynamic-update-slice_fusion.8.grad_ref, f32[2048,768]{1,0:T(8,128)} %get-tuple-element.138.y_ref, f32[2048,768]{1,0:T(8,128)} %get-tuple-element.151.z_ref, ...), custom_call_target="tpu_custom_call" | custom-call | flops 1572864 | bytes 1572864 | tf_op jit(solution)/shard_map/gate_backward/pallas_call | solution.py:433
  428.5 9.6 %convolution_convert_fusion.2 = bf16[1536,768]{1,0:T(8,128)(2,1)} fusion(bf16[2048,1536]{1,0:T(8,128)(2,1)} %constant_dynamic-update-slice_fusion.8.grad_ref, bf16[2048,768]{1,0:T(8,128)(2,1)} %get-tuple-element.153), kind=kOutput, calls=%fused_computation.4 | convolution fusion | flops 4833017856 | bytes 11796480 | tf_op jit(solution)/shard_map/dot_general | solution.py:34
  439.9 63.7 %scan_backward.2 = (bf16[2048,1920]{1,0:T(8,128)(2,1)}, bf16[2048,1536]{1,0:T(8,128)(2,1)}, f32[8,1024]{1,0:T(8,128)}, f32[8,128]{1,0:T(8,128)}, f32[8,768]{1,0:T(8,128)}) custom-call(s32[1]{0:T(128)} %bitcast.5.me_ref, f32[2048,768]{1,0:T(8,128)} %get-tuple-element.155.dy_ref, f32[2048,768]{1,0:T(8,128)} %get-tuple-element.138.y_ref, ...), custom_call_target="tpu_custom_call" | custom-call | flops 1572864 | bytes 1572864 | tf_op jit(solution)/shard_map/scan_backward/pallas_call | solution.py:489
  508.2 2.9 collective-permute-done.36
  520.0 15.6 %convolution_convert_fusion = bf16[1536,1920]{1,0:T(8,128)(2,1)} fusion(bf16[2048,1536]{1,0:T(8,128)(2,1)S(1)} %bitcast.121, bf16[2048,1920]{1,0:T(8,128)(2,1)S(1)} %copy-done.104), kind=kOutput, calls=%fused_computation | convolution fusion | flops 12082544640 | bytes 20054016 | tf_op jit(solution)/shard_map/dot_general | solution.py:34
  535.5 2.9 collective-permute-done.39
  542.5 17.4 %collective-permute-done.37 = bf16[256,1536]{1,0:T(8,128)(2,1)} collective-permute-done((bf16[256,1536]{1,0:T(8,128)(2,1)}, bf16[256,1536]{1,0:T(8,128)(2,1)}, u32[]{:S(2)}, u32[]{:S(2)}) %collective-permute-start.37) | collective-permute-done | bytes 786464 | tf_op jit(solution)/shard_map/ppermute | solution.py:553
  562.2 4.4 multiply_reduce_fusion.7
  569.9 3.0 multiply_reduce_fusion.6
  577.3 7.5 collective-permute-done.40
  590.0 11.8 %collective-permute-done.41 = bf16[256,1536]{1,0:T(8,128)(2,1)S(1)} collective-permute-done((bf16[256,1536]{1,0:T(8,128)(2,1)S(1)}, bf16[256,1536]{1,0:T(8,128)(2,1)S(1)}, u32[]{:S(2)}, u32[]{:S(2)}) %collective-permute-start.41) | collective-permute-done | bytes 786464 | tf_op jit(solution)/shard_map/ppermute | solution.py:553
  607.7 17.7 %gate_backward.3 = (bf16[2048,768]{1,0:T(8,128)(2,1)}, f32[2048,768]{1,0:T(8,128)}, bf16[2048,768]{1,0:T(8,128)(2,1)}, f32[1,768]{1,0:T(1,128)}) custom-call(bf16[2048,1536]{1,0:T(8,128)(2,1)} %constant_dynamic-update-slice_fusion.17.grad_ref, f32[2048,768]{1,0:T(8,128)} %get-tuple-element.122.y_ref, f32[2048,768]{1,0:T(8,128)} %get-tuple-element.169.z_ref, ...), custom_call_target="tpu_custom_call" | custom-call | flops 1572864 | bytes 1572864 | tf_op jit(solution)/shard_map/gate_backward/pallas_call | solution.py:433
  625.3 9.3 %convolution_convert_fusion.1 = bf16[1536,768]{1,0:T(8,128)(2,1)} fusion(bf16[2048,1536]{1,0:T(8,128)(2,1)} %constant_dynamic-update-slice_fusion.17.grad_ref, bf16[2048,768]{1,0:T(8,128)(2,1)} %get-tuple-element.171), kind=kOutput, calls=%fused_computation.3 | convolution fusion | flops 4833017856 | bytes 11796480 | tf_op jit(solution)/shard_map/dot_general | solution.py:34
  634.7 14.8 %reduce-scatter.6.cloned.1.call-done = bf16[192,1920]{1,0:T(8,128)(2,1)} async-done(((bf16[1536,1920]{1,0:T(8,128)(2,1)}), bf16[192,1920]{1,0:T(8,128)(2,1)}) %reduce-scatter.6.cloned.1.call-update) | async-done | bytes 737296 | tf_op jit(solution)/shard_map/reduce_scatter | solution.py:864
  654.2 64.0 %scan_backward.3 = (bf16[2048,1920]{1,0:T(8,128)(2,1)}, bf16[2048,1536]{1,0:T(8,128)(2,1)}, f32[8,1024]{1,0:T(8,128)}, f32[8,128]{1,0:T(8,128)}, f32[8,768]{1,0:T(8,128)}) custom-call(s32[1]{0:T(128)} %bitcast.5.me_ref, f32[2048,768]{1,0:T(8,128)} %get-tuple-element.174.dy_ref, f32[2048,768]{1,0:T(8,128)} %get-tuple-element.122.y_ref, ...), custom_call_target="tpu_custom_call" | custom-call | flops 1572864 | bytes 1572864 | tf_op jit(solution)/shard_map/scan_backward/pallas_call | solution.py:489
  725.2 19.6 %fusion.67 = f32[1536,1920]{1,0:T(8,128)} fusion(bf16[2048,1536]{1,0:T(8,128)(2,1)} %pad_maximum_fusion.rows_ref, bf16[2048,1920]{1,0:T(8,128)(2,1)} %get-tuple-element.181), kind=kOutput, calls=%fused_computation.287 | convolution fusion | flops 12079595520 | bytes 25952256 | tf_op jit(solution)/shard_map/dot_general | solution.py:34
  759.4 3.3 maximum_bitcast_fusion.1
  767.6 3.1 dynamic-slice_convert_fusion.1
  773.5 3.7 multiply_subtract_fusion.5
  783.2 4.6 collective-permute-done.68
  794.5 6.9 collective-permute-done.52
  801.4 14.6 %collective-permute-done.51 = bf16[256,1536]{1,0:T(8,128)(2,1)} collective-permute-done((bf16[256,1536]{1,0:T(8,128)(2,1)}, bf16[256,1536]{1,0:T(8,128)(2,1)}, u32[]{:S(2)}, u32[]{:S(2)}) %collective-permute-start.51) | collective-permute-done | bytes 786464 | tf_op jit(solution)/shard_map/ppermute | solution.py:553
  816.0 3.3 multiply_reduce_fusion.3
  822.5 3.4 add_convert_fusion.3
  833.3 11.6 %collective-permute-done.71 = f32[2,1536]{1,0:T(2,128)S(1)} collective-permute-done((f32[2,1536]{1,0:T(2,128)S(1)}, f32[2,1536]{1,0:T(2,128)S(1)}, u32[]{:S(2)}, u32[]{:S(2)}) %collective-permute-start.71) | collective-permute-done | bytes 12320 | tf_op jit(solution)/shard_map/ppermute | solution.py:645
  849.8 3.1 multiply_subtract_fusion.2
  857.5 10.4 %collective-permute-done.73 = f32[2,1536]{1,0:T(2,128)S(1)} collective-permute-done((f32[2,1536]{1,0:T(2,128)S(1)}, f32[2,1536]{1,0:T(2,128)S(1)}, u32[]{:S(2)}, u32[]{:S(2)}) %collective-permute-start.73) | collective-permute-done | bytes 12320 | tf_op jit(solution)/shard_map/ppermute | solution.py:645
  875.9 9.2 %multiply_subtract_fusion = (f32[2,192,2,768]{3,2,1,0:T(2,128)}, f32[2,192,2,768]{3,2,1,0:T(2,128)}, f32[2,192,2,768]{3,2,1,0:T(2,128)}) fusion(f32[2,192,2,768]{3,2,1,0:T(2,128)S(1)} %copy-done.17, f32[1,192,2,768]{3,2,1,0:T(2,128)S(1)} %copy-done.23, f32[1,192,2,768]{3,2,1,0:T(2,128)S(1)} %copy.241, f32[2,192,2,768]{3,2,1,0:T(2,128)S(1)} %copy-done.32, ...), kind=kLoop, calls=%fused_computation.19 | loop fusion | flops 9437184 | bytes 16515072 | tf_op jit(solution)/shard_map/sub | solution.py:677
  (595 shorter events, 226.6 us)
Async XLA Ops:
  7.2 78.3 %all-gather.5.cloned.1.call-start = ((), (), s32[]{:S(2)}) async-start(), calls=%async_computation.3 | async-start | bytes 3981312 | tf_op jit(solution)/shard_map/all_gather | solution.py:757
  18.6 148.1 %all-gather.7.cloned.1.call-start = ((), (), s32[]{:S(2)}) async-start(), calls=%async_computation.4 | async-start | bytes 5308416 | tf_op jit(solution)/shard_map/all_gather | solution.py:758
  20.8 264.7 %all-gather.9.cloned.1.call-start = ((), (), s32[]{:S(2)}) async-start(), calls=%async_computation.5 | async-start | bytes 3981312 | tf_op jit(solution)/shard_map/all_gather | solution.py:757
  21.7 298.9 %all-gather.11.cloned.1.call-start = ((), (), s32[]{:S(2)}) async-start(), calls=%async_computation.6 | async-start | bytes 5308416 | tf_op jit(solution)/shard_map/all_gather | solution.py:758
  46.4 36.3 %collective-permute-start.5 = (bf16[512,1536]{1,0:T(8,128)(2,1)}, bf16[512,1536]{1,0:T(8,128)(2,1)}, u32[]{:S(2)}, u32[]{:S(2)}) collective-permute-start(bf16[512,1536]{1,0:T(8,128)(2,1)} %multiply_convert_fusion), channel_id=1, source_target_pairs={{0,2},{1,3},{2,0},{3,1},{4,6},{5,7},{6,4},{7,5},{8,10},{9,11},{10,... | collective-permute-start | bytes 4718600 | tf_op jit(solution)/shard_map/ppermute | solution.py:553
  49.2 456.1 %reduce-scatter.4.cloned.1.call-start = ((), (), s32[]{:S(2)}) async-start(), calls=%async_computation.7 | async-start | bytes 2654208 | tf_op jit(solution)/shard_map/reduce_scatter | solution.py:864
  50.0 46.8 %collective-permute-start.6 = (bf16[512,1536]{1,0:T(8,128)(2,1)}, bf16[512,1536]{1,0:T(8,128)(2,1)}, u32[]{:S(2)}, u32[]{:S(2)}) collective-permute-start(bf16[512,1536]{1,0:T(8,128)(2,1)} %multiply_convert_fusion), channel_id=1, source_target_pairs={{0,1},{1,0},{2,3},{3,2},{4,5},{5,4},{6,7},{7,6},{8,9},{9,8},{10,11... | collective-permute-start | bytes 4718600 | tf_op jit(solution)/shard_map/ppermute | solution.py:553
  103.4 36.8 %collective-permute-start.8 = (bf16[512,1536]{1,0:T(8,128)(2,1)S(1)}, bf16[512,1536]{1,0:T(8,128)(2,1)S(1)}, u32[]{:S(2)}, u32[]{:S(2)}) collective-permute-start(bf16[512,1536]{1,0:T(8,128)(2,1)S(1)} %copy-done.19), channel_id=1, source_target_pairs={{0,2},{1,3},{2,0},{3,1},{4,6},{5,7},{6,4},{7,5},{8,10},{9,11},{10,... | collective-permute-start | bytes 4718600 | tf_op jit(solution)/shard_map/ppermute | solution.py:553
  193.7 43.1 %collective-permute-start.12 = (bf16[256,1536]{1,0:T(8,128)(2,1)S(1)}, bf16[256,1536]{1,0:T(8,128)(2,1)S(1)}, u32[]{:S(2)}, u32[]{:S(2)}) collective-permute-start(bf16[256,1536]{1,0:T(8,128)(2,1)S(1)} %slice.650), channel_id=1, source_target_pairs={{0,2},{1,3},{2,0},{3,1},{4,6},{5,7},{6,4},{7,5},{8,10},{9,11},{10,... | collective-permute-start | bytes 2359304 | tf_op jit(solution)/shard_map/ppermute | solution.py:553
  198.2 42.3 %collective-permute-start.14 = (bf16[256,1536]{1,0:T(8,128)(2,1)S(1)}, bf16[256,1536]{1,0:T(8,128)(2,1)S(1)}, u32[]{:S(2)}, u32[]{:S(2)}) collective-permute-start(bf16[256,1536]{1,0:T(8,128)(2,1)S(1)} %slice.649), channel_id=1, source_target_pairs={{0,2},{1,3},{2,0},{3,1},{4,6},{5,7},{6,4},{7,5},{8,10},{9,11},{10,... | collective-permute-start | bytes 2359304 | tf_op jit(solution)/shard_map/ppermute | solution.py:553
  199.8 34.0 %collective-permute-start.11 = (f32[256,1]{1,0:T(8,128)S(1)}, f32[256,1]{1,0:T(8,128)S(1)}, u32[]{:S(2)}, u32[]{:S(2)}) collective-permute-start(f32[256,1]{1,0:T(8,128)S(1)} %slice.451), channel_id=1, source_target_pairs={{0,2},{1,3},{2,0},{3,1},{4,6},{5,7},{6,4},{7,5},{8,10},{9,11},{10,... | collective-permute-start | bytes 3080 | tf_op jit(solution)/shard_map/ppermute | solution.py:553
  200.5 35.7 %collective-permute-start.16 = (f32[256,1]{1,0:T(8,128)S(1)}, f32[256,1]{1,0:T(8,128)S(1)}, u32[]{:S(2)}, u32[]{:S(2)}) collective-permute-start(f32[256,1]{1,0:T(8,128)S(1)} %slice.456), channel_id=1, source_target_pairs={{0,2},{1,3},{2,0},{3,1},{4,6},{5,7},{6,4},{7,5},{8,10},{9,11},{10,... | collective-permute-start | bytes 3080 | tf_op jit(solution)/shard_map/ppermute | solution.py:553
  239.0 19.4 %collective-permute-start.17 = (bf16[256,1536]{1,0:T(8,128)(2,1)}, bf16[256,1536]{1,0:T(8,128)(2,1)S(1)}, u32[]{:S(2)}, u32[]{:S(2)}) collective-permute-start(bf16[256,1536]{1,0:T(8,128)(2,1)} %multiply_convert_fusion.2), channel_id=1, source_target_pairs={{0,2},{1,3},{2,0},{3,1},{4,6},{5,7},{6,4},{7,5},{8,10},{9,11},{10,... | collective-permute-start | bytes 2359304 | tf_op jit(solution)/shard_map/ppermute | solution.py:553
  259.3 18.7 %collective-permute-start.18 = (bf16[256,1536]{1,0:T(8,128)(2,1)}, bf16[256,1536]{1,0:T(8,128)(2,1)}, u32[]{:S(2)}, u32[]{:S(2)}) collective-permute-start(bf16[256,1536]{1,0:T(8,128)(2,1)} %get-tuple-element.137), channel_id=1, source_target_pairs={{0,2},{1,3},{2,0},{3,1},{4,6},{5,7},{6,4},{7,5},{8,10},{9,11},{10,... | collective-permute-start | bytes 2359304 | tf_op jit(solution)/shard_map/ppermute | solution.py:553
  260.7 19.3 %collective-permute-start.19 = (bf16[256,1536]{1,0:T(8,128)(2,1)}, bf16[256,1536]{1,0:T(8,128)(2,1)}, u32[]{:S(2)}, u32[]{:S(2)}) collective-permute-start(bf16[256,1536]{1,0:T(8,128)(2,1)} %multiply_convert_fusion.2), channel_id=1, source_target_pairs={{0,1},{1,0},{2,3},{3,2},{4,5},{5,4},{6,7},{7,6},{8,9},{9,8},{10,11... | collective-permute-start | bytes 2359304 | tf_op jit(solution)/shard_map/ppermute | solution.py:553
  262.3 20.3 %collective-permute-start.20 = (bf16[256,1536]{1,0:T(8,128)(2,1)}, bf16[256,1536]{1,0:T(8,128)(2,1)S(1)}, u32[]{:S(2)}, u32[]{:S(2)}) collective-permute-start(bf16[256,1536]{1,0:T(8,128)(2,1)} %get-tuple-element.137), channel_id=1, source_target_pairs={{0,1},{1,0},{2,3},{3,2},{4,5},{5,4},{6,7},{7,6},{8,9},{9,8},{10,11... | collective-permute-start | bytes 2359304 | tf_op jit(solution)/shard_map/ppermute | solution.py:553
  263.5 83.9 %collective-permute-start.31 = (bf16[512,1536]{1,0:T(8,128)(2,1)S(1)}, bf16[512,1536]{1,0:T(8,128)(2,1)}, u32[]{:S(2)}, u32[]{:S(2)}) collective-permute-start(bf16[512,1536]{1,0:T(8,128)(2,1)S(1)} %copy-done.20), channel_id=1, source_target_pairs={{0,1},{1,0},{2,3},{3,2},{4,5},{5,4},{6,7},{7,6},{8,9},{9,8},{10,11... | collective-permute-start | bytes 4718600 | tf_op jit(solution)/shard_map/ppermute | solution.py:553
  263.5 20.0 %collective-permute-start.21 = (bf16[256,1536]{1,0:T(8,128)(2,1)}, bf16[256,1536]{1,0:T(8,128)(2,1)S(1)}, u32[]{:S(2)}, u32[]{:S(2)}) collective-permute-start(bf16[256,1536]{1,0:T(8,128)(2,1)} %copy-done.42), channel_id=1, source_target_pairs={{0,1},{1,0},{2,3},{3,2},{4,5},{5,4},{6,7},{7,6},{8,9},{9,8},{10,11... | collective-permute-start | bytes 2359304 | tf_op jit(solution)/shard_map/ppermute | solution.py:553
  280.0 70.1 %collective-permute-start.32 = (bf16[512,1536]{1,0:T(8,128)(2,1)S(1)}, bf16[512,1536]{1,0:T(8,128)(2,1)}, u32[]{:S(2)}, u32[]{:S(2)}) collective-permute-start(bf16[512,1536]{1,0:T(8,128)(2,1)S(1)} %copy-done.35), channel_id=1, source_target_pairs={{0,1},{1,0},{2,3},{3,2},{4,5},{5,4},{6,7},{7,6},{8,9},{9,8},{10,11... | collective-permute-start | bytes 4718600 | tf_op jit(solution)/shard_map/ppermute | solution.py:553
  332.5 20.5 %collective-permute-start.23 = (bf16[512,1536]{1,0:T(8,128)(2,1)}, bf16[512,1536]{1,0:T(8,128)(2,1)S(1)}, u32[]{:S(2)}, u32[]{:S(2)}) collective-permute-start(bf16[512,1536]{1,0:T(8,128)(2,1)} %get-tuple-element.140), channel_id=1, source_target_pairs={{0,1},{1,0},{2,3},{3,2},{4,5},{5,4},{6,7},{7,6},{8,9},{9,8},{10,11... | collective-permute-start | bytes 4718600 | tf_op jit(solution)/shard_map/ppermute | solution.py:553
  355.1 44.4 %collective-permute-start.26 = (bf16[256,1536]{1,0:T(8,128)(2,1)}, bf16[256,1536]{1,0:T(8,128)(2,1)}, u32[]{:S(2)}, u32[]{:S(2)}) collective-permute-start(bf16[256,1536]{1,0:T(8,128)(2,1)} %slice.648), channel_id=1, source_target_pairs={{0,2},{1,3},{2,0},{3,1},{4,6},{5,7},{6,4},{7,5},{8,10},{9,11},{10,... | collective-permute-start | bytes 2359304 | tf_op jit(solution)/shard_map/ppermute | solution.py:553
  359.0 40.5 %collective-permute-start.30 = (bf16[256,1536]{1,0:T(8,128)(2,1)}, bf16[256,1536]{1,0:T(8,128)(2,1)}, u32[]{:S(2)}, u32[]{:S(2)}) collective-permute-start(bf16[256,1536]{1,0:T(8,128)(2,1)} %slice.647), channel_id=1, source_target_pairs={{0,2},{1,3},{2,0},{3,1},{4,6},{5,7},{6,4},{7,5},{8,10},{9,11},{10,... | collective-permute-start | bytes 2359304 | tf_op jit(solution)/shard_map/ppermute | solution.py:553
  359.9 35.4 %collective-permute-start.25 = (f32[256,1]{1,0:T(8,128)S(1)}, f32[256,1]{1,0:T(8,128)S(1)}, u32[]{:S(2)}, u32[]{:S(2)}) collective-permute-start(f32[256,1]{1,0:T(8,128)S(1)} %slice.463), channel_id=1, source_target_pairs={{0,2},{1,3},{2,0},{3,1},{4,6},{5,7},{6,4},{7,5},{8,10},{9,11},{10,... | collective-permute-start | bytes 3080 | tf_op jit(solution)/shard_map/ppermute | solution.py:553
  361.8 36.0 %collective-permute-start.29 = (f32[256,1]{1,0:T(8,128)}, f32[256,1]{1,0:T(8,128)}, u32[]{:S(2)}, u32[]{:S(2)}) collective-permute-start(f32[256,1]{1,0:T(8,128)} %slice.466), channel_id=1, source_target_pairs={{0,2},{1,3},{2,0},{3,1},{4,6},{5,7},{6,4},{7,5},{8,10},{9,11},{10,... | collective-permute-start | bytes 3080 | tf_op jit(solution)/shard_map/ppermute | solution.py:553
  438.1 211.3 %reduce-scatter.6.cloned.1.call-start = ((), (), s32[]{:S(2)}) async-start(), calls=%async_computation.8 | async-start | bytes 6635520 | tf_op jit(solution)/shard_map/reduce_scatter | solution.py:864
  518.5 19.9 %collective-permute-start.39 = (bf16[256,1536]{1,0:T(8,128)(2,1)}, bf16[256,1536]{1,0:T(8,128)(2,1)}, u32[]{:S(2)}, u32[]{:S(2)}) collective-permute-start(bf16[256,1536]{1,0:T(8,128)(2,1)} %slice.645), channel_id=1, source_target_pairs={{0,2},{1,3},{2,0},{3,1},{4,6},{5,7},{6,4},{7,5},{8,10},{9,11},{10,... | collective-permute-start | bytes 2359304 | tf_op jit(solution)/shard_map/ppermute | solution.py:553
  538.4 184.0 %reduce-scatter.8.cloned.1.call-start = ((), (), s32[]{:S(2)}) async-start(), calls=%async_computation.9 | async-start | bytes 2654208 | tf_op jit(solution)/shard_map/reduce_scatter | solution.py:864
  540.9 19.1 %collective-permute-start.37 = (bf16[256,1536]{1,0:T(8,128)(2,1)}, bf16[256,1536]{1,0:T(8,128)(2,1)}, u32[]{:S(2)}, u32[]{:S(2)}) collective-permute-start(bf16[256,1536]{1,0:T(8,128)(2,1)} %slice.646), channel_id=1, source_target_pairs={{0,2},{1,3},{2,0},{3,1},{4,6},{5,7},{6,4},{7,5},{8,10},{9,11},{10,... | collective-permute-start | bytes 2359304 | tf_op jit(solution)/shard_map/ppermute | solution.py:553
  566.7 18.1 %collective-permute-start.40 = (bf16[256,1536]{1,0:T(8,128)(2,1)}, bf16[256,1536]{1,0:T(8,128)(2,1)S(1)}, u32[]{:S(2)}, u32[]{:S(2)}) collective-permute-start(bf16[256,1536]{1,0:T(8,128)(2,1)} %get-tuple-element.165), channel_id=1, source_target_pairs={{0,2},{1,3},{2,0},{3,1},{4,6},{5,7},{6,4},{7,5},{8,10},{9,11},{10,... | collective-permute-start | bytes 2359304 | tf_op jit(solution)/shard_map/ppermute | solution.py:553
  572.9 13.5 %collective-permute-start.47 = (f32[512,2]{0,1:T(2,128)S(1)}, f32[512,2]{0,1:T(2,128)S(1)}, u32[]{:S(2)}, u32[]{:S(2)}) collective-permute-start(f32[512,2]{0,1:T(2,128)S(1)} %maximum_maximum_fusion.1), channel_id=1, source_target_pairs={{0,1},{1,0},{2,3},{3,2},{4,5},{5,4},{6,7},{7,6},{8,9},{9,8},{10,11... | collective-permute-start | bytes 12296 | tf_op jit(solution)/shard_map/ppermute | solution.py:553
  574.0 28.7 %collective-permute-start.42 = (bf16[256,1536]{1,0:T(8,128)(2,1)}, bf16[256,1536]{1,0:T(8,128)(2,1)S(1)}, u32[]{:S(2)}, u32[]{:S(2)}) collective-permute-start(bf16[256,1536]{1,0:T(8,128)(2,1)} %get-tuple-element.165), channel_id=1, source_target_pairs={{0,1},{1,0},{2,3},{3,2},{4,5},{5,4},{6,7},{7,6},{8,9},{9,8},{10,11... | collective-permute-start | bytes 2359304 | tf_op jit(solution)/shard_map/ppermute | solution.py:553
  584.8 17.0 %collective-permute-start.41 = (bf16[256,1536]{1,0:T(8,128)(2,1)S(1)}, bf16[256,1536]{1,0:T(8,128)(2,1)S(1)}, u32[]{:S(2)}, u32[]{:S(2)}) collective-permute-start(bf16[256,1536]{1,0:T(8,128)(2,1)S(1)} %get-tuple-element.168), channel_id=1, source_target_pairs={{0,2},{1,3},{2,0},{3,1},{4,6},{5,7},{6,4},{7,5},{8,10},{9,11},{10,... | collective-permute-start | bytes 2359304 | tf_op jit(solution)/shard_map/ppermute | solution.py:553
  586.4 17.3 %collective-permute-start.43 = (bf16[256,1536]{1,0:T(8,128)(2,1)S(1)}, bf16[256,1536]{1,0:T(8,128)(2,1)}, u32[]{:S(2)}, u32[]{:S(2)}) collective-permute-start(bf16[256,1536]{1,0:T(8,128)(2,1)S(1)} %get-tuple-element.168), channel_id=1, source_target_pairs={{0,1},{1,0},{2,3},{3,2},{4,5},{5,4},{6,7},{7,6},{8,9},{9,8},{10,11... | collective-permute-start | bytes 2359304 | tf_op jit(solution)/shard_map/ppermute | solution.py:553
  588.9 16.9 %collective-permute-start.44 = (bf16[256,1536]{1,0:T(8,128)(2,1)S(1)}, bf16[256,1536]{1,0:T(8,128)(2,1)S(1)}, u32[]{:S(2)}, u32[]{:S(2)}) collective-permute-start(bf16[256,1536]{1,0:T(8,128)(2,1)S(1)} %collective-permute-done.40), channel_id=1, source_target_pairs={{0,1},{1,0},{2,3},{3,2},{4,5},{5,4},{6,7},{7,6},{8,9},{9,8},{10,11... | collective-permute-start | bytes 2359304 | tf_op jit(solution)/shard_map/ppermute | solution.py:553
  724.6 20.2 %collective-permute-start.50 = (bf16[512,1536]{1,0:T(8,128)(2,1)S(1)}, bf16[512,1536]{1,0:T(8,128)(2,1)S(1)}, u32[]{:S(2)}, u32[]{:S(2)}) collective-permute-start(bf16[512,1536]{1,0:T(8,128)(2,1)S(1)} %get-tuple-element.424), channel_id=1, source_target_pairs={{0,1},{1,0},{2,3},{3,2},{4,5},{5,4},{6,7},{7,6},{8,9},{9,8},{10,11... | collective-permute-start | bytes 4718600 | tf_op jit(solution)/shard_map/ppermute | solution.py:553
  724.7 20.1 %collective-permute-start.49 = (bf16[512,1536]{1,0:T(8,128)(2,1)S(1)}, bf16[512,1536]{1,0:T(8,128)(2,1)S(1)}, u32[]{:S(2)}, u32[]{:S(2)}) collective-permute-start(bf16[512,1536]{1,0:T(8,128)(2,1)S(1)} %get-tuple-element.425), channel_id=1, source_target_pairs={{0,1},{1,0},{2,3},{3,2},{4,5},{5,4},{6,7},{7,6},{8,9},{9,8},{10,11... | collective-permute-start | bytes 4718600 | tf_op jit(solution)/shard_map/ppermute | solution.py:553
  770.7 19.7 %collective-permute-start.53 = (bf16[192,1920]{1,0:T(8,128)(2,1)}, bf16[192,1920]{1,0:T(8,128)(2,1)}, u32[]{:S(2)}, u32[]{:S(2)}) collective-permute-start(bf16[192,1920]{1,0:T(8,128)(2,1)} %get-tuple-element.420), channel_id=1, source_target_pairs={{0,8},{8,16},{16,24},{24,28},{28,20},{20,12},{12,4},{4,0},{1,9},{9... | collective-permute-start | bytes 2211848 | tf_op jit(solution)/shard_map/ppermute | solution.py:611
  771.4 16.4 %collective-permute-start.68 = (f32[2,5924]{1,0:T(2,128)S(1)}, f32[2,5924]{1,0:T(2,128)S(1)}, u32[]{:S(2)}, u32[]{:S(2)}) collective-permute-start(f32[2,5924]{1,0:T(2,128)S(1)} %add.607), channel_id=1, source_target_pairs={{0,16},{4,20},{8,24},{12,28},{16,0},{20,4},{24,8},{28,12},{1,17},{... | collective-permute-start | bytes 142184 | tf_op jit(solution)/shard_map/ppermute | solution.py:645
  780.6 20.8 %collective-permute-start.52 = (bf16[256,1536]{1,0:T(8,128)(2,1)}, bf16[256,1536]{1,0:T(8,128)(2,1)}, u32[]{:S(2)}, u32[]{:S(2)}) collective-permute-start(bf16[256,1536]{1,0:T(8,128)(2,1)} %slice.643), channel_id=1, source_target_pairs={{0,2},{1,3},{2,0},{3,1},{4,6},{5,7},{6,4},{7,5},{8,10},{9,11},{10,... | collective-permute-start | bytes 2359304 | tf_op jit(solution)/shard_map/ppermute | solution.py:553
  781.1 34.8 %collective-permute-start.51 = (bf16[256,1536]{1,0:T(8,128)(2,1)}, bf16[256,1536]{1,0:T(8,128)(2,1)}, u32[]{:S(2)}, u32[]{:S(2)}) collective-permute-start(bf16[256,1536]{1,0:T(8,128)(2,1)} %slice.644), channel_id=1, source_target_pairs={{0,2},{1,3},{2,0},{3,1},{4,6},{5,7},{6,4},{7,5},{8,10},{9,11},{10,... | collective-permute-start | bytes 2359304 | tf_op jit(solution)/shard_map/ppermute | solution.py:553
  782.6 39.9 %collective-permute-start.57 = (bf16[192,1920]{1,0:T(8,128)(2,1)}, bf16[192,1920]{1,0:T(8,128)(2,1)}, u32[]{:S(2)}, u32[]{:S(2)}) collective-permute-start(bf16[192,1920]{1,0:T(8,128)(2,1)} %get-tuple-element.421), channel_id=1, source_target_pairs={{0,4},{8,0},{16,8},{24,16},{28,24},{20,28},{12,20},{4,12},{1,5},{9... | collective-permute-start | bytes 2211848 | tf_op jit(solution)/shard_map/ppermute | solution.py:611
  792.1 30.4 %collective-permute-start.54 = (bf16[192,1920]{1,0:T(8,128)(2,1)S(1)}, bf16[192,1920]{1,0:T(8,128)(2,1)S(1)}, u32[]{:S(2)}, u32[]{:S(2)}) collective-permute-start(bf16[192,1920]{1,0:T(8,128)(2,1)S(1)} %add_convert_fusion.4), channel_id=1, source_target_pairs={{0,8},{8,16},{16,24},{24,28},{28,20},{20,12},{12,4},{4,0},{1,9},{9... | collective-permute-start | bytes 2211848 | tf_op jit(solution)/shard_map/ppermute | solution.py:611
  825.8 19.2 %collective-permute-start.55 = (bf16[192,1920]{1,0:T(8,128)(2,1)}, bf16[192,1920]{1,0:T(8,128)(2,1)}, u32[]{:S(2)}, u32[]{:S(2)}) collective-permute-start(bf16[192,1920]{1,0:T(8,128)(2,1)} %get-tuple-element.418), channel_id=1, source_target_pairs={{0,8},{8,16},{16,24},{24,28},{28,20},{20,12},{12,4},{4,0},{1,9},{9... | collective-permute-start | bytes 2211848 | tf_op jit(solution)/shard_map/ppermute | solution.py:611
  826.4 18.7 %collective-permute-start.58 = (bf16[192,1920]{1,0:T(8,128)(2,1)}, bf16[192,1920]{1,0:T(8,128)(2,1)}, u32[]{:S(2)}, u32[]{:S(2)}) collective-permute-start(bf16[192,1920]{1,0:T(8,128)(2,1)} %get-tuple-element.419), channel_id=1, source_target_pairs={{0,4},{8,0},{16,8},{24,16},{28,24},{20,28},{12,20},{4,12},{1,5},{9... | collective-permute-start | bytes 2211848 | tf_op jit(solution)/shard_map/ppermute | solution.py:611
  831.5 13.4 %collective-permute-start.71 = (f32[2,1536]{1,0:T(2,128)S(1)}, f32[2,1536]{1,0:T(2,128)S(1)}, u32[]{:S(2)}, u32[]{:S(2)}) collective-permute-start(f32[2,1536]{1,0:T(2,128)S(1)} %fusion.76), channel_id=1, source_target_pairs={{0,4},{4,0},{8,12},{12,8},{16,20},{20,16},{24,28},{28,24},{1,5},{5... | collective-permute-start | bytes 36872 | tf_op jit(solution)/shard_map/ppermute | solution.py:645
  847.7 20.8 %collective-permute-start.56 = (bf16[192,1920]{1,0:T(8,128)(2,1)S(1)}, bf16[192,1920]{1,0:T(8,128)(2,1)S(1)}, u32[]{:S(2)}, u32[]{:S(2)}) collective-permute-start(bf16[192,1920]{1,0:T(8,128)(2,1)S(1)} %get-tuple-element.416), channel_id=1, source_target_pairs={{0,8},{8,16},{16,24},{24,28},{28,20},{20,12},{12,4},{4,0},{1,9},{9... | collective-permute-start | bytes 2211848 | tf_op jit(solution)/shard_map/ppermute | solution.py:611
  849.6 19.0 %collective-permute-start.59 = (bf16[192,1920]{1,0:T(8,128)(2,1)S(1)}, bf16[192,1920]{1,0:T(8,128)(2,1)S(1)}, u32[]{:S(2)}, u32[]{:S(2)}) collective-permute-start(bf16[192,1920]{1,0:T(8,128)(2,1)S(1)} %get-tuple-element.417), channel_id=1, source_target_pairs={{0,4},{8,0},{16,8},{24,16},{28,24},{20,28},{12,20},{4,12},{1,5},{9... | collective-permute-start | bytes 2211848 | tf_op jit(solution)/shard_map/ppermute | solution.py:611
  852.9 14.9 %collective-permute-start.73 = (f32[2,1536]{1,0:T(2,128)S(1)}, f32[2,1536]{1,0:T(2,128)S(1)}, u32[]{:S(2)}, u32[]{:S(2)}) collective-permute-start(f32[2,1536]{1,0:T(2,128)S(1)} %add.633), channel_id=1, source_target_pairs={{0,16},{4,20},{8,24},{12,28},{16,0},{20,4},{24,8},{28,12},{1,17},{... | collective-permute-start | bytes 36872 | tf_op jit(solution)/shard_map/ppermute | solution.py:645
  (142 other events, 1476.6 us)
Sparse Core Ops, SparseCore 0:
  18.7 66.7 all-gather.4
  88.3 78.3 all-gather.6
  168.9 63.3 all-gather.8
  234.3 78.3 all-gather.10
  438.2 67.0 reduce-scatter.3
  538.5 110.8 reduce-scatter.5
  653.5 68.8 reduce-scatter.7

commit v2 on v1

--- a/solution.py
+++ b/solution.py
@@ -806,17 +806,24 @@
             first_full = jnp.concatenate(
                 [first_grad, first_far, swap(first_grad, 1, tensor_count), swap(first_far, 1, tensor_count)], axis=0
             )
+            y, first_full = lax.optimization_barrier((y, first_full))
         gate_z = None
-        far_list, near_list, inv_list = [], [], []
+        near_list, square_list = [], []
         for part in range(pieces):
             gate_z, sent, held, squares = gate_forward(rows, y, gate_weight, gain_q, gate_z, part, pieces)
-            near = reduce_near(sent, held, tensor_count, LOW)
-            near, squares = lax.optimization_barrier((near, squares))
-            middle = squares.shape[0] // 2
-            square_own = reduce_slots(squares[middle:], squares[:middle], tensor_count, F32)
-            inv_list.append(lax.rsqrt(square_own / INNER + NORM_EPS))
-            near_list.append(near)
-            far_list.append(swap_far(near, tensor_count, LOW))
+            near_list.append(reduce_near(sent, held, tensor_count, LOW))
+            square_list.append(squares)
+        middle = square_list[0].shape[0] // 2
+        square_sent = jnp.concatenate(
+            [vals[middle + spot : middle + spot + BLOCK] for spot in range(0, middle, BLOCK) for vals in square_list]
+        )
+        square_held = jnp.concatenate(
+            [vals[spot : spot + BLOCK] for spot in range(0, middle, BLOCK) for vals in square_list]
+        )
+        square_own = reduce_slots(square_sent, square_held, tensor_count, F32)
+        near_list, square_own = lax.optimization_barrier((near_list, square_own))
+        inv_list = in_parts(lax.rsqrt(square_own / INNER + NORM_EPS))
+        far_list = [swap_far(near, tensor_count, LOW) for near in near_list]
         next_gain = gain_all[min(layer + 1, layer_total - 1)][None, :]
 
         def next_rows(spot, far, near_list=near_list, inv_list=inv_list, hidden=hidden, next_gain=next_gain):
@@ -881,7 +888,6 @@
         dy, out_grad = lax.optimization_barrier((dy, out_grad))
         if layer + 1 < layer_total:
             late, out_grad = lax.optimization_barrier((late, out_grad))
-            place_scan(layer + 1, late.astype(F32))
         out_sum = owned(out_grad)
         dmerged, dnormed, conv_grad, head_grad, skip_grad = scan_backward(
             me, dy, y, pre, states, conv_par, head_vals, skip, spread, dz, gate_weight, scan_weight, pieces
@@ -896,12 +902,17 @@
             )
         merged_grad = dot(rows, dmerged, 0, 0)
         if layer == 0:
-            small_sums = (conv_grad, head_grad, skip_grad, gain_five)
-            near_list, merged_grad, small_sums = lax.optimization_barrier((near_list, merged_grad, small_sums))
-            conv_grad, head_grad, skip_grad, gain_five = small_sums
+            near_list, merged_grad = lax.optimization_barrier((near_list, merged_grad))
         far_list = [swap_far(near, tensor_count, LOW) for near in near_list]
         if layer == 0:
-            place_scan(layer, RingReduce(merged_grad, dp_count).finish())
+            ring = RingReduce(merged_grad, dp_count)
+            ring.hop()
+            rest = (conv_grad, head_grad, skip_grad, gain_five, out_sum, late)
+            ring.moving, rest = lax.optimization_barrier((ring.moving, rest))
+            conv_grad, head_grad, skip_grad, gain_five, out_sum, late = rest
+            if layer + 1 < layer_total:
+                place_scan(layer + 1, late.astype(F32))
+            place_scan(layer, ring.finish())
         else:
             far_list[-1], merged_grad = lax.optimization_barrier((far_list[-1], merged_grad.astype(LOW)))
             late = owned(merged_grad)

time: 905 us -> 903 us (level)
  waiting for transfers between devices: 279 us -> 257 us
  other arithmetic: 104 us -> 118 us
  local copies, waits for them, and re-layouts: 94.7 us -> 104 us
    ppermute x52 -> x48, waiting for transfers between devices: 199 us -> 176 us  [swap(): lax.ppermute(vals, 'tensor', [(src, src ^ distance) for src in range(coun...]
    ppermute x7, waiting for transfers between devices: 0.02 us -> 20.5 us  [ring_step(): return lax.ppermute(vals, 'dp', pairs)]
    slice x4 -> x20, local copies, waits for them, and re-layouts: 0.07 us -> 18.7 us  [the longest x12 10.4 us: local(): vals[spot:spot + BLOCK]]
    all_gather x2, waiting for transfers between devices: 25.3 us -> 9.33 us  [local(): gate_weight = lax.all_gather(gate_share, 'dp', axis=0, tiled=True)]
    ppermute x15, waiting for transfers between devices: 34.3 us -> 24 us  [xor_step(): lax.ppermute(vals, axis, [(src, src ^ distance) for src in range(count)])]
    unnamed x250 -> x231, local copies, waits for them, and re-layouts: 40.4 us -> 31.9 us
    ppermute x52 -> x48, starting transfers between devices: 34.8 us -> 29.8 us  [swap(): lax.ppermute(vals, 'tensor', [(src, src ^ distance) for src in range(coun...]
  transfers between devices with their start and end apart: 81 -> 77, of which waited for: 35 -> 38; matrix products, arithmetic and copies ran while one was open for 22% -> 25% of each run, Pallas kernels for 30% -> 28%
where the time goes in v2:
time: 903 us; the launch traced here: 894 us
  Pallas kernels  283 us (31%)
  waiting for transfers between devices  257 us (28%)
  other arithmetic  118 us (13%)
  local copies, waits for them, and re-layouts  104 us (12%)
  starting transfers between devices  57.3 us (6%)
  matrix products  52.4 us (6%)
  between operations  16.5 us (2%)
    ppermute x48, waiting for transfers between devices, swap(): lax.ppermute(vals, 'tensor', [(src, src ^ distance) for src in range(coun...  176 us
    pallas_call x2, Pallas kernels, scan_backward(): pl.pallas_call(scan_back_kernel, out_shape=(jax.ShapeDtypeStruct((total,...  127 us
    pallas_call x2, Pallas kernels, scan_forward(): pl.pallas_call(scan_kernel, out_shape=(jax.ShapeDtypeStruct((total, pre_w...  70 us
    dot_general x4, matrix products, dot(): lax.dot_general(left, right, (((left_dim,), (right_dim,)), ((), ())), pre...  52.4 us
    pallas_call x4, Pallas kernels, gate_forward(): pl.pallas_call(gate_kernel, out_shape=(jax.ShapeDtypeStruct((total, width...  47.5 us
    pallas_call x2, Pallas kernels, gate_backward(): pl.pallas_call(gate_back_kernel, out_shape=(jax.ShapeDtypeStruct((total,...  34.8 us
    unnamed x231, local copies, waits for them, and re-layouts  31.9 us
    ppermute x48, starting transfers between devices, swap(): lax.ppermute(vals, 'tensor', [(src, src ^ distance) for src in range(coun...  29.8 us
  transfers between devices with their start and end apart: 77, of which 38 were waited for; matrix products, arithmetic and copies ran while one was open for 25% of the time, Pallas kernels for 28%

profile of v2, /device:TPU:0, one launch (start us, length us, event | category | flops | bytes accessed | tf_op | source)
XLA Modules:
  0.0 894.2 jit_solution(217899575464386259)
XLA Ops:
  8.1 6.8 all_gather.15
  22.0 3.0 first_root.1
  32.9 2.8 collective-permute-start.2
  45.6 3.2 concatenate.137
  57.7 34.4 %collective-permute-done.5 = bf16[512,1536]{1,0:T(8,128)(2,1)} collective-permute-done((bf16[512,1536]{1,0:T(8,128)(2,1)}, bf16[512,1536]{1,0:T(8,128)(2,1)}, u32[]{:S(2)}, u32[]{:S(2)}) %collective-permute-start.5) | collective-permute-done | bytes 1572896 | tf_op jit(solution)/shard_map/ppermute | solution.py:553
  93.6 3.3 convert_element_type.235
  104.9 6.3 pad_maximum_fusion.rows_ref
  112.0 35.1 %scan_forward.2 = (f32[2048,1152]{1,0:T(8,128)}, f32[2048,768]{1,0:T(8,128)}, f32[8,128,768]{2,1,0:T(8,128)}) custom-call(s32[1]{0:T(128)} %bitcast.5.me_ref, bf16[2048,1536]{1,0:T(8,128)(2,1)} %pad_maximum_fusion.rows_ref, bf16[1536,1152]{1,0:T(8,128)(2,1)} %all-gather.5.cloned.1.call-done.weight_ref, f32[8,1024]{1,0:T(8,128)} %select_maximum_fusion.1.conv_ref, ...), custom_call_target="tpu_custom_call" | custom-call | flops 28991029248 | bytes 1572864 | tf_op jit(solution)/shard_map/scan_forward/pallas_call | solution.py:341
  152.2 6.5 pad_maximum_fusion.1.grad_ref
  158.7 9.3 %all-gather.7.cloned.1.call-done.z_weight_ref.out_weight_ref = bf16[1536,1536]{1,0:T(8,128)(2,1)} async-done(((bf16[192,1536]{1,0:T(8,128)(2,1)}), bf16[1536,1536]{1,0:T(8,128)(2,1)}) %all-gather.7.cloned.1.call-update) | async-done | bytes 4718608 | tf_op jit(solution)/shard_map/all_gather | solution.py:758
  168.0 11.8 %gate_forward.4 = (f32[2048,768]{1,0:T(8,128)}, bf16[512,1536]{1,0:T(8,128)(2,1)}, bf16[512,1536]{1,0:T(8,128)(2,1)}, f32[1024,1]{1,0:T(8,128)}) custom-call(bf16[2048,1536]{1,0:T(8,128)(2,1)} %pad_maximum_fusion.rows_ref, f32[2048,768]{1,0:T(8,128)} %get-tuple-element.128.y_ref, bf16[1536,1536]{1,0:T(8,128)(2,1)} %all-gather.7.cloned.1.call-done.z_weight_ref.out_weight_ref, ...), custom_call_target="tpu_custom_call" | custom-call | flops 19327352832 | bytes 12582912 | tf_op jit(solution)/shard_map/gate_forward/pallas_call | solution.py:392
  179.9 11.9 %gate_forward.5 = (f32[2048,768]{1,0:T(8,128)}, bf16[512,1536]{1,0:T(8,128)(2,1)}, bf16[512,1536]{1,0:T(8,128)(2,1)}, f32[1024,1]{1,0:T(8,128)}) custom-call(bf16[2048,1536]{1,0:T(8,128)(2,1)} %pad_maximum_fusion.rows_ref, f32[2048,768]{1,0:T(8,128)} %get-tuple-element.128.y_ref, ...), custom_call_target="tpu_custom_call", output_to_operand_aliasing={{0}: (5, {})} | custom-call | flops 19327352832 | bytes 12582912 | tf_op jit(solution)/shard_map/gate_forward/pallas_call | solution.py:392
  207.2 4.7 convert_add_fusion.6
  216.5 17.1 %collective-permute-done.15 = bf16[256,1536]{1,0:T(8,128)(2,1)} collective-permute-done((bf16[256,1536]{1,0:T(8,128)(2,1)}, bf16[256,1536]{1,0:T(8,128)(2,1)}, u32[]{:S(2)}, u32[]{:S(2)}) %collective-permute-start.15) | collective-permute-done | bytes 786464 | tf_op jit(solution)/shard_map/ppermute | solution.py:553
  238.6 11.8 %collective-permute-done.16 = bf16[256,1536]{1,0:T(8,128)(2,1)S(1)} collective-permute-done((bf16[256,1536]{1,0:T(8,128)(2,1)S(1)}, bf16[256,1536]{1,0:T(8,128)(2,1)S(1)}, u32[]{:S(2)}, u32[]{:S(2)}) %collective-permute-start.16) | collective-permute-done | bytes 786464 | tf_op jit(solution)/shard_map/ppermute | solution.py:553
  251.2 2.7 constant_dynamic-update-slice_fusion.7
  255.1 10.7 %collective-permute-done.17 = bf16[256,1536]{1,0:T(8,128)(2,1)S(1)} collective-permute-done((bf16[256,1536]{1,0:T(8,128)(2,1)}, bf16[256,1536]{1,0:T(8,128)(2,1)S(1)}, u32[]{:S(2)}, u32[]{:S(2)}) %collective-permute-start.17) | collective-permute-done | bytes 786464 | tf_op jit(solution)/shard_map/ppermute | solution.py:553
  273.1 11.8 %collective-permute-done.18 = bf16[256,1536]{1,0:T(8,128)(2,1)S(1)} collective-permute-done((bf16[256,1536]{1,0:T(8,128)(2,1)S(1)}, bf16[256,1536]{1,0:T(8,128)(2,1)S(1)}, u32[]{:S(2)}, u32[]{:S(2)}) %collective-permute-start.18) | collective-permute-done | bytes 786464 | tf_op jit(solution)/shard_map/ppermute | solution.py:553
  289.6 34.9 %scan_forward.3 = (f32[2048,1152]{1,0:T(8,128)}, f32[2048,768]{1,0:T(8,128)}, f32[8,128,768]{2,1,0:T(8,128)}) custom-call(s32[1]{0:T(128)} %bitcast.5.me_ref, bf16[2048,1536]{1,0:T(8,128)(2,1)} %constant_dynamic-update-slice_fusion.rows_ref, bf16[1536,1152]{1,0:T(8,128)(2,1)} %all-gather.9.cloned.1.call-done.weight_ref, ...), custom_call_target="tpu_custom_call" | custom-call | flops 362387872 | bytes 1572864 | tf_op jit(solution)/shard_map/scan_forward/pallas_call | solution.py:341
  324.5 12.0 %gate_forward.6 = (f32[2048,768]{1,0:T(8,128)}, bf16[512,1536]{1,0:T(8,128)(2,1)}, bf16[512,1536]{1,0:T(8,128)(2,1)}, f32[1024,1]{1,0:T(8,128)}) custom-call(bf16[2048,1536]{1,0:T(8,128)(2,1)} %constant_dynamic-update-slice_fusion.rows_ref, f32[2048,768]{1,0:T(8,128)} %get-tuple-element.143.y_ref, ...), custom_call_target="tpu_custom_call" | custom-call | flops 19327352832 | bytes 12582912 | tf_op jit(solution)/shard_map/gate_forward/pallas_call | solution.py:392
  337.1 11.8 %gate_forward.7 = (f32[2048,768]{1,0:T(8,128)}, bf16[512,1536]{1,0:T(8,128)(2,1)}, bf16[512,1536]{1,0:T(8,128)(2,1)}, f32[1024,1]{1,0:T(8,128)}) custom-call(bf16[2048,1536]{1,0:T(8,128)(2,1)} %constant_dynamic-update-slice_fusion.rows_ref, f32[2048,768]{1,0:T(8,128)} %get-tuple-element.143.y_ref, ...), custom_call_target="tpu_custom_call", output_to_operand_aliasing={{0}: (5, {})} | custom-call | flops 19327352832 | bytes 12582912 | tf_op jit(solution)/shard_map/gate_forward/pallas_call | solution.py:392
  371.8 18.3 %collective-permute-done.28 = bf16[256,1536]{1,0:T(8,128)(2,1)S(1)} collective-permute-done((bf16[256,1536]{1,0:T(8,128)(2,1)S(1)}, bf16[256,1536]{1,0:T(8,128)(2,1)S(1)}, u32[]{:S(2)}, u32[]{:S(2)}) %collective-permute-start.28) | collective-permute-done | bytes 786464 | tf_op jit(solution)/shard_map/ppermute | solution.py:553
  390.1 14.7 %collective-permute-done.27 = bf16[256,1536]{1,0:T(8,128)(2,1)S(1)} collective-permute-done((bf16[256,1536]{1,0:T(8,128)(2,1)S(1)}, bf16[256,1536]{1,0:T(8,128)(2,1)S(1)}, u32[]{:S(2)}, u32[]{:S(2)}) %collective-permute-start.27) | collective-permute-done | bytes 786464 | tf_op jit(solution)/shard_map/ppermute | solution.py:553
  413.4 17.3 %gate_backward.2 = (bf16[2048,768]{1,0:T(8,128)(2,1)}, f32[2048,768]{1,0:T(8,128)}, bf16[2048,768]{1,0:T(8,128)(2,1)}, f32[1,768]{1,0:T(1,128)}) custom-call(bf16[2048,1536]{1,0:T(8,128)(2,1)} %pad_maximum_fusion.1.grad_ref, f32[2048,768]{1,0:T(8,128)} %get-tuple-element.143.y_ref, f32[2048,768]{1,0:T(8,128)} %get-tuple-element.155.z_ref, ...), custom_call_target="tpu_custom_call" | custom-call | flops 1572864 | bytes 1572864 | tf_op jit(solution)/shard_map/gate_backward/pallas_call | solution.py:433
  430.7 9.2 %convolution_convert_fusion.2 = bf16[1536,768]{1,0:T(8,128)(2,1)} fusion(bf16[2048,1536]{1,0:T(8,128)(2,1)} %pad_maximum_fusion.1.grad_ref, bf16[2048,768]{1,0:T(8,128)(2,1)} %get-tuple-element.157), kind=kOutput, calls=%fused_computation.5 | convolution fusion | flops 4833017856 | bytes 11796480 | tf_op jit(solution)/shard_map/dot_general | solution.py:34
  441.7 63.9 %scan_backward.2 = (bf16[2048,1920]{1,0:T(8,128)(2,1)}, bf16[2048,1536]{1,0:T(8,128)(2,1)}, f32[8,1024]{1,0:T(8,128)}, f32[8,128]{1,0:T(8,128)}, f32[8,768]{1,0:T(8,128)}) custom-call(s32[1]{0:T(128)} %bitcast.5.me_ref, f32[2048,768]{1,0:T(8,128)} %get-tuple-element.159.dy_ref, f32[2048,768]{1,0:T(8,128)} %get-tuple-element.143.y_ref, ...), custom_call_target="tpu_custom_call" | custom-call | flops 1572864 | bytes 1572864 | tf_op jit(solution)/shard_map/scan_backward/pallas_call | solution.py:489
  510.1 2.9 collective-permute-done.32
  522.0 15.8 %convolution_convert_fusion = bf16[1536,1920]{1,0:T(8,128)(2,1)} fusion(bf16[2048,1536]{1,0:T(8,128)(2,1)S(1)} %bitcast.125, bf16[2048,1920]{1,0:T(8,128)(2,1)S(1)} %copy-done.96), kind=kOutput, calls=%fused_computation | convolution fusion | flops 12082544640 | bytes 20054016 | tf_op jit(solution)/shard_map/dot_general | solution.py:34
  543.6 17.3 %collective-permute-done.33 = bf16[256,1536]{1,0:T(8,128)(2,1)S(1)} collective-permute-done((bf16[256,1536]{1,0:T(8,128)(2,1)S(1)}, bf16[256,1536]{1,0:T(8,128)(2,1)S(1)}, u32[]{:S(2)}, u32[]{:S(2)}) %collective-permute-start.33) | collective-permute-done | bytes 786464 | tf_op jit(solution)/shard_map/ppermute | solution.py:553
  562.8 4.4 multiply_reduce_fusion.7
  570.6 3.1 multiply_reduce_fusion.6
  577.7 7.8 collective-permute-done.36
  590.7 11.9 %collective-permute-done.37 = bf16[256,1536]{1,0:T(8,128)(2,1)S(1)} collective-permute-done((bf16[256,1536]{1,0:T(8,128)(2,1)S(1)}, bf16[256,1536]{1,0:T(8,128)(2,1)S(1)}, u32[]{:S(2)}, u32[]{:S(2)}) %collective-permute-start.37) | collective-permute-done | bytes 786464 | tf_op jit(solution)/shard_map/ppermute | solution.py:553
  608.5 17.4 %gate_backward.3 = (bf16[2048,768]{1,0:T(8,128)(2,1)}, f32[2048,768]{1,0:T(8,128)}, bf16[2048,768]{1,0:T(8,128)(2,1)}, f32[1,768]{1,0:T(1,128)}) custom-call(bf16[2048,1536]{1,0:T(8,128)(2,1)} %constant_dynamic-update-slice_fusion.13.grad_ref, f32[2048,768]{1,0:T(8,128)} %get-tuple-element.128.y_ref, f32[2048,768]{1,0:T(8,128)} %get-tuple-element.173.z_ref, ...), custom_call_target="tpu_custom_call" | custom-call | flops 1572864 | bytes 1572864 | tf_op jit(solution)/shard_map/gate_backward/pallas_call | solution.py:433
  626.0 9.3 %convolution_convert_fusion.1 = bf16[1536,768]{1,0:T(8,128)(2,1)} fusion(bf16[2048,1536]{1,0:T(8,128)(2,1)} %constant_dynamic-update-slice_fusion.13.grad_ref, bf16[2048,768]{1,0:T(8,128)(2,1)} %get-tuple-element.175), kind=kOutput, calls=%fused_computation.4 | convolution fusion | flops 4833017856 | bytes 11796480 | tf_op jit(solution)/shard_map/dot_general | solution.py:34
  635.2 16.3 %reduce-scatter.6.cloned.1.call-done = bf16[192,1920]{1,0:T(8,128)(2,1)} async-done(((bf16[1536,1920]{1,0:T(8,128)(2,1)}), bf16[192,1920]{1,0:T(8,128)(2,1)}) %reduce-scatter.6.cloned.1.call-update) | async-done | bytes 737296 | tf_op jit(solution)/shard_map/reduce_scatter | solution.py:871
  652.5 63.5 %scan_backward.3 = (bf16[2048,1920]{1,0:T(8,128)(2,1)}, bf16[2048,1536]{1,0:T(8,128)(2,1)}, f32[8,1024]{1,0:T(8,128)}, f32[8,128]{1,0:T(8,128)}, f32[8,768]{1,0:T(8,128)}) custom-call(s32[1]{0:T(128)} %bitcast.5.me_ref, f32[2048,768]{1,0:T(8,128)} %get-tuple-element.178.dy_ref, f32[2048,768]{1,0:T(8,128)} %get-tuple-element.128.y_ref, ...), custom_call_target="tpu_custom_call" | custom-call | flops 1572864 | bytes 1572864 | tf_op jit(solution)/shard_map/scan_backward/pallas_call | solution.py:489
  716.0 8.4 reduce-scatter.8.cloned.1.call-done
  727.2 18.1 %fusion.53 = f32[1536,1920]{1,0:T(8,128)S(1)} fusion(bf16[2048,1536]{1,0:T(8,128)(2,1)} %pad_maximum_fusion.rows_ref, bf16[2048,1920]{1,0:T(8,128)(2,1)} %get-tuple-element.185), kind=kOutput, calls=%fused_computation.274 | convolution fusion | flops 12079595520 | bytes 25952256 | tf_op jit(solution)/shard_map/dot_general | solution.py:34
  748.0 3.3 copy-done.15
  763.8 7.7 collective-permute-done.50
  772.2 3.6 add_convert_fusion.3
  791.9 5.4 collective-permute-done.61
  799.5 4.0 multiply_reduce_fusion.3
  809.9 4.1 multiply_subtract_fusion.2
  823.0 12.1 %collective-permute-done.68 = f32[2,1536]{1,0:T(2,128)S(1)} collective-permute-done((f32[2,1536]{1,0:T(2,128)S(1)}, f32[2,1536]{1,0:T(2,128)S(1)}, u32[]{:S(2)}, u32[]{:S(2)}) %collective-permute-start.68) | collective-permute-done | bytes 12320 | tf_op jit(solution)/shard_map/ppermute | solution.py:645
  847.8 10.6 %collective-permute-done.55 = bf16[192,1920]{1,0:T(8,128)(2,1)S(1)} collective-permute-done((bf16[192,1920]{1,0:T(8,128)(2,1)S(1)}, bf16[192,1920]{1,0:T(8,128)(2,1)S(1)}, u32[]{:S(2)}, u32[]{:S(2)}) %collective-permute-start.55) | collective-permute-done | bytes 737312 | tf_op jit(solution)/shard_map/ppermute | solution.py:611
  867.9 10.8 %multiply_subtract_fusion = (f32[2,192,2,768]{3,2,1,0:T(2,128)}, f32[2,192,2,768]{3,2,1,0:T(2,128)}, f32[2,192,2,768]{3,2,1,0:T(2,128)}) fusion(f32[2,192,2,768]{3,2,1,0:T(2,128)S(1)} %copy-done.14, f32[1,192,2,768]{3,2,1,0:T(2,128)S(1)} %copy-done.19, f32[1,192,2,768]{3,2,1,0:T(2,128)} %copy.277, f32[2,192,2,768]{3,2,1,0:T(2,128)} %param.36, ...), kind=kLoop, calls=%fused_computation.20 | loop fusion | flops 9437184 | bytes 16515072 | tf_op jit(solution)/shard_map/sub | solution.py:677
  (580 shorter events, 244.5 us)
Async XLA Ops:
  7.2 84.9 %all-gather.5.cloned.1.call-start = ((), (), s32[]{:S(2)}) async-start(), calls=%async_computation.3 | async-start | bytes 3981312 | tf_op jit(solution)/shard_map/all_gather | solution.py:757
  19.9 148.1 %all-gather.7.cloned.1.call-start = ((), (), s32[]{:S(2)}) async-start(), calls=%async_computation.4 | async-start | bytes 5308416 | tf_op jit(solution)/shard_map/all_gather | solution.py:758
  21.7 267.9 %all-gather.9.cloned.1.call-start = ((), (), s32[]{:S(2)}) async-start(), calls=%async_computation.5 | async-start | bytes 3981312 | tf_op jit(solution)/shard_map/all_gather | solution.py:757
  55.6 36.5 %collective-permute-start.5 = (bf16[512,1536]{1,0:T(8,128)(2,1)}, bf16[512,1536]{1,0:T(8,128)(2,1)}, u32[]{:S(2)}, u32[]{:S(2)}) collective-permute-start(bf16[512,1536]{1,0:T(8,128)(2,1)} %multiply_convert_fusion), channel_id=1, source_target_pairs={{0,2},{1,3},{2,0},{3,1},{4,6},{5,7},{6,4},{7,5},{8,10},{9,11},{10,... | collective-permute-start | bytes 4718600 | tf_op jit(solution)/shard_map/ppermute | solution.py:553
  57.5 267.0 %all-gather.11.cloned.1.call-start = ((), (), s32[]{:S(2)}) async-start(), calls=%async_computation.6 | async-start | bytes 5308416 | tf_op jit(solution)/shard_map/all_gather | solution.py:758
  57.6 47.3 %collective-permute-start.6 = (bf16[512,1536]{1,0:T(8,128)(2,1)}, bf16[512,1536]{1,0:T(8,128)(2,1)}, u32[]{:S(2)}, u32[]{:S(2)}) collective-permute-start(bf16[512,1536]{1,0:T(8,128)(2,1)} %multiply_convert_fusion), channel_id=1, source_target_pairs={{0,1},{1,0},{2,3},{3,2},{4,5},{5,4},{6,7},{7,6},{8,9},{9,8},{10,11... | collective-permute-start | bytes 4718600 | tf_op jit(solution)/shard_map/ppermute | solution.py:553
  111.3 37.2 %collective-permute-start.8 = (bf16[512,1536]{1,0:T(8,128)(2,1)}, bf16[512,1536]{1,0:T(8,128)(2,1)}, u32[]{:S(2)}, u32[]{:S(2)}) collective-permute-start(bf16[512,1536]{1,0:T(8,128)(2,1)} %convert_element_type.235), channel_id=1, source_target_pairs={{0,2},{1,3},{2,0},{3,1},{4,6},{5,7},{6,4},{7,5},{8,10},{9,11},{10,... | collective-permute-start | bytes 4718600 | tf_op jit(solution)/shard_map/ppermute | solution.py:553
  111.7 39.6 %collective-permute-start.9 = (bf16[512,1536]{1,0:T(8,128)(2,1)}, bf16[512,1536]{1,0:T(8,128)(2,1)}, u32[]{:S(2)}, u32[]{:S(2)}) collective-permute-start(bf16[512,1536]{1,0:T(8,128)(2,1)} %convert_element_type.235), channel_id=1, source_target_pairs={{0,1},{1,0},{2,3},{3,2},{4,5},{5,4},{6,7},{7,6},{8,9},{9,8},{10,11... | collective-permute-start | bytes 4718600 | tf_op jit(solution)/shard_map/ppermute | solution.py:553
  149.4 357.9 %reduce-scatter.4.cloned.1.call-start = ((), (), s32[]{:S(2)}) async-start(), calls=%async_computation.7 | async-start | bytes 2654208 | tf_op jit(solution)/shard_map/reduce_scatter | solution.py:871
  179.8 24.8 %collective-permute-start.11 = (bf16[512,1536]{1,0:T(8,128)(2,1)}, bf16[512,1536]{1,0:T(8,128)(2,1)}, u32[]{:S(2)}, u32[]{:S(2)}) collective-permute-start(bf16[512,1536]{1,0:T(8,128)(2,1)} %get-tuple-element.130), channel_id=1, source_target_pairs={{0,1},{1,0},{2,3},{3,2},{4,5},{5,4},{6,7},{7,6},{8,9},{9,8},{10,11... | collective-permute-start | bytes 4718600 | tf_op jit(solution)/shard_map/ppermute | solution.py:553
  191.8 15.4 %collective-permute-start.12 = (bf16[512,1536]{1,0:T(8,128)(2,1)}, bf16[512,1536]{1,0:T(8,128)(2,1)}, u32[]{:S(2)}, u32[]{:S(2)}) collective-permute-start(bf16[512,1536]{1,0:T(8,128)(2,1)} %get-tuple-element.133), channel_id=1, source_target_pairs={{0,1},{1,0},{2,3},{3,2},{4,5},{5,4},{6,7},{7,6},{8,9},{9,8},{10,11... | collective-permute-start | bytes 4718600 | tf_op jit(solution)/shard_map/ppermute | solution.py:553
  212.8 20.8 %collective-permute-start.15 = (bf16[256,1536]{1,0:T(8,128)(2,1)}, bf16[256,1536]{1,0:T(8,128)(2,1)}, u32[]{:S(2)}, u32[]{:S(2)}) collective-permute-start(bf16[256,1536]{1,0:T(8,128)(2,1)} %slice.652), channel_id=1, source_target_pairs={{0,2},{1,3},{2,0},{3,1},{4,6},{5,7},{6,4},{7,5},{8,10},{9,11},{10,... | collective-permute-start | bytes 2359304 | tf_op jit(solution)/shard_map/ppermute | solution.py:553
  215.8 34.5 %collective-permute-start.16 = (bf16[256,1536]{1,0:T(8,128)(2,1)S(1)}, bf16[256,1536]{1,0:T(8,128)(2,1)S(1)}, u32[]{:S(2)}, u32[]{:S(2)}) collective-permute-start(bf16[256,1536]{1,0:T(8,128)(2,1)S(1)} %slice.651), channel_id=1, source_target_pairs={{0,2},{1,3},{2,0},{3,1},{4,6},{5,7},{6,4},{7,5},{8,10},{9,11},{10,... | collective-permute-start | bytes 2359304 | tf_op jit(solution)/shard_map/ppermute | solution.py:553
  237.1 28.7 %collective-permute-start.17 = (bf16[256,1536]{1,0:T(8,128)(2,1)}, bf16[256,1536]{1,0:T(8,128)(2,1)S(1)}, u32[]{:S(2)}, u32[]{:S(2)}) collective-permute-start(bf16[256,1536]{1,0:T(8,128)(2,1)} %multiply_convert_fusion.2), channel_id=1, source_target_pairs={{0,2},{1,3},{2,0},{3,1},{4,6},{5,7},{6,4},{7,5},{8,10},{9,11},{10,... | collective-permute-start | bytes 2359304 | tf_op jit(solution)/shard_map/ppermute | solution.py:553
  266.7 18.2 %collective-permute-start.18 = (bf16[256,1536]{1,0:T(8,128)(2,1)S(1)}, bf16[256,1536]{1,0:T(8,128)(2,1)S(1)}, u32[]{:S(2)}, u32[]{:S(2)}) collective-permute-start(bf16[256,1536]{1,0:T(8,128)(2,1)S(1)} %get-tuple-element.142), channel_id=1, source_target_pairs={{0,2},{1,3},{2,0},{3,1},{4,6},{5,7},{6,4},{7,5},{8,10},{9,11},{10,... | collective-permute-start | bytes 2359304 | tf_op jit(solution)/shard_map/ppermute | solution.py:553
  268.2 17.7 %collective-permute-start.19 = (bf16[256,1536]{1,0:T(8,128)(2,1)}, bf16[256,1536]{1,0:T(8,128)(2,1)S(1)}, u32[]{:S(2)}, u32[]{:S(2)}) collective-permute-start(bf16[256,1536]{1,0:T(8,128)(2,1)} %multiply_convert_fusion.2), channel_id=1, source_target_pairs={{0,1},{1,0},{2,3},{3,2},{4,5},{5,4},{6,7},{7,6},{8,9},{9,8},{10,11... | collective-permute-start | bytes 2359304 | tf_op jit(solution)/shard_map/ppermute | solution.py:553
  269.8 17.0 %collective-permute-start.20 = (bf16[256,1536]{1,0:T(8,128)(2,1)S(1)}, bf16[256,1536]{1,0:T(8,128)(2,1)S(1)}, u32[]{:S(2)}, u32[]{:S(2)}) collective-permute-start(bf16[256,1536]{1,0:T(8,128)(2,1)S(1)} %get-tuple-element.142), channel_id=1, source_target_pairs={{0,1},{1,0},{2,3},{3,2},{4,5},{5,4},{6,7},{7,6},{8,9},{9,8},{10,11... | collective-permute-start | bytes 2359304 | tf_op jit(solution)/shard_map/ppermute | solution.py:553
  271.0 16.8 %collective-permute-start.21 = (bf16[256,1536]{1,0:T(8,128)(2,1)}, bf16[256,1536]{1,0:T(8,128)(2,1)S(1)}, u32[]{:S(2)}, u32[]{:S(2)}) collective-permute-start(bf16[256,1536]{1,0:T(8,128)(2,1)} %copy-done.34), channel_id=1, source_target_pairs={{0,1},{1,0},{2,3},{3,2},{4,5},{5,4},{6,7},{7,6},{8,9},{9,8},{10,11... | collective-permute-start | bytes 2359304 | tf_op jit(solution)/shard_map/ppermute | solution.py:553
  336.5 29.5 %collective-permute-start.23 = (bf16[512,1536]{1,0:T(8,128)(2,1)}, bf16[512,1536]{1,0:T(8,128)(2,1)S(1)}, u32[]{:S(2)}, u32[]{:S(2)}) collective-permute-start(bf16[512,1536]{1,0:T(8,128)(2,1)} %get-tuple-element.145), channel_id=1, source_target_pairs={{0,1},{1,0},{2,3},{3,2},{4,5},{5,4},{6,7},{7,6},{8,9},{9,8},{10,11... | collective-permute-start | bytes 4718600 | tf_op jit(solution)/shard_map/ppermute | solution.py:553
  348.9 17.6 %collective-permute-start.24 = (bf16[512,1536]{1,0:T(8,128)(2,1)}, bf16[512,1536]{1,0:T(8,128)(2,1)}, u32[]{:S(2)}, u32[]{:S(2)}) collective-permute-start(bf16[512,1536]{1,0:T(8,128)(2,1)} %get-tuple-element.148), channel_id=1, source_target_pairs={{0,1},{1,0},{2,3},{3,2},{4,5},{5,4},{6,7},{7,6},{8,9},{9,8},{10,11... | collective-permute-start | bytes 4718600 | tf_op jit(solution)/shard_map/ppermute | solution.py:553
  369.6 20.5 %collective-permute-start.28 = (bf16[256,1536]{1,0:T(8,128)(2,1)S(1)}, bf16[256,1536]{1,0:T(8,128)(2,1)S(1)}, u32[]{:S(2)}, u32[]{:S(2)}) collective-permute-start(bf16[256,1536]{1,0:T(8,128)(2,1)S(1)} %slice.649), channel_id=1, source_target_pairs={{0,2},{1,3},{2,0},{3,1},{4,6},{5,7},{6,4},{7,5},{8,10},{9,11},{10,... | collective-permute-start | bytes 2359304 | tf_op jit(solution)/shard_map/ppermute | solution.py:553
  371.3 33.5 %collective-permute-start.27 = (bf16[256,1536]{1,0:T(8,128)(2,1)S(1)}, bf16[256,1536]{1,0:T(8,128)(2,1)S(1)}, u32[]{:S(2)}, u32[]{:S(2)}) collective-permute-start(bf16[256,1536]{1,0:T(8,128)(2,1)S(1)} %slice.650), channel_id=1, source_target_pairs={{0,2},{1,3},{2,0},{3,1},{4,6},{5,7},{6,4},{7,5},{8,10},{9,11},{10,... | collective-permute-start | bytes 2359304 | tf_op jit(solution)/shard_map/ppermute | solution.py:553
  439.9 211.6 %reduce-scatter.6.cloned.1.call-start = ((), (), s32[]{:S(2)}) async-start(), calls=%async_computation.8 | async-start | bytes 6635520 | tf_op jit(solution)/shard_map/reduce_scatter | solution.py:871
  520.5 19.9 %collective-permute-start.35 = (bf16[256,1536]{1,0:T(8,128)(2,1)}, bf16[256,1536]{1,0:T(8,128)(2,1)}, u32[]{:S(2)}, u32[]{:S(2)}) collective-permute-start(bf16[256,1536]{1,0:T(8,128)(2,1)} %slice.647), channel_id=1, source_target_pairs={{0,2},{1,3},{2,0},{3,1},{4,6},{5,7},{6,4},{7,5},{8,10},{9,11},{10,... | collective-permute-start | bytes 2359304 | tf_op jit(solution)/shard_map/ppermute | solution.py:553
  540.5 183.9 %reduce-scatter.8.cloned.1.call-start = ((), (), s32[]{:S(2)}) async-start(), calls=%async_computation.9 | async-start | bytes 2654208 | tf_op jit(solution)/shard_map/reduce_scatter | solution.py:871
  542.0 18.8 %collective-permute-start.33 = (bf16[256,1536]{1,0:T(8,128)(2,1)S(1)}, bf16[256,1536]{1,0:T(8,128)(2,1)S(1)}, u32[]{:S(2)}, u32[]{:S(2)}) collective-permute-start(bf16[256,1536]{1,0:T(8,128)(2,1)S(1)} %slice.648), channel_id=1, source_target_pairs={{0,2},{1,3},{2,0},{3,1},{4,6},{5,7},{6,4},{7,5},{8,10},{9,11},{10,... | collective-permute-start | bytes 2359304 | tf_op jit(solution)/shard_map/ppermute | solution.py:553
  567.2 18.3 %collective-permute-start.36 = (bf16[256,1536]{1,0:T(8,128)(2,1)}, bf16[256,1536]{1,0:T(8,128)(2,1)S(1)}, u32[]{:S(2)}, u32[]{:S(2)}) collective-permute-start(bf16[256,1536]{1,0:T(8,128)(2,1)} %get-tuple-element.169), channel_id=1, source_target_pairs={{0,2},{1,3},{2,0},{3,1},{4,6},{5,7},{6,4},{7,5},{8,10},{9,11},{10,... | collective-permute-start | bytes 2359304 | tf_op jit(solution)/shard_map/ppermute | solution.py:553
  568.8 34.8 %collective-permute-start.38 = (bf16[256,1536]{1,0:T(8,128)(2,1)}, bf16[256,1536]{1,0:T(8,128)(2,1)}, u32[]{:S(2)}, u32[]{:S(2)}) collective-permute-start(bf16[256,1536]{1,0:T(8,128)(2,1)} %get-tuple-element.169), channel_id=1, source_target_pairs={{0,1},{1,0},{2,3},{3,2},{4,5},{5,4},{6,7},{7,6},{8,9},{9,8},{10,11... | collective-permute-start | bytes 2359304 | tf_op jit(solution)/shard_map/ppermute | solution.py:553
  573.7 13.3 %collective-permute-start.42 = (f32[512,2]{0,1:T(2,128)S(1)}, f32[512,2]{0,1:T(2,128)S(1)}, u32[]{:S(2)}, u32[]{:S(2)}) collective-permute-start(f32[512,2]{0,1:T(2,128)S(1)} %maximum_maximum_fusion.1), channel_id=1, source_target_pairs={{0,2},{1,3},{2,0},{3,1},{4,6},{5,7},{6,4},{7,5},{8,10},{9,11},{10,... | collective-permute-start | bytes 12296 | tf_op jit(solution)/shard_map/ppermute | solution.py:553
  585.5 17.1 %collective-permute-start.37 = (bf16[256,1536]{1,0:T(8,128)(2,1)S(1)}, bf16[256,1536]{1,0:T(8,128)(2,1)S(1)}, u32[]{:S(2)}, u32[]{:S(2)}) collective-permute-start(bf16[256,1536]{1,0:T(8,128)(2,1)S(1)} %get-tuple-element.172), channel_id=1, source_target_pairs={{0,2},{1,3},{2,0},{3,1},{4,6},{5,7},{6,4},{7,5},{8,10},{9,11},{10,... | collective-permute-start | bytes 2359304 | tf_op jit(solution)/shard_map/ppermute | solution.py:553
  587.1 18.5 %collective-permute-start.39 = (bf16[256,1536]{1,0:T(8,128)(2,1)S(1)}, bf16[256,1536]{1,0:T(8,128)(2,1)S(1)}, u32[]{:S(2)}, u32[]{:S(2)}) collective-permute-start(bf16[256,1536]{1,0:T(8,128)(2,1)S(1)} %get-tuple-element.172), channel_id=1, source_target_pairs={{0,1},{1,0},{2,3},{3,2},{4,5},{5,4},{6,7},{7,6},{8,9},{9,8},{10,11... | collective-permute-start | bytes 2359304 | tf_op jit(solution)/shard_map/ppermute | solution.py:553
  589.6 17.0 %collective-permute-start.40 = (bf16[256,1536]{1,0:T(8,128)(2,1)S(1)}, bf16[256,1536]{1,0:T(8,128)(2,1)S(1)}, u32[]{:S(2)}, u32[]{:S(2)}) collective-permute-start(bf16[256,1536]{1,0:T(8,128)(2,1)S(1)} %collective-permute-done.36), channel_id=1, source_target_pairs={{0,1},{1,0},{2,3},{3,2},{4,5},{5,4},{6,7},{7,6},{8,9},{9,8},{10,11... | collective-permute-start | bytes 2359304 | tf_op jit(solution)/shard_map/ppermute | solution.py:553
  726.6 18.7 %collective-permute-start.46 = (bf16[512,1536]{1,0:T(8,128)(2,1)S(1)}, bf16[512,1536]{1,0:T(8,128)(2,1)S(1)}, u32[]{:S(2)}, u32[]{:S(2)}) collective-permute-start(bf16[512,1536]{1,0:T(8,128)(2,1)S(1)} %get-tuple-element.424), channel_id=1, source_target_pairs={{0,1},{1,0},{2,3},{3,2},{4,5},{5,4},{6,7},{7,6},{8,9},{9,8},{10,11... | collective-permute-start | bytes 4718600 | tf_op jit(solution)/shard_map/ppermute | solution.py:553
  726.7 18.6 %collective-permute-start.45 = (bf16[512,1536]{1,0:T(8,128)(2,1)S(1)}, bf16[512,1536]{1,0:T(8,128)(2,1)S(1)}, u32[]{:S(2)}, u32[]{:S(2)}) collective-permute-start(bf16[512,1536]{1,0:T(8,128)(2,1)S(1)} %get-tuple-element.425), channel_id=1, source_target_pairs={{0,1},{1,0},{2,3},{3,2},{4,5},{5,4},{6,7},{7,6},{8,9},{9,8},{10,11... | collective-permute-start | bytes 4718600 | tf_op jit(solution)/shard_map/ppermute | solution.py:553
  752.6 18.9 %collective-permute-start.50 = (bf16[192,1920]{1,0:T(8,128)(2,1)}, bf16[192,1920]{1,0:T(8,128)(2,1)}, u32[]{:S(2)}, u32[]{:S(2)}) collective-permute-start(bf16[192,1920]{1,0:T(8,128)(2,1)} %get-tuple-element.420), channel_id=1, source_target_pairs={{0,8},{8,16},{16,24},{24,28},{28,20},{20,12},{12,4},{4,0},{1,9},{9... | collective-permute-start | bytes 2211848 | tf_op jit(solution)/shard_map/ppermute | solution.py:611
  753.5 18.6 %collective-permute-start.49 = (bf16[192,1920]{1,0:T(8,128)(2,1)}, bf16[192,1920]{1,0:T(8,128)(2,1)}, u32[]{:S(2)}, u32[]{:S(2)}) collective-permute-start(bf16[192,1920]{1,0:T(8,128)(2,1)} %get-tuple-element.421), channel_id=1, source_target_pairs={{0,4},{8,0},{16,8},{24,16},{28,24},{20,28},{12,20},{4,12},{1,5},{9... | collective-permute-start | bytes 2211848 | tf_op jit(solution)/shard_map/ppermute | solution.py:611
  760.8 38.7 %collective-permute-start.47 = (bf16[256,1536]{1,0:T(8,128)(2,1)}, bf16[256,1536]{1,0:T(8,128)(2,1)}, u32[]{:S(2)}, u32[]{:S(2)}) collective-permute-start(bf16[256,1536]{1,0:T(8,128)(2,1)} %slice.646), channel_id=1, source_target_pairs={{0,2},{1,3},{2,0},{3,1},{4,6},{5,7},{6,4},{7,5},{8,10},{9,11},{10,... | collective-permute-start | bytes 2359304 | tf_op jit(solution)/shard_map/ppermute | solution.py:553
  763.3 36.2 %collective-permute-start.48 = (bf16[256,1536]{1,0:T(8,128)(2,1)}, bf16[256,1536]{1,0:T(8,128)(2,1)}, u32[]{:S(2)}, u32[]{:S(2)}) collective-permute-start(bf16[256,1536]{1,0:T(8,128)(2,1)} %slice.645), channel_id=1, source_target_pairs={{0,2},{1,3},{2,0},{3,1},{4,6},{5,7},{6,4},{7,5},{8,10},{9,11},{10,... | collective-permute-start | bytes 2359304 | tf_op jit(solution)/shard_map/ppermute | solution.py:553
  777.1 38.3 %collective-permute-start.51 = (bf16[192,1920]{1,0:T(8,128)(2,1)}, bf16[192,1920]{1,0:T(8,128)(2,1)}, u32[]{:S(2)}, u32[]{:S(2)}) collective-permute-start(bf16[192,1920]{1,0:T(8,128)(2,1)} %get-tuple-element.195), channel_id=1, source_target_pairs={{0,8},{8,16},{16,24},{24,28},{28,20},{20,12},{12,4},{4,0},{1,9},{9... | collective-permute-start | bytes 2211848 | tf_op jit(solution)/shard_map/ppermute | solution.py:611
  778.2 60.2 %collective-permute-start.54 = (bf16[192,1920]{1,0:T(8,128)(2,1)}, bf16[192,1920]{1,0:T(8,128)(2,1)}, u32[]{:S(2)}, u32[]{:S(2)}) collective-permute-start(bf16[192,1920]{1,0:T(8,128)(2,1)} %get-tuple-element.196), channel_id=1, source_target_pairs={{0,4},{8,0},{16,8},{24,16},{28,24},{20,28},{12,20},{4,12},{1,5},{9... | collective-permute-start | bytes 2211848 | tf_op jit(solution)/shard_map/ppermute | solution.py:611
  798.8 19.3 %collective-permute-start.62 = (f32[2,5924]{1,0:T(2,128)}, f32[2,5924]{1,0:T(2,128)}, u32[]{:S(2)}, u32[]{:S(2)}) collective-permute-start(f32[2,5924]{1,0:T(2,128)} %pad_maximum_fusion.12), channel_id=1, source_target_pairs={{0,4},{4,0},{8,12},{12,8},{16,20},{20,16},{24,28},{28,24},{1,5},{5... | collective-permute-start | bytes 142184 | tf_op jit(solution)/shard_map/ppermute | solution.py:645
  817.1 21.2 %collective-permute-start.52 = (bf16[192,1920]{1,0:T(8,128)(2,1)S(1)}, bf16[192,1920]{1,0:T(8,128)(2,1)S(1)}, u32[]{:S(2)}, u32[]{:S(2)}) collective-permute-start(bf16[192,1920]{1,0:T(8,128)(2,1)S(1)} %add_convert_fusion.2), channel_id=1, source_target_pairs={{0,8},{8,16},{16,24},{24,28},{28,20},{20,12},{12,4},{4,0},{1,9},{9... | collective-permute-start | bytes 2211848 | tf_op jit(solution)/shard_map/ppermute | solution.py:611
  819.0 17.8 %collective-permute-start.63 = (f32[2,5924]{1,0:T(2,128)S(1)}, f32[2,5924]{1,0:T(2,128)S(1)}, u32[]{:S(2)}, u32[]{:S(2)}) collective-permute-start(f32[2,5924]{1,0:T(2,128)S(1)} %fusion.31), channel_id=1, source_target_pairs={{0,8},{4,12},{8,0},{12,4},{16,24},{20,28},{24,16},{28,20},{1,9},{5... | collective-permute-start | bytes 142184 | tf_op jit(solution)/shard_map/ppermute | solution.py:645
  820.1 15.0 %collective-permute-start.68 = (f32[2,1536]{1,0:T(2,128)S(1)}, f32[2,1536]{1,0:T(2,128)S(1)}, u32[]{:S(2)}, u32[]{:S(2)}) collective-permute-start(f32[2,1536]{1,0:T(2,128)S(1)} %add.608), channel_id=1, source_target_pairs={{0,8},{4,12},{8,0},{12,4},{16,24},{20,28},{24,16},{28,20},{1,9},{5... | collective-permute-start | bytes 36872 | tf_op jit(solution)/shard_map/ppermute | solution.py:645
  840.7 17.6 %collective-permute-start.55 = (bf16[192,1920]{1,0:T(8,128)(2,1)S(1)}, bf16[192,1920]{1,0:T(8,128)(2,1)S(1)}, u32[]{:S(2)}, u32[]{:S(2)}) collective-permute-start(bf16[192,1920]{1,0:T(8,128)(2,1)S(1)} %get-tuple-element.417), channel_id=1, source_target_pairs={{0,4},{8,0},{16,8},{24,16},{28,24},{20,28},{12,20},{4,12},{1,5},{9... | collective-permute-start | bytes 2211848 | tf_op jit(solution)/shard_map/ppermute | solution.py:611
  843.1 16.8 %collective-permute-start.53 = (bf16[192,1920]{1,0:T(8,128)(2,1)S(1)}, bf16[192,1920]{1,0:T(8,128)(2,1)S(1)}, u32[]{:S(2)}, u32[]{:S(2)}) collective-permute-start(bf16[192,1920]{1,0:T(8,128)(2,1)S(1)} %get-tuple-element.416), channel_id=1, source_target_pairs={{0,8},{8,16},{16,24},{24,28},{28,20},{20,12},{12,4},{4,0},{1,9},{9... | collective-permute-start | bytes 2211848 | tf_op jit(solution)/shard_map/ppermute | solution.py:611
  865.6 13.8 %collective-permute-start.58 = (f32[96,256]{1,0:T(8,128)}, f32[96,256]{1,0:T(8,128)}, u32[]{:S(2)}, u32[]{:S(2)}) collective-permute-start(f32[96,256]{1,0:T(8,128)} %pad_maximum_fusion.10), channel_id=1, source_target_pairs={{0,1},{1,0},{2,3},{3,2},{4,5},{5,4},{6,7},{7,6},{8,9},{9,8},{10,11... | collective-permute-start | bytes 294920 | tf_op jit(solution)/shard_map/ppermute | solution.py:553
  866.2 14.7 %collective-permute-start.56 = (f32[96,256]{1,0:T(8,128)}, f32[96,256]{1,0:T(8,128)}, u32[]{:S(2)}, u32[]{:S(2)}) collective-permute-start(f32[96,256]{1,0:T(8,128)} %pad_maximum_fusion.9), channel_id=1, source_target_pairs={{0,1},{1,0},{2,3},{3,2},{4,5},{5,4},{6,7},{7,6},{8,9},{9,8},{10,11... | collective-permute-start | bytes 294920 | tf_op jit(solution)/shard_map/ppermute | solution.py:553
  (130 other events, 1254.1 us)
Sparse Core Ops, SparseCore 0:
  20.0 66.7 all-gather.4
  89.6 78.3 all-gather.6
  170.2 63.3 all-gather.8
  235.6 78.3 all-gather.10
  440.1 67.1 reduce-scatter.3
  540.6 110.8 reduce-scatter.5
  655.6 68.7 reduce-scatter.7

commit v3 on v2

--- a/solution.py
+++ b/solution.py
@@ -906,10 +906,13 @@
         far_list = [swap_far(near, tensor_count, LOW) for near in near_list]
         if layer == 0:
             ring = RingReduce(merged_grad, dp_count)
-            ring.hop()
-            rest = (conv_grad, head_grad, skip_grad, gain_five, out_sum, late)
+            for hop in range(1, ring.total_hops):
+                ring.hop()
+                if hop == 2:
+                    ring.moving, far_list = lax.optimization_barrier((ring.moving, far_list))
+            rest = (conv_grad, head_grad, skip_grad, gain_five, out_sum, late, far_list)
             ring.moving, rest = lax.optimization_barrier((ring.moving, rest))
-            conv_grad, head_grad, skip_grad, gain_five, out_sum, late = rest
+            conv_grad, head_grad, skip_grad, gain_five, out_sum, late, far_list = rest
             if layer + 1 < layer_total:
                 place_scan(layer + 1, late.astype(F32))
             place_scan(layer, ring.finish())

time: 903 us -> 936 us (1.037)
  waiting for transfers between devices: 257 us -> 286 us
    ppermute x7, waiting for transfers between devices: 20.5 us -> 38.7 us  [ring_step(): return lax.ppermute(vals, 'dp', pairs)]
    ppermute x48, waiting for transfers between devices: 176 us -> 194 us  [swap(): lax.ppermute(vals, 'tensor', [(src, src ^ distance) for src in range(coun...]
    unnamed x231 -> x249, local copies, waits for them, and re-layouts: 31.9 us -> 33.8 us
  transfers between devices with their start and end apart: 77 -> 77, of which waited for: 38 -> 45; matrix products, arithmetic and copies ran while one was open for 25% -> 23% of each run, Pallas kernels for 28% -> 27%
where the time goes in v3:
time: 936 us; the launch traced here: 927 us
  waiting for transfers between devices  286 us (31%)
  Pallas kernels  283 us (30%)
  other arithmetic  120 us (13%)
  local copies, waits for them, and re-layouts  107 us (11%)
  starting transfers between devices  55.7 us (6%)
  matrix products  52.4 us (6%)
  between operations  16.2 us (2%)
    ppermute x48, waiting for transfers between devices, swap(): lax.ppermute(vals, 'tensor', [(src, src ^ distance) for src in range(coun...  194 us
    pallas_call x2, Pallas kernels, scan_backward(): pl.pallas_call(scan_back_kernel, out_shape=(jax.ShapeDtypeStruct((total,...  127 us
    pallas_call x2, Pallas kernels, scan_forward(): pl.pallas_call(scan_kernel, out_shape=(jax.ShapeDtypeStruct((total, pre_w...  70 us
    dot_general x4, matrix products, dot(): lax.dot_general(left, right, (((left_dim,), (right_dim,)), ((), ())), pre...  52.4 us
    pallas_call x4, Pallas kernels, gate_forward(): pl.pallas_call(gate_kernel, out_shape=(jax.ShapeDtypeStruct((total, width...  47.5 us
    ppermute x7, waiting for transfers between devices, ring_step(): return lax.ppermute(vals, 'dp', pairs)  38.7 us
    pallas_call x2, Pallas kernels, gate_backward(): pl.pallas_call(gate_back_kernel, out_shape=(jax.ShapeDtypeStruct((total,...  34.8 us
    unnamed x249, local copies, waits for them, and re-layouts  33.8 us
  transfers between devices with their start and end apart: 77, of which 45 were waited for; matrix products, arithmetic and copies ran while one was open for 23% of the time, Pallas kernels for 27%

profile of v3, /device:TPU:0, one launch (start us, length us, event | category | flops | bytes accessed | tf_op | source)
XLA Modules:
  0.0 927.2 jit_solution(15240389164417720804)
XLA Ops:
  8.1 6.8 all_gather.15
  22.0 3.0 first_root.1
  45.6 3.2 concatenate.137
  57.6 34.4 %collective-permute-done.5 = bf16[512,1536]{1,0:T(8,128)(2,1)} collective-permute-done((bf16[512,1536]{1,0:T(8,128)(2,1)}, bf16[512,1536]{1,0:T(8,128)(2,1)}, u32[]{:S(2)}, u32[]{:S(2)}) %collective-permute-start.5) | collective-permute-done | bytes 1572896 | tf_op jit(solution)/shard_map/ppermute | solution.py:553
  93.5 3.3 convert_element_type.235
  104.9 6.3 pad_maximum_fusion.rows_ref
  111.9 35.1 %scan_forward.2 = (f32[2048,1152]{1,0:T(8,128)}, f32[2048,768]{1,0:T(8,128)}, f32[8,128,768]{2,1,0:T(8,128)}) custom-call(s32[1]{0:T(128)} %bitcast.5.me_ref, bf16[2048,1536]{1,0:T(8,128)(2,1)} %pad_maximum_fusion.rows_ref, bf16[1536,1152]{1,0:T(8,128)(2,1)} %all-gather.5.cloned.1.call-done.weight_ref, f32[8,1024]{1,0:T(8,128)} %select_maximum_fusion.1.conv_ref, ...), custom_call_target="tpu_custom_call" | custom-call | flops 28991029248 | bytes 1572864 | tf_op jit(solution)/shard_map/scan_forward/pallas_call | solution.py:341
  152.2 6.5 pad_maximum_fusion.1.grad_ref
  158.7 9.3 %all-gather.7.cloned.1.call-done.z_weight_ref.out_weight_ref = bf16[1536,1536]{1,0:T(8,128)(2,1)} async-done(((bf16[192,1536]{1,0:T(8,128)(2,1)}), bf16[1536,1536]{1,0:T(8,128)(2,1)}) %all-gather.7.cloned.1.call-update) | async-done | bytes 4718608 | tf_op jit(solution)/shard_map/all_gather | solution.py:758
  168.0 11.8 %gate_forward.4 = (f32[2048,768]{1,0:T(8,128)}, bf16[512,1536]{1,0:T(8,128)(2,1)}, bf16[512,1536]{1,0:T(8,128)(2,1)}, f32[1024,1]{1,0:T(8,128)}) custom-call(bf16[2048,1536]{1,0:T(8,128)(2,1)} %pad_maximum_fusion.rows_ref, f32[2048,768]{1,0:T(8,128)} %get-tuple-element.134.y_ref, bf16[1536,1536]{1,0:T(8,128)(2,1)} %all-gather.7.cloned.1.call-done.z_weight_ref.out_weight_ref, ...), custom_call_target="tpu_custom_call" | custom-call | flops 19327352832 | bytes 12582912 | tf_op jit(solution)/shard_map/gate_forward/pallas_call | solution.py:392
  179.9 11.9 %gate_forward.5 = (f32[2048,768]{1,0:T(8,128)}, bf16[512,1536]{1,0:T(8,128)(2,1)}, bf16[512,1536]{1,0:T(8,128)(2,1)}, f32[1024,1]{1,0:T(8,128)}) custom-call(bf16[2048,1536]{1,0:T(8,128)(2,1)} %pad_maximum_fusion.rows_ref, f32[2048,768]{1,0:T(8,128)} %get-tuple-element.134.y_ref, ...), custom_call_target="tpu_custom_call", output_to_operand_aliasing={{0}: (5, {})} | custom-call | flops 19327352832 | bytes 12582912 | tf_op jit(solution)/shard_map/gate_forward/pallas_call | solution.py:392
  207.2 4.7 convert_add_fusion.6
  216.5 17.1 %collective-permute-done.15 = bf16[256,1536]{1,0:T(8,128)(2,1)} collective-permute-done((bf16[256,1536]{1,0:T(8,128)(2,1)}, bf16[256,1536]{1,0:T(8,128)(2,1)}, u32[]{:S(2)}, u32[]{:S(2)}) %collective-permute-start.15) | collective-permute-done | bytes 786464 | tf_op jit(solution)/shard_map/ppermute | solution.py:553
  238.6 11.8 %collective-permute-done.16 = bf16[256,1536]{1,0:T(8,128)(2,1)S(1)} collective-permute-done((bf16[256,1536]{1,0:T(8,128)(2,1)S(1)}, bf16[256,1536]{1,0:T(8,128)(2,1)S(1)}, u32[]{:S(2)}, u32[]{:S(2)}) %collective-permute-start.16) | collective-permute-done | bytes 786464 | tf_op jit(solution)/shard_map/ppermute | solution.py:553
  255.1 10.7 %collective-permute-done.17 = bf16[256,1536]{1,0:T(8,128)(2,1)S(1)} collective-permute-done((bf16[256,1536]{1,0:T(8,128)(2,1)}, bf16[256,1536]{1,0:T(8,128)(2,1)S(1)}, u32[]{:S(2)}, u32[]{:S(2)}) %collective-permute-start.17) | collective-permute-done | bytes 786464 | tf_op jit(solution)/shard_map/ppermute | solution.py:553
  273.1 11.8 %collective-permute-done.18 = bf16[256,1536]{1,0:T(8,128)(2,1)S(1)} collective-permute-done((bf16[256,1536]{1,0:T(8,128)(2,1)S(1)}, bf16[256,1536]{1,0:T(8,128)(2,1)S(1)}, u32[]{:S(2)}, u32[]{:S(2)}) %collective-permute-start.18) | collective-permute-done | bytes 786464 | tf_op jit(solution)/shard_map/ppermute | solution.py:553
  289.6 34.9 %scan_forward.3 = (f32[2048,1152]{1,0:T(8,128)}, f32[2048,768]{1,0:T(8,128)}, f32[8,128,768]{2,1,0:T(8,128)}) custom-call(s32[1]{0:T(128)} %bitcast.5.me_ref, bf16[2048,1536]{1,0:T(8,128)(2,1)} %constant_dynamic-update-slice_fusion.rows_ref, bf16[1536,1152]{1,0:T(8,128)(2,1)} %all-gather.9.cloned.1.call-done.weight_ref, ...), custom_call_target="tpu_custom_call" | custom-call | flops 362387872 | bytes 1572864 | tf_op jit(solution)/shard_map/scan_forward/pallas_call | solution.py:341
  324.5 12.0 %gate_forward.6 = (f32[2048,768]{1,0:T(8,128)}, bf16[512,1536]{1,0:T(8,128)(2,1)}, bf16[512,1536]{1,0:T(8,128)(2,1)}, f32[1024,1]{1,0:T(8,128)}) custom-call(bf16[2048,1536]{1,0:T(8,128)(2,1)} %constant_dynamic-update-slice_fusion.rows_ref, f32[2048,768]{1,0:T(8,128)} %get-tuple-element.149.y_ref, ...), custom_call_target="tpu_custom_call" | custom-call | flops 19327352832 | bytes 12582912 | tf_op jit(solution)/shard_map/gate_forward/pallas_call | solution.py:392
  337.1 11.8 %gate_forward.7 = (f32[2048,768]{1,0:T(8,128)}, bf16[512,1536]{1,0:T(8,128)(2,1)}, bf16[512,1536]{1,0:T(8,128)(2,1)}, f32[1024,1]{1,0:T(8,128)}) custom-call(bf16[2048,1536]{1,0:T(8,128)(2,1)} %constant_dynamic-update-slice_fusion.rows_ref, f32[2048,768]{1,0:T(8,128)} %get-tuple-element.149.y_ref, ...), custom_call_target="tpu_custom_call", output_to_operand_aliasing={{0}: (5, {})} | custom-call | flops 19327352832 | bytes 12582912 | tf_op jit(solution)/shard_map/gate_forward/pallas_call | solution.py:392
  371.8 18.3 %collective-permute-done.28 = bf16[256,1536]{1,0:T(8,128)(2,1)S(1)} collective-permute-done((bf16[256,1536]{1,0:T(8,128)(2,1)S(1)}, bf16[256,1536]{1,0:T(8,128)(2,1)S(1)}, u32[]{:S(2)}, u32[]{:S(2)}) %collective-permute-start.28) | collective-permute-done | bytes 786464 | tf_op jit(solution)/shard_map/ppermute | solution.py:553
  390.1 14.7 %collective-permute-done.27 = bf16[256,1536]{1,0:T(8,128)(2,1)S(1)} collective-permute-done((bf16[256,1536]{1,0:T(8,128)(2,1)S(1)}, bf16[256,1536]{1,0:T(8,128)(2,1)S(1)}, u32[]{:S(2)}, u32[]{:S(2)}) %collective-permute-start.27) | collective-permute-done | bytes 786464 | tf_op jit(solution)/shard_map/ppermute | solution.py:553
  413.3 17.3 %gate_backward.2 = (bf16[2048,768]{1,0:T(8,128)(2,1)}, f32[2048,768]{1,0:T(8,128)}, bf16[2048,768]{1,0:T(8,128)(2,1)}, f32[1,768]{1,0:T(1,128)}) custom-call(bf16[2048,1536]{1,0:T(8,128)(2,1)} %pad_maximum_fusion.1.grad_ref, f32[2048,768]{1,0:T(8,128)} %get-tuple-element.149.y_ref, f32[2048,768]{1,0:T(8,128)} %get-tuple-element.161.z_ref, ...), custom_call_target="tpu_custom_call" | custom-call | flops 1572864 | bytes 1572864 | tf_op jit(solution)/shard_map/gate_backward/pallas_call | solution.py:433
  430.6 9.2 convolution_convert_fusion.2
  441.6 63.9 %scan_backward.2 = (bf16[2048,1920]{1,0:T(8,128)(2,1)}, bf16[2048,1536]{1,0:T(8,128)(2,1)}, f32[8,1024]{1,0:T(8,128)}, f32[8,128]{1,0:T(8,128)}, f32[8,768]{1,0:T(8,128)}) custom-call(s32[1]{0:T(128)} %bitcast.5.me_ref, f32[2048,768]{1,0:T(8,128)} %get-tuple-element.165.dy_ref, f32[2048,768]{1,0:T(8,128)} %get-tuple-element.149.y_ref, ...), custom_call_target="tpu_custom_call" | custom-call | flops 1572864 | bytes 1572864 | tf_op jit(solution)/shard_map/scan_backward/pallas_call | solution.py:489
  522.0 15.8 %convolution_convert_fusion = bf16[1536,1920]{1,0:T(8,128)(2,1)} fusion(bf16[2048,1536]{1,0:T(8,128)(2,1)S(1)} %bitcast.125, bf16[2048,1920]{1,0:T(8,128)(2,1)S(1)} %copy-done.105), kind=kOutput, calls=%fused_computation | convolution fusion | flops 12082544640 | bytes 20054016 | tf_op jit(solution)/shard_map/dot_general | solution.py:34
  543.6 17.3 %collective-permute-done.33 = bf16[256,1536]{1,0:T(8,128)(2,1)S(1)} collective-permute-done((bf16[256,1536]{1,0:T(8,128)(2,1)S(1)}, bf16[256,1536]{1,0:T(8,128)(2,1)S(1)}, u32[]{:S(2)}, u32[]{:S(2)}) %collective-permute-start.33) | collective-permute-done | bytes 786464 | tf_op jit(solution)/shard_map/ppermute | solution.py:553
  562.9 4.4 multiply_reduce_fusion.7
  570.6 3.1 multiply_reduce_fusion.6
  577.7 7.8 collective-permute-done.36
  590.7 11.9 %collective-permute-done.37 = bf16[256,1536]{1,0:T(8,128)(2,1)S(1)} collective-permute-done((bf16[256,1536]{1,0:T(8,128)(2,1)S(1)}, bf16[256,1536]{1,0:T(8,128)(2,1)S(1)}, u32[]{:S(2)}, u32[]{:S(2)}) %collective-permute-start.37) | collective-permute-done | bytes 786464 | tf_op jit(solution)/shard_map/ppermute | solution.py:553
  608.5 17.4 %gate_backward.3 = (bf16[2048,768]{1,0:T(8,128)(2,1)}, f32[2048,768]{1,0:T(8,128)}, bf16[2048,768]{1,0:T(8,128)(2,1)}, f32[1,768]{1,0:T(1,128)}) custom-call(bf16[2048,1536]{1,0:T(8,128)(2,1)} %constant_dynamic-update-slice_fusion.13.grad_ref, f32[2048,768]{1,0:T(8,128)} %get-tuple-element.134.y_ref, f32[2048,768]{1,0:T(8,128)} %get-tuple-element.179.z_ref, ...), custom_call_target="tpu_custom_call" | custom-call | flops 1572864 | bytes 1572864 | tf_op jit(solution)/shard_map/gate_backward/pallas_call | solution.py:433
  626.0 9.3 %convolution_convert_fusion.1 = bf16[1536,768]{1,0:T(8,128)(2,1)} fusion(bf16[2048,1536]{1,0:T(8,128)(2,1)} %constant_dynamic-update-slice_fusion.13.grad_ref, bf16[2048,768]{1,0:T(8,128)(2,1)} %get-tuple-element.181), kind=kOutput, calls=%fused_computation.4 | convolution fusion | flops 4833017856 | bytes 11796480 | tf_op jit(solution)/shard_map/dot_general | solution.py:34
  635.2 16.3 %reduce-scatter.6.cloned.1.call-done = bf16[192,1920]{1,0:T(8,128)(2,1)} async-done(((bf16[1536,1920]{1,0:T(8,128)(2,1)}), bf16[192,1920]{1,0:T(8,128)(2,1)}) %reduce-scatter.6.cloned.1.call-update) | async-done | bytes 737296 | tf_op jit(solution)/shard_map/reduce_scatter | solution.py:871
  651.6 63.5 %scan_backward.3 = (bf16[2048,1920]{1,0:T(8,128)(2,1)}, bf16[2048,1536]{1,0:T(8,128)(2,1)}, f32[8,1024]{1,0:T(8,128)}, f32[8,128]{1,0:T(8,128)}, f32[8,768]{1,0:T(8,128)}) custom-call(s32[1]{0:T(128)} %bitcast.5.me_ref, f32[2048,768]{1,0:T(8,128)} %get-tuple-element.184.dy_ref, f32[2048,768]{1,0:T(8,128)} %get-tuple-element.134.y_ref, ...), custom_call_target="tpu_custom_call" | custom-call | flops 1572864 | bytes 1572864 | tf_op jit(solution)/shard_map/scan_backward/pallas_call | solution.py:489
  715.2 9.3 %reduce-scatter.8.cloned.1.call-done = bf16[192,768]{1,0:T(8,128)(2,1)} async-done(((bf16[1536,768]{1,0:T(8,128)(2,1)}), bf16[192,768]{1,0:T(8,128)(2,1)}) %reduce-scatter.8.cloned.1.call-update) | async-done | bytes 294928 | tf_op jit(solution)/shard_map/reduce_scatter | solution.py:871
  727.3 18.1 %fusion.53 = f32[1536,1920]{1,0:T(8,128)S(1)} fusion(bf16[2048,1536]{1,0:T(8,128)(2,1)} %pad_maximum_fusion.rows_ref, bf16[2048,1920]{1,0:T(8,128)(2,1)} %get-tuple-element.191), kind=kOutput, calls=%fused_computation.274 | convolution fusion | flops 12079595520 | bytes 25952256 | tf_op jit(solution)/shard_map/dot_general | solution.py:34
  745.4 3.1 convert_add_fusion
  754.2 16.9 %collective-permute-done.49 = bf16[192,1920]{1,0:T(8,128)(2,1)} collective-permute-done((bf16[192,1920]{1,0:T(8,128)(2,1)}, bf16[192,1920]{1,0:T(8,128)(2,1)}, u32[]{:S(2)}, u32[]{:S(2)}) %collective-permute-start.49) | collective-permute-done | bytes 737312 | tf_op jit(solution)/shard_map/ppermute | solution.py:611
  771.8 3.6 add_convert_fusion.2
  782.9 10.2 %collective-permute-done.50 = bf16[192,1920]{1,0:T(8,128)(2,1)} collective-permute-done((bf16[192,1920]{1,0:T(8,128)(2,1)}, bf16[192,1920]{1,0:T(8,128)(2,1)}, u32[]{:S(2)}, u32[]{:S(2)}) %collective-permute-start.50) | collective-permute-done | bytes 737312 | tf_op jit(solution)/shard_map/ppermute | solution.py:611
  793.9 3.6 add_convert_fusion.1
  797.5 3.0 collective-permute-done.51
  800.5 14.2 %collective-permute-done.52 = bf16[256,1536]{1,0:T(8,128)(2,1)S(1)} collective-permute-done((bf16[256,1536]{1,0:T(8,128)(2,1)}, bf16[256,1536]{1,0:T(8,128)(2,1)S(1)}, u32[]{:S(2)}, u32[]{:S(2)}) %collective-permute-start.52) | collective-permute-done | bytes 786464 | tf_op jit(solution)/shard_map/ppermute | solution.py:553
  821.8 9.3 collective-permute-done.54
  835.8 3.9 multiply_reduce_fusion.3
  852.5 3.4 multiply_subtract_fusion.2
  884.4 3.9 collective-permute-done.64
  900.8 10.8 %multiply_subtract_fusion = (f32[2,192,2,768]{3,2,1,0:T(2,128)}, f32[2,192,2,768]{3,2,1,0:T(2,128)}, f32[2,192,2,768]{3,2,1,0:T(2,128)}) fusion(f32[2,192,2,768]{3,2,1,0:T(2,128)S(1)} %copy-done.15, f32[1,192,2,768]{3,2,1,0:T(2,128)S(1)} %maximum_bitcast_fusion.1, f32[1,192,2,768]{3,2,1,0:T(2,128)} %copy.277, f32[2,192,2,768]{3,2,1,0:T(2,128)} %param.36, ...), kind=kLoop, calls=%fused_computation.20 | loop fusion | flops 9437184 | bytes 16515072 | tf_op jit(solution)/shard_map/sub | solution.py:677
  (598 shorter events, 260.7 us)
Async XLA Ops:
  7.2 84.9 %all-gather.5.cloned.1.call-start = ((), (), s32[]{:S(2)}) async-start(), calls=%async_computation.3 | async-start | bytes 3981312 | tf_op jit(solution)/shard_map/all_gather | solution.py:757
  19.9 148.1 %all-gather.7.cloned.1.call-start = ((), (), s32[]{:S(2)}) async-start(), calls=%async_computation.4 | async-start | bytes 5308416 | tf_op jit(solution)/shard_map/all_gather | solution.py:758
  21.7 267.9 %all-gather.9.cloned.1.call-start = ((), (), s32[]{:S(2)}) async-start(), calls=%async_computation.5 | async-start | bytes 3981312 | tf_op jit(solution)/shard_map/all_gather | solution.py:757
  55.6 36.5 %collective-permute-start.5 = (bf16[512,1536]{1,0:T(8,128)(2,1)}, bf16[512,1536]{1,0:T(8,128)(2,1)}, u32[]{:S(2)}, u32[]{:S(2)}) collective-permute-start(bf16[512,1536]{1,0:T(8,128)(2,1)} %multiply_convert_fusion), channel_id=1, source_target_pairs={{0,2},{1,3},{2,0},{3,1},{4,6},{5,7},{6,4},{7,5},{8,10},{9,11},{10,... | collective-permute-start | bytes 4718600 | tf_op jit(solution)/shard_map/ppermute | solution.py:553
  57.5 267.0 %all-gather.11.cloned.1.call-start = ((), (), s32[]{:S(2)}) async-start(), calls=%async_computation.6 | async-start | bytes 5308416 | tf_op jit(solution)/shard_map/all_gather | solution.py:758
  57.6 47.4 %collective-permute-start.6 = (bf16[512,1536]{1,0:T(8,128)(2,1)}, bf16[512,1536]{1,0:T(8,128)(2,1)}, u32[]{:S(2)}, u32[]{:S(2)}) collective-permute-start(bf16[512,1536]{1,0:T(8,128)(2,1)} %multiply_convert_fusion), channel_id=1, source_target_pairs={{0,1},{1,0},{2,3},{3,2},{4,5},{5,4},{6,7},{7,6},{8,9},{9,8},{10,11... | collective-permute-start | bytes 4718600 | tf_op jit(solution)/shard_map/ppermute | solution.py:553
  92.1 12.8 %collective-permute-start.7 = (bf16[512,1536]{1,0:T(8,128)(2,1)}, bf16[512,1536]{1,0:T(8,128)(2,1)}, u32[]{:S(2)}, u32[]{:S(2)}) collective-permute-start(bf16[512,1536]{1,0:T(8,128)(2,1)} %collective-permute-done.5), channel_id=1, source_target_pairs={{0,1},{1,0},{2,3},{3,2},{4,5},{5,4},{6,7},{7,6},{8,9},{9,8},{10,11... | collective-permute-start | bytes 4718600 | tf_op jit(solution)/shard_map/ppermute | solution.py:553
  111.3 37.2 %collective-permute-start.8 = (bf16[512,1536]{1,0:T(8,128)(2,1)}, bf16[512,1536]{1,0:T(8,128)(2,1)}, u32[]{:S(2)}, u32[]{:S(2)}) collective-permute-start(bf16[512,1536]{1,0:T(8,128)(2,1)} %convert_element_type.235), channel_id=1, source_target_pairs={{0,2},{1,3},{2,0},{3,1},{4,6},{5,7},{6,4},{7,5},{8,10},{9,11},{10,... | collective-permute-start | bytes 4718600 | tf_op jit(solution)/shard_map/ppermute | solution.py:553
  111.7 39.5 %collective-permute-start.9 = (bf16[512,1536]{1,0:T(8,128)(2,1)}, bf16[512,1536]{1,0:T(8,128)(2,1)}, u32[]{:S(2)}, u32[]{:S(2)}) collective-permute-start(bf16[512,1536]{1,0:T(8,128)(2,1)} %convert_element_type.235), channel_id=1, source_target_pairs={{0,1},{1,0},{2,3},{3,2},{4,5},{5,4},{6,7},{7,6},{8,9},{9,8},{10,11... | collective-permute-start | bytes 4718600 | tf_op jit(solution)/shard_map/ppermute | solution.py:553
  149.4 358.0 %reduce-scatter.4.cloned.1.call-start = ((), (), s32[]{:S(2)}) async-start(), calls=%async_computation.7 | async-start | bytes 2654208 | tf_op jit(solution)/shard_map/reduce_scatter | solution.py:871
  179.8 24.8 %collective-permute-start.11 = (bf16[512,1536]{1,0:T(8,128)(2,1)}, bf16[512,1536]{1,0:T(8,128)(2,1)}, u32[]{:S(2)}, u32[]{:S(2)}) collective-permute-start(bf16[512,1536]{1,0:T(8,128)(2,1)} %get-tuple-element.136), channel_id=1, source_target_pairs={{0,1},{1,0},{2,3},{3,2},{4,5},{5,4},{6,7},{7,6},{8,9},{9,8},{10,11... | collective-permute-start | bytes 4718600 | tf_op jit(solution)/shard_map/ppermute | solution.py:553
  191.8 15.4 %collective-permute-start.12 = (bf16[512,1536]{1,0:T(8,128)(2,1)}, bf16[512,1536]{1,0:T(8,128)(2,1)}, u32[]{:S(2)}, u32[]{:S(2)}) collective-permute-start(bf16[512,1536]{1,0:T(8,128)(2,1)} %get-tuple-element.139), channel_id=1, source_target_pairs={{0,1},{1,0},{2,3},{3,2},{4,5},{5,4},{6,7},{7,6},{8,9},{9,8},{10,11... | collective-permute-start | bytes 4718600 | tf_op jit(solution)/shard_map/ppermute | solution.py:553
  212.8 20.8 %collective-permute-start.15 = (bf16[256,1536]{1,0:T(8,128)(2,1)}, bf16[256,1536]{1,0:T(8,128)(2,1)}, u32[]{:S(2)}, u32[]{:S(2)}) collective-permute-start(bf16[256,1536]{1,0:T(8,128)(2,1)} %slice.652), channel_id=1, source_target_pairs={{0,2},{1,3},{2,0},{3,1},{4,6},{5,7},{6,4},{7,5},{8,10},{9,11},{10,... | collective-permute-start | bytes 2359304 | tf_op jit(solution)/shard_map/ppermute | solution.py:553
  215.8 34.5 %collective-permute-start.16 = (bf16[256,1536]{1,0:T(8,128)(2,1)S(1)}, bf16[256,1536]{1,0:T(8,128)(2,1)S(1)}, u32[]{:S(2)}, u32[]{:S(2)}) collective-permute-start(bf16[256,1536]{1,0:T(8,128)(2,1)S(1)} %slice.651), channel_id=1, source_target_pairs={{0,2},{1,3},{2,0},{3,1},{4,6},{5,7},{6,4},{7,5},{8,10},{9,11},{10,... | collective-permute-start | bytes 2359304 | tf_op jit(solution)/shard_map/ppermute | solution.py:553
  237.1 28.6 %collective-permute-start.17 = (bf16[256,1536]{1,0:T(8,128)(2,1)}, bf16[256,1536]{1,0:T(8,128)(2,1)S(1)}, u32[]{:S(2)}, u32[]{:S(2)}) collective-permute-start(bf16[256,1536]{1,0:T(8,128)(2,1)} %multiply_convert_fusion.2), channel_id=1, source_target_pairs={{0,2},{1,3},{2,0},{3,1},{4,6},{5,7},{6,4},{7,5},{8,10},{9,11},{10,... | collective-permute-start | bytes 2359304 | tf_op jit(solution)/shard_map/ppermute | solution.py:553
  266.7 18.2 %collective-permute-start.18 = (bf16[256,1536]{1,0:T(8,128)(2,1)S(1)}, bf16[256,1536]{1,0:T(8,128)(2,1)S(1)}, u32[]{:S(2)}, u32[]{:S(2)}) collective-permute-start(bf16[256,1536]{1,0:T(8,128)(2,1)S(1)} %get-tuple-element.148), channel_id=1, source_target_pairs={{0,2},{1,3},{2,0},{3,1},{4,6},{5,7},{6,4},{7,5},{8,10},{9,11},{10,... | collective-permute-start | bytes 2359304 | tf_op jit(solution)/shard_map/ppermute | solution.py:553
  268.2 17.7 %collective-permute-start.19 = (bf16[256,1536]{1,0:T(8,128)(2,1)}, bf16[256,1536]{1,0:T(8,128)(2,1)S(1)}, u32[]{:S(2)}, u32[]{:S(2)}) collective-permute-start(bf16[256,1536]{1,0:T(8,128)(2,1)} %multiply_convert_fusion.2), channel_id=1, source_target_pairs={{0,1},{1,0},{2,3},{3,2},{4,5},{5,4},{6,7},{7,6},{8,9},{9,8},{10,11... | collective-permute-start | bytes 2359304 | tf_op jit(solution)/shard_map/ppermute | solution.py:553
  269.8 17.0 %collective-permute-start.20 = (bf16[256,1536]{1,0:T(8,128)(2,1)S(1)}, bf16[256,1536]{1,0:T(8,128)(2,1)S(1)}, u32[]{:S(2)}, u32[]{:S(2)}) collective-permute-start(bf16[256,1536]{1,0:T(8,128)(2,1)S(1)} %get-tuple-element.148), channel_id=1, source_target_pairs={{0,1},{1,0},{2,3},{3,2},{4,5},{5,4},{6,7},{7,6},{8,9},{9,8},{10,11... | collective-permute-start | bytes 2359304 | tf_op jit(solution)/shard_map/ppermute | solution.py:553
  271.0 16.7 %collective-permute-start.21 = (bf16[256,1536]{1,0:T(8,128)(2,1)}, bf16[256,1536]{1,0:T(8,128)(2,1)S(1)}, u32[]{:S(2)}, u32[]{:S(2)}) collective-permute-start(bf16[256,1536]{1,0:T(8,128)(2,1)} %copy-done.38), channel_id=1, source_target_pairs={{0,1},{1,0},{2,3},{3,2},{4,5},{5,4},{6,7},{7,6},{8,9},{9,8},{10,11... | collective-permute-start | bytes 2359304 | tf_op jit(solution)/shard_map/ppermute | solution.py:553
  336.6 29.4 %collective-permute-start.23 = (bf16[512,1536]{1,0:T(8,128)(2,1)}, bf16[512,1536]{1,0:T(8,128)(2,1)S(1)}, u32[]{:S(2)}, u32[]{:S(2)}) collective-permute-start(bf16[512,1536]{1,0:T(8,128)(2,1)} %get-tuple-element.151), channel_id=1, source_target_pairs={{0,1},{1,0},{2,3},{3,2},{4,5},{5,4},{6,7},{7,6},{8,9},{9,8},{10,11... | collective-permute-start | bytes 4718600 | tf_op jit(solution)/shard_map/ppermute | solution.py:553
  348.9 17.5 %collective-permute-start.24 = (bf16[512,1536]{1,0:T(8,128)(2,1)}, bf16[512,1536]{1,0:T(8,128)(2,1)}, u32[]{:S(2)}, u32[]{:S(2)}) collective-permute-start(bf16[512,1536]{1,0:T(8,128)(2,1)} %get-tuple-element.154), channel_id=1, source_target_pairs={{0,1},{1,0},{2,3},{3,2},{4,5},{5,4},{6,7},{7,6},{8,9},{9,8},{10,11... | collective-permute-start | bytes 4718600 | tf_op jit(solution)/shard_map/ppermute | solution.py:553
  369.5 20.5 %collective-permute-start.28 = (bf16[256,1536]{1,0:T(8,128)(2,1)S(1)}, bf16[256,1536]{1,0:T(8,128)(2,1)S(1)}, u32[]{:S(2)}, u32[]{:S(2)}) collective-permute-start(bf16[256,1536]{1,0:T(8,128)(2,1)S(1)} %slice.649), channel_id=1, source_target_pairs={{0,2},{1,3},{2,0},{3,1},{4,6},{5,7},{6,4},{7,5},{8,10},{9,11},{10,... | collective-permute-start | bytes 2359304 | tf_op jit(solution)/shard_map/ppermute | solution.py:553
  371.3 33.5 %collective-permute-start.27 = (bf16[256,1536]{1,0:T(8,128)(2,1)S(1)}, bf16[256,1536]{1,0:T(8,128)(2,1)S(1)}, u32[]{:S(2)}, u32[]{:S(2)}) collective-permute-start(bf16[256,1536]{1,0:T(8,128)(2,1)S(1)} %slice.650), channel_id=1, source_target_pairs={{0,2},{1,3},{2,0},{3,1},{4,6},{5,7},{6,4},{7,5},{8,10},{9,11},{10,... | collective-permute-start | bytes 2359304 | tf_op jit(solution)/shard_map/ppermute | solution.py:553
  439.9 211.6 %reduce-scatter.6.cloned.1.call-start = ((), (), s32[]{:S(2)}) async-start(), calls=%async_computation.8 | async-start | bytes 6635520 | tf_op jit(solution)/shard_map/reduce_scatter | solution.py:871
  520.6 19.9 %collective-permute-start.35 = (bf16[256,1536]{1,0:T(8,128)(2,1)}, bf16[256,1536]{1,0:T(8,128)(2,1)}, u32[]{:S(2)}, u32[]{:S(2)}) collective-permute-start(bf16[256,1536]{1,0:T(8,128)(2,1)} %slice.647), channel_id=1, source_target_pairs={{0,2},{1,3},{2,0},{3,1},{4,6},{5,7},{6,4},{7,5},{8,10},{9,11},{10,... | collective-permute-start | bytes 2359304 | tf_op jit(solution)/shard_map/ppermute | solution.py:553
  540.5 183.9 %reduce-scatter.8.cloned.1.call-start = ((), (), s32[]{:S(2)}) async-start(), calls=%async_computation.9 | async-start | bytes 2654208 | tf_op jit(solution)/shard_map/reduce_scatter | solution.py:871
  542.1 18.8 %collective-permute-start.33 = (bf16[256,1536]{1,0:T(8,128)(2,1)S(1)}, bf16[256,1536]{1,0:T(8,128)(2,1)S(1)}, u32[]{:S(2)}, u32[]{:S(2)}) collective-permute-start(bf16[256,1536]{1,0:T(8,128)(2,1)S(1)} %slice.648), channel_id=1, source_target_pairs={{0,2},{1,3},{2,0},{3,1},{4,6},{5,7},{6,4},{7,5},{8,10},{9,11},{10,... | collective-permute-start | bytes 2359304 | tf_op jit(solution)/shard_map/ppermute | solution.py:553
  567.3 18.3 %collective-permute-start.36 = (bf16[256,1536]{1,0:T(8,128)(2,1)}, bf16[256,1536]{1,0:T(8,128)(2,1)S(1)}, u32[]{:S(2)}, u32[]{:S(2)}) collective-permute-start(bf16[256,1536]{1,0:T(8,128)(2,1)} %get-tuple-element.175), channel_id=1, source_target_pairs={{0,2},{1,3},{2,0},{3,1},{4,6},{5,7},{6,4},{7,5},{8,10},{9,11},{10,... | collective-permute-start | bytes 2359304 | tf_op jit(solution)/shard_map/ppermute | solution.py:553
  568.8 34.8 %collective-permute-start.38 = (bf16[256,1536]{1,0:T(8,128)(2,1)}, bf16[256,1536]{1,0:T(8,128)(2,1)}, u32[]{:S(2)}, u32[]{:S(2)}) collective-permute-start(bf16[256,1536]{1,0:T(8,128)(2,1)} %get-tuple-element.175), channel_id=1, source_target_pairs={{0,1},{1,0},{2,3},{3,2},{4,5},{5,4},{6,7},{7,6},{8,9},{9,8},{10,11... | collective-permute-start | bytes 2359304 | tf_op jit(solution)/shard_map/ppermute | solution.py:553
  573.7 13.3 %collective-permute-start.42 = (f32[512,2]{0,1:T(2,128)S(1)}, f32[512,2]{0,1:T(2,128)S(1)}, u32[]{:S(2)}, u32[]{:S(2)}) collective-permute-start(f32[512,2]{0,1:T(2,128)S(1)} %maximum_maximum_fusion.1), channel_id=1, source_target_pairs={{0,2},{1,3},{2,0},{3,1},{4,6},{5,7},{6,4},{7,5},{8,10},{9,11},{10,... | collective-permute-start | bytes 12296 | tf_op jit(solution)/shard_map/ppermute | solution.py:553
  574.6 12.5 %collective-permute-start.43 = (f32[512,2]{0,1:T(2,128)S(1)}, f32[512,2]{0,1:T(2,128)S(1)}, u32[]{:S(2)}, u32[]{:S(2)}) collective-permute-start(f32[512,2]{0,1:T(2,128)S(1)} %maximum_maximum_fusion.1), channel_id=1, source_target_pairs={{0,1},{1,0},{2,3},{3,2},{4,5},{5,4},{6,7},{7,6},{8,9},{9,8},{10,11... | collective-permute-start | bytes 12296 | tf_op jit(solution)/shard_map/ppermute | solution.py:553
  585.6 17.1 %collective-permute-start.37 = (bf16[256,1536]{1,0:T(8,128)(2,1)S(1)}, bf16[256,1536]{1,0:T(8,128)(2,1)S(1)}, u32[]{:S(2)}, u32[]{:S(2)}) collective-permute-start(bf16[256,1536]{1,0:T(8,128)(2,1)S(1)} %get-tuple-element.178), channel_id=1, source_target_pairs={{0,2},{1,3},{2,0},{3,1},{4,6},{5,7},{6,4},{7,5},{8,10},{9,11},{10,... | collective-permute-start | bytes 2359304 | tf_op jit(solution)/shard_map/ppermute | solution.py:553
  587.1 18.5 %collective-permute-start.39 = (bf16[256,1536]{1,0:T(8,128)(2,1)S(1)}, bf16[256,1536]{1,0:T(8,128)(2,1)S(1)}, u32[]{:S(2)}, u32[]{:S(2)}) collective-permute-start(bf16[256,1536]{1,0:T(8,128)(2,1)S(1)} %get-tuple-element.178), channel_id=1, source_target_pairs={{0,1},{1,0},{2,3},{3,2},{4,5},{5,4},{6,7},{7,6},{8,9},{9,8},{10,11... | collective-permute-start | bytes 2359304 | tf_op jit(solution)/shard_map/ppermute | solution.py:553
  589.6 17.0 %collective-permute-start.40 = (bf16[256,1536]{1,0:T(8,128)(2,1)S(1)}, bf16[256,1536]{1,0:T(8,128)(2,1)S(1)}, u32[]{:S(2)}, u32[]{:S(2)}) collective-permute-start(bf16[256,1536]{1,0:T(8,128)(2,1)S(1)} %collective-permute-done.36), channel_id=1, source_target_pairs={{0,1},{1,0},{2,3},{3,2},{4,5},{5,4},{6,7},{7,6},{8,9},{9,8},{10,11... | collective-permute-start | bytes 2359304 | tf_op jit(solution)/shard_map/ppermute | solution.py:553
  726.7 18.7 %collective-permute-start.46 = (bf16[512,1536]{1,0:T(8,128)(2,1)S(1)}, bf16[512,1536]{1,0:T(8,128)(2,1)S(1)}, u32[]{:S(2)}, u32[]{:S(2)}) collective-permute-start(bf16[512,1536]{1,0:T(8,128)(2,1)S(1)} %get-tuple-element.436), channel_id=1, source_target_pairs={{0,1},{1,0},{2,3},{3,2},{4,5},{5,4},{6,7},{7,6},{8,9},{9,8},{10,11... | collective-permute-start | bytes 4718600 | tf_op jit(solution)/shard_map/ppermute | solution.py:553
  726.8 18.6 %collective-permute-start.45 = (bf16[512,1536]{1,0:T(8,128)(2,1)S(1)}, bf16[512,1536]{1,0:T(8,128)(2,1)S(1)}, u32[]{:S(2)}, u32[]{:S(2)}) collective-permute-start(bf16[512,1536]{1,0:T(8,128)(2,1)S(1)} %get-tuple-element.437), channel_id=1, source_target_pairs={{0,1},{1,0},{2,3},{3,2},{4,5},{5,4},{6,7},{7,6},{8,9},{9,8},{10,11... | collective-permute-start | bytes 4718600 | tf_op jit(solution)/shard_map/ppermute | solution.py:553
  752.2 18.9 %collective-permute-start.49 = (bf16[192,1920]{1,0:T(8,128)(2,1)}, bf16[192,1920]{1,0:T(8,128)(2,1)}, u32[]{:S(2)}, u32[]{:S(2)}) collective-permute-start(bf16[192,1920]{1,0:T(8,128)(2,1)} %get-tuple-element.432), channel_id=1, source_target_pairs={{0,8},{8,16},{16,24},{24,28},{28,20},{20,12},{12,4},{4,0},{1,9},{9... | collective-permute-start | bytes 2211848 | tf_op jit(solution)/shard_map/ppermute | solution.py:611
  753.1 18.6 %collective-permute-start.47 = (bf16[192,1920]{1,0:T(8,128)(2,1)}, bf16[192,1920]{1,0:T(8,128)(2,1)}, u32[]{:S(2)}, u32[]{:S(2)}) collective-permute-start(bf16[192,1920]{1,0:T(8,128)(2,1)} %get-tuple-element.433), channel_id=1, source_target_pairs={{0,4},{8,0},{16,8},{24,16},{28,24},{20,28},{12,20},{4,12},{1,5},{9... | collective-permute-start | bytes 2211848 | tf_op jit(solution)/shard_map/ppermute | solution.py:611
  775.4 17.8 %collective-permute-start.50 = (bf16[192,1920]{1,0:T(8,128)(2,1)}, bf16[192,1920]{1,0:T(8,128)(2,1)}, u32[]{:S(2)}, u32[]{:S(2)}) collective-permute-start(bf16[192,1920]{1,0:T(8,128)(2,1)} %get-tuple-element.430), channel_id=1, source_target_pairs={{0,8},{8,16},{16,24},{24,28},{28,20},{20,12},{12,4},{4,0},{1,9},{9... | collective-permute-start | bytes 2211848 | tf_op jit(solution)/shard_map/ppermute | solution.py:611
  776.4 17.5 %collective-permute-start.48 = (bf16[192,1920]{1,0:T(8,128)(2,1)}, bf16[192,1920]{1,0:T(8,128)(2,1)}, u32[]{:S(2)}, u32[]{:S(2)}) collective-permute-start(bf16[192,1920]{1,0:T(8,128)(2,1)} %get-tuple-element.431), channel_id=1, source_target_pairs={{0,4},{8,0},{16,8},{24,16},{28,24},{20,28},{12,20},{4,12},{1,5},{9... | collective-permute-start | bytes 2211848 | tf_op jit(solution)/shard_map/ppermute | solution.py:611
  779.8 20.8 %collective-permute-start.51 = (bf16[256,1536]{1,0:T(8,128)(2,1)}, bf16[256,1536]{1,0:T(8,128)(2,1)}, u32[]{:S(2)}, u32[]{:S(2)}) collective-permute-start(bf16[256,1536]{1,0:T(8,128)(2,1)} %slice.646), channel_id=1, source_target_pairs={{0,2},{1,3},{2,0},{3,1},{4,6},{5,7},{6,4},{7,5},{8,10},{9,11},{10,... | collective-permute-start | bytes 2359304 | tf_op jit(solution)/shard_map/ppermute | solution.py:553
  782.2 32.6 %collective-permute-start.52 = (bf16[256,1536]{1,0:T(8,128)(2,1)}, bf16[256,1536]{1,0:T(8,128)(2,1)S(1)}, u32[]{:S(2)}, u32[]{:S(2)}) collective-permute-start(bf16[256,1536]{1,0:T(8,128)(2,1)} %slice.645), channel_id=1, source_target_pairs={{0,2},{1,3},{2,0},{3,1},{4,6},{5,7},{6,4},{7,5},{8,10},{9,11},{10,... | collective-permute-start | bytes 2359304 | tf_op jit(solution)/shard_map/ppermute | solution.py:553
  814.8 16.3 %collective-permute-start.54 = (bf16[192,1920]{1,0:T(8,128)(2,1)}, bf16[192,1920]{1,0:T(8,128)(2,1)}, u32[]{:S(2)}, u32[]{:S(2)}) collective-permute-start(bf16[192,1920]{1,0:T(8,128)(2,1)} %get-tuple-element.196), channel_id=1, source_target_pairs={{0,8},{8,16},{16,24},{24,28},{28,20},{20,12},{12,4},{4,0},{1,9},{9... | collective-permute-start | bytes 2211848 | tf_op jit(solution)/shard_map/ppermute | solution.py:611
  818.5 16.1 %collective-permute-start.53 = (bf16[192,1920]{1,0:T(8,128)(2,1)}, bf16[192,1920]{1,0:T(8,128)(2,1)}, u32[]{:S(2)}, u32[]{:S(2)}) collective-permute-start(bf16[192,1920]{1,0:T(8,128)(2,1)} %get-tuple-element.195), channel_id=1, source_target_pairs={{0,4},{8,0},{16,8},{24,16},{28,24},{20,28},{12,20},{4,12},{1,5},{9... | collective-permute-start | bytes 2211848 | tf_op jit(solution)/shard_map/ppermute | solution.py:611
  844.8 47.0 %collective-permute-start.55 = (bf16[192,1920]{1,0:T(8,128)(2,1)}, bf16[192,1920]{1,0:T(8,128)(2,1)}, u32[]{:S(2)}, u32[]{:S(2)}) collective-permute-start(bf16[192,1920]{1,0:T(8,128)(2,1)} %add_convert_fusion), channel_id=1, source_target_pairs={{0,8},{8,16},{16,24},{24,28},{28,20},{20,12},{12,4},{4,0},{1,9},{9... | collective-permute-start | bytes 2211848 | tf_op jit(solution)/shard_map/ppermute | solution.py:611
  848.1 14.5 %collective-permute-start.60 = (f32[2,1280]{1,0:T(2,128)}, f32[2,1280]{1,0:T(2,128)}, u32[]{:S(2)}, u32[]{:S(2)}) collective-permute-start(f32[2,1280]{1,0:T(2,128)} %pad_maximum_fusion.17), channel_id=1, source_target_pairs={{0,1},{1,0},{2,3},{3,2},{4,5},{5,4},{6,7},{7,6},{8,9},{9,8},{10,11... | collective-permute-start | bytes 30728 | tf_op jit(solution)/shard_map/ppermute | solution.py:645
  898.0 14.4 %collective-permute-start.58 = (f32[96,256]{1,0:T(8,128)}, f32[96,256]{1,0:T(8,128)}, u32[]{:S(2)}, u32[]{:S(2)}) collective-permute-start(f32[96,256]{1,0:T(8,128)} %pad_maximum_fusion.10), channel_id=1, source_target_pairs={{0,1},{1,0},{2,3},{3,2},{4,5},{5,4},{6,7},{7,6},{8,9},{9,8},{10,11... | collective-permute-start | bytes 294920 | tf_op jit(solution)/shard_map/ppermute | solution.py:553
  898.6 15.4 %collective-permute-start.56 = (f32[96,256]{1,0:T(8,128)}, f32[96,256]{1,0:T(8,128)}, u32[]{:S(2)}, u32[]{:S(2)}) collective-permute-start(f32[96,256]{1,0:T(8,128)} %pad_maximum_fusion.9), channel_id=1, source_target_pairs={{0,1},{1,0},{2,3},{3,2},{4,5},{5,4},{6,7},{7,6},{8,9},{9,8},{10,11... | collective-permute-start | bytes 294920 | tf_op jit(solution)/shard_map/ppermute | solution.py:553
  (139 other events, 1400.4 us)
Sparse Core Ops, SparseCore 0:
  20.0 66.7 all-gather.4
  89.6 78.3 all-gather.6
  170.2 63.3 all-gather.8
  235.6 78.3 all-gather.10
  440.0 67.2 reduce-scatter.3
  540.7 110.8 reduce-scatter.5
  655.6 68.8 reduce-scatter.7
